TPU v7x, 32 devices: a whole 2x2x4 slice. The times are simulated.
32 devices in a mesh: row: 8 (over z, x), col: 4 (over y, core).
Axes of the slice: x: 2, y: 2, z: 4, core: 2. Of those that a mesh axis runs over, the one named last changes fastest.
Arguments:
- feats: bfloat16 [8, 2, 64, 96], P('row', None, 'col'), may hold values from -6 to 6
- proj_weight: bfloat16 [96, 48], replicated, may hold values from -0.625 to 0.625
- conv_weight: bfloat16 [48, 9, 48], replicated, may hold values from -0.3125 to 0.3125
- head_weight: float32 [48], replicated, may hold values from -0.875 to 0.875
- tile_table: int32 [8, 4, 5, 3], P('row', 'col'), may hold values from 0 to 15, as said below
- targets: float32 [8, 4, 5, 64, 64], P('row', 'col'), may hold values from -10 to 10
Outputs:
- feat_grad: float32 [8, 2, 64, 96], P('row', None, 'col')
- proj_grad: float32 [96, 48], replicated
- conv_grad: float32 [48, 9, 48], replicated
- head_grad: float32 [48], replicated
Inputs may be any that keep to these rules, and one draw needn't show every extreme that they name: `tile_table`: for row index r, the slots over all column indices hold every tile (a, b) with a in r, 15 - r and a <= b exactly once as (a, b, 1); every other slot holds (r, r, 0). The tiles of row r then of row 15 - r, by rising column, are dealt one per column index in turn from a column index drawn for each r.
All inputs are finite; a program needn't handle non-finite values.
Results may differ from a plain program's by a relative error of at most 0.0043.
Values may be sent and summed in bfloat16 or wider, within the bound.
No kernel may reach another device: no remote copies, remote signals or barrier semaphores. Data moves between devices by JAX's collectives and lax.ppermute only.
A program may use at most 64 MiB of HBM per device.

v0:
```python
import math

import jax
import jax.numpy as jnp
from jax import lax
from jax.sharding import PartitionSpec as P

MAP_CHANNELS = 48
TILE_BINS = 64
DILATION_SIZE = 8


def tile_terms(
    padded_map,
    conv_flat,
    head_weight,
    sequence_length,
    tile_row_index,
    tile_column_index,
    is_live,
    goal,
):
    padded_extent = TILE_BINS + 2 * DILATION_SIZE
    rows_part = lax.dynamic_slice_in_dim(padded_map, tile_row_index * TILE_BINS, padded_extent, 0)
    cols_part = lax.dynamic_slice_in_dim(
        padded_map, tile_column_index * TILE_BINS, padded_extent, 0
    )
    step_index = jnp.arange(padded_extent, dtype=jnp.int32)
    row_position = tile_row_index * TILE_BINS - DILATION_SIZE + step_index
    column_position = tile_column_index * TILE_BINS - DILATION_SIZE + step_index
    in_row = (row_position >= 0) & (row_position < sequence_length)
    in_col = (column_position >= 0) & (column_position < sequence_length)
    paired_map = 0.5 * (
        rows_part.T.astype(jnp.float32)[:, :, None] + cols_part.T.astype(jnp.float32)[:, None, :]
    )
    active = in_row[None, :, None] & in_col[None, None, :] & (paired_map > 0)
    relu_act = jnp.where(active, paired_map, jnp.zeros_like(paired_map)).astype(jnp.bfloat16)
    tap_shifts = [
        (row_shift, column_shift)
        for row_shift in (0, DILATION_SIZE, 2 * DILATION_SIZE)
        for column_shift in (0, DILATION_SIZE, 2 * DILATION_SIZE)
    ]
    stacked = jnp.concatenate(
        [
            relu_act[
                :, row_shift : row_shift + TILE_BINS, column_shift : column_shift + TILE_BINS
            ].reshape(MAP_CHANNELS, TILE_BINS * TILE_BINS)
            for row_shift, column_shift in tap_shifts
        ],
        axis=0,
    )
    inner_region = paired_map[
        :, DILATION_SIZE : DILATION_SIZE + TILE_BINS, DILATION_SIZE : DILATION_SIZE + TILE_BINS
    ].reshape(MAP_CHANNELS, TILE_BINS * TILE_BINS)
    outputs = inner_region + jnp.dot(conv_flat, stacked, preferred_element_type=jnp.float32)
    predicted = jnp.dot(head_weight, outputs, precision=lax.Precision.HIGHEST)
    misfit = (predicted - goal.reshape(TILE_BINS * TILE_BINS)) * is_live.astype(jnp.float32)
    output_gradient_whole = head_weight[:, None] * misfit[None, :]
    dy_half = output_gradient_whole.astype(jnp.bfloat16)
    conv_term = lax.dot_general(
        dy_half, stacked, (((1,), (1,)), ((), ())), preferred_element_type=jnp.float32
    )
    head_term = jnp.dot(outputs, misfit, precision=lax.Precision.HIGHEST)
    backed = lax.dot_general(
        conv_flat, dy_half, (((0,), (0,)), ((), ())), preferred_element_type=jnp.float32
    )
    margin_total = 2 * DILATION_SIZE
    up_grad = jnp.zeros((MAP_CHANNELS, padded_extent, padded_extent), jnp.float32)
    for index, (row_shift, column_shift) in enumerate(tap_shifts):
        piece = backed[index * MAP_CHANNELS : (index + 1) * MAP_CHANNELS].reshape(
            MAP_CHANNELS, TILE_BINS, TILE_BINS
        )
        up_grad = up_grad + jnp.pad(
            piece,
            (
                (0, 0),
                (row_shift, margin_total - row_shift),
                (column_shift, margin_total - column_shift),
            ),
        )
    direct_part = jnp.pad(
        output_gradient_whole.reshape(MAP_CHANNELS, TILE_BINS, TILE_BINS),
        ((0, 0), (DILATION_SIZE, DILATION_SIZE), (DILATION_SIZE, DILATION_SIZE)),
    )
    input_gradient = jnp.where(active, up_grad, jnp.zeros_like(up_grad)) + direct_part
    grad_rows = 0.5 * jnp.sum(input_gradient, axis=2).T
    grad_cols = 0.5 * jnp.sum(input_gradient, axis=1).T
    return (conv_term, head_term, grad_rows, grad_cols)


def add_into(scratch_buffer, start, piece):
    current = lax.dynamic_slice_in_dim(scratch_buffer, start, piece.shape[0], 0)
    return lax.dynamic_update_slice_in_dim(scratch_buffer, current + piece, start, 0)


def project_rows(values, proj_weight):
    lead = values.shape[:-1]
    flat = values.reshape(-1, values.shape[-1])
    return jnp.dot(flat, proj_weight, preferred_element_type=jnp.float32).reshape(
        lead + (proj_weight.shape[1],)
    )


def body(feats, proj_weight, conv_weight, head_weight, tile_table, targets):
    rows_dev = lax.axis_size("row")
    block_list = 2 * rows_dev
    sequence_length = block_list * TILE_BINS
    conv_flat = conv_weight.reshape(MAP_CHANNELS, 9 * MAP_CHANNELS)
    band_feats = lax.all_gather(feats, "col", axis=2, tiled=True)
    all_feats = lax.all_gather(band_feats, "row", axis=0, tiled=True)
    folded = project_rows(all_feats, proj_weight).astype(jnp.bfloat16)
    natural_order = jnp.concatenate([folded[:, 0], folded[::-1, 1]], axis=0).reshape(
        sequence_length, MAP_CHANNELS
    )
    padded_map = jnp.pad(natural_order, ((DILATION_SIZE, DILATION_SIZE), (0, 0)))

    def slot_step(carry, inputs):
        conv_acc, head_acc, scratch_buffer = carry
        entry, goal = inputs
        conv_term, head_term, grad_rows, grad_cols = tile_terms(
            padded_map, conv_flat, head_weight, sequence_length, entry[0], entry[1], entry[2], goal
        )
        scratch_buffer = add_into(scratch_buffer, entry[0] * TILE_BINS, grad_rows)
        scratch_buffer = add_into(scratch_buffer, entry[1] * TILE_BINS, grad_cols)
        return ((conv_acc + conv_term, head_acc + head_term, scratch_buffer), None)

    initial_carry = (
        jnp.zeros((MAP_CHANNELS, 9 * MAP_CHANNELS), jnp.float32),
        jnp.zeros((MAP_CHANNELS,), jnp.float32),
        jnp.zeros((sequence_length + 2 * DILATION_SIZE, MAP_CHANNELS), jnp.float32),
    )
    (conv_acc, head_acc, scratch_buffer), _ = lax.scan(
        slot_step, initial_carry, (tile_table[0, 0], targets[0, 0])
    )
    natural_gradient = scratch_buffer[DILATION_SIZE : DILATION_SIZE + sequence_length].reshape(
        block_list, TILE_BINS, MAP_CHANNELS
    )
    grad_fold = jnp.stack([natural_gradient[:rows_dev], natural_gradient[rows_dev:][::-1]], axis=1)
    weights_wide = proj_weight.astype(jnp.float32)
    band_grad = lax.psum_scatter(
        jnp.einsum("rhtd,cd->rhtc", grad_fold, weights_wide, precision=lax.Precision.HIGHEST),
        "row",
        scatter_dimension=0,
        tiled=True,
    )
    feat_grad = lax.psum_scatter(band_grad, "col", scatter_dimension=2, tiled=True) / math.sqrt(
        sequence_length
    )
    proj_term = jnp.einsum(
        "rhtc,rhtd->cd", all_feats.astype(jnp.float32), grad_fold, precision=lax.Precision.HIGHEST
    )
    conv_total, head_total, proj_total = lax.psum((conv_acc, head_acc, proj_term), ("row", "col"))
    scale = 1.0 / (sequence_length * TILE_BINS)
    return (
        feat_grad,
        proj_total * scale,
        (conv_total * scale).reshape(MAP_CHANNELS, 9, MAP_CHANNELS),
        head_total * scale,
    )


def solution(mesh):
    return jax.shard_map(
        body,
        mesh=mesh,
        in_specs=(
            P("row", None, "col", None),
            P(),
            P(),
            P(),
            P("row", "col", None, None),
            P("row", "col", None, None, None),
        ),
        out_specs=(P("row", None, "col", None), P(), P(), P()),
        check_vma=False,
    )
```

profile of v0, /device:TPU:0, one launch (start us, length us, event | category | flops | bytes accessed | tf_op | source)
XLA Modules:
  0.0 576.1 jit_solution(3145839638722581912)
XLA Ops:
  9.3 6.4 %all_gather.6 = bf16[1,2,64,96]{3,2,1,0:T(8,128)(2,1)S(1)} all-gather(bf16[1,2,16,96]{3,2,1,0:T(8,128)(2,1)} %param.8), channel_id=1, replica_groups=mesh['row'=8,'col'=4] {'col'}, dimensions={2}, use_global_device_ids=true | all-gather | bytes 30720 | tf_op jit(solution)/shard_map/all_gather | solution.py:109
  16.9 31.6 %all_gather.7 = bf16[8,2,64,96]{3,2,1,0:T(8,128)(2,1)S(1)} all-gather(bf16[1,2,64,96]{3,2,1,0:T(8,128)(2,1)S(1)} %all_gather.6), channel_id=1, replica_groups=mesh['row'=8,'col'=4] {'row'}, dimensions={0}, use_global_device_ids=true | all-gather | bytes 221184 | tf_op jit(solution)/shard_map/all_gather | solution.py:110
  51.3 380.1 %while.18 = (s32[]{:T(128)}, f32[48,432]{1,0:T(8,128)S(1)}, f32[48]{0:T(128)}, f32[1040,48]{0,1:T(8,128)}, f32[48]{0:T(128)S(1)}, /*index=5*/s32[5,3]{0,1:T(4,12...) while((s32[]{:T(128)}, f32[48,432]{1,0:T(8,128)S(1)}, ...), condition=%wide.region_3.4_spmd.clone, body=%wide.region_0.3_spmd.clone.sunk | while | flops 522336736 | bytes 95551896 | solution.py:132
  59.4 3.7 fusion.50
  100.5 3.0 reshape.306
  106.4 3.0 reshape.308
  115.3 7.5 %fusion.55 = (f32[48,80]{1,0:T(8,128)S(1)}, f32[48,80]{1,0:T(8,128)S(1)}) fusion(f32[48,64,64]{2,1,0:T(8,128)S(1)} %broadcast_multiply_fusion.6, f32[48,64,64]{2,1,0:T(8,128)S(1)} %reshape.302, f32[48,64,64]{2,1,0:T(8,128)} %reshape.303, f32[48,64,64]{2,1,0:T(8,128)} %reshape.304, f32[48,64,64]{2,1,0:T(8,128)} %reshape.305, ...), kind=kLoop, calls=%fused_computation.55.clone.1 | loop fusion | flops 4907520 | bytes 7932160 | tf_op jit(solution)/shard_map/while/body/eval_jaxpr/reduce_sum | solution.py:87
  135.3 3.7 fusion.50
  182.4 3.0 reshape.308
  191.2 7.5 %fusion.55 = (f32[48,80]{1,0:T(8,128)S(1)}, f32[48,80]{1,0:T(8,128)S(1)}) fusion(f32[48,64,64]{2,1,0:T(8,128)S(1)} %broadcast_multiply_fusion.6, f32[48,64,64]{2,1,0:T(8,128)S(1)} %reshape.302, f32[48,64,64]{2,1,0:T(8,128)} %reshape.303, f32[48,64,64]{2,1,0:T(8,128)} %reshape.304, f32[48,64,64]{2,1,0:T(8,128)} %reshape.305, ...), kind=kLoop, calls=%fused_computation.55.clone.1 | loop fusion | flops 4907520 | bytes 7932160 | tf_op jit(solution)/shard_map/while/body/eval_jaxpr/reduce_sum | solution.py:87
  211.2 3.7 fusion.50
  252.4 3.0 reshape.306
  258.3 3.0 reshape.308
  267.2 7.5 %fusion.55 = (f32[48,80]{1,0:T(8,128)S(1)}, f32[48,80]{1,0:T(8,128)S(1)}) fusion(f32[48,64,64]{2,1,0:T(8,128)S(1)} %broadcast_multiply_fusion.6, f32[48,64,64]{2,1,0:T(8,128)S(1)} %reshape.302, f32[48,64,64]{2,1,0:T(8,128)} %reshape.303, f32[48,64,64]{2,1,0:T(8,128)} %reshape.304, f32[48,64,64]{2,1,0:T(8,128)} %reshape.305, ...), kind=kLoop, calls=%fused_computation.55.clone.1 | loop fusion | flops 4907520 | bytes 7932160 | tf_op jit(solution)/shard_map/while/body/eval_jaxpr/reduce_sum | solution.py:87
  287.2 3.7 fusion.50
  328.3 3.0 reshape.306
  334.2 3.0 reshape.308
  343.1 7.5 %fusion.55 = (f32[48,80]{1,0:T(8,128)S(1)}, f32[48,80]{1,0:T(8,128)S(1)}) fusion(f32[48,64,64]{2,1,0:T(8,128)S(1)} %broadcast_multiply_fusion.6, f32[48,64,64]{2,1,0:T(8,128)S(1)} %reshape.302, f32[48,64,64]{2,1,0:T(8,128)} %reshape.303, f32[48,64,64]{2,1,0:T(8,128)} %reshape.304, f32[48,64,64]{2,1,0:T(8,128)} %reshape.305, ...), kind=kLoop, calls=%fused_computation.55.clone.1 | loop fusion | flops 4907520 | bytes 7932160 | tf_op jit(solution)/shard_map/while/body/eval_jaxpr/reduce_sum | solution.py:87
  363.2 3.7 fusion.50
  410.2 3.0 reshape.308
  419.1 7.5 %fusion.55 = (f32[48,80]{1,0:T(8,128)S(1)}, f32[48,80]{1,0:T(8,128)S(1)}) fusion(f32[48,64,64]{2,1,0:T(8,128)S(1)} %broadcast_multiply_fusion.6, f32[48,64,64]{2,1,0:T(8,128)S(1)} %reshape.302, f32[48,64,64]{2,1,0:T(8,128)} %reshape.303, f32[48,64,64]{2,1,0:T(8,128)} %reshape.304, f32[48,64,64]{2,1,0:T(8,128)} %reshape.305, ...), kind=kLoop, calls=%fused_computation.55.clone.1 | loop fusion | flops 4907520 | bytes 7932160 | tf_op jit(solution)/shard_map/while/body/eval_jaxpr/reduce_sum | solution.py:87
  435.6 41.0 %all-reduce.11 = (f32[96,48]{0,1:T(8,128)S(1)}, f32[48]{0:T(128)S(1)}) all-reduce(f32[96,48]{0,1:T(8,128)S(1)} %convolution_bitcast_fusion.3, f32[48]{0:T(128)S(1)} %copy-done.17), channel_id=1, replica_groups=mesh['row'=8,'col'=4] {'row','col'}, use_global_device_ids=true, to_apply=%region_6.7 | all-reduce | flops 4656 | bytes 37248 | tf_op jit(solution)/shard_map/psum | solution.py:152
  477.7 20.6 %reduce-scatter.3.cloned.1.call-done = f32[1,2,64,96]{3,2,1,0:T(8,128)} async-done(((f32[8,2,64,96]{3,2,1,0:T(8,128)}), f32[1,2,64,96]{3,2,1,0:T(8,128)}) %reduce-scatter.3.cloned.1.call-update) | async-done | bytes 49168 | tf_op jit(solution)/shard_map/reduce_scatter | solution.py:140
  498.3 67.2 %all-reduce.14.cloned.1.call-done = f32[48,432]{0,1:T(8,128)} async-done(((f32[48,432]{0,1:T(8,128)}), f32[48,432]{0,1:T(8,128)}) %all-reduce.14.cloned.1.call-update) | async-done | bytes 82960 | tf_op jit(solution)/shard_map/psum | solution.py:152
  (416 shorter events, 302.8 us)
Async XLA Ops:
  8.0 41.2 %copy-start = (bf16[96,48]{0,1:T(8,128)(2,1)S(1)}, bf16[96,48]{0,1:T(8,128)(2,1)}, u32[]{:S(2)}) copy-start(bf16[96,48]{0,1:T(8,128)(2,1)} %param.9) | copy-start | bytes 27652
  8.0 43.3 %copy-start.14 = (f32[48]{0:T(128)S(1)}, f32[48]{0:T(128)}, u32[]{:S(2)}) copy-start(f32[48]{0:T(128)} %param.11) | copy-start | bytes 580
  8.0 490.3 %reduce-scatter.3.cloned.1.call-start = ((), (), s32[]{:S(2)}) async-start(), calls=%async_computation.2 | async-start | bytes 589824 | tf_op jit(solution)/shard_map/reduce_scatter | solution.py:140
  54.5 3.0 copy-start.9
  68.1 7.7 %copy-start.1 = (bf16[48,64,64]{2,1,0:T(8,128)(2,1)S(1)}, bf16[48,64,64]{2,1,0:T(8,128)(2,1)}, u32[]{:S(2)}) copy-start(bf16[48,64,64]{2,1,0:T(8,128)(2,1)} %get-tuple-element.354) | copy-start | bytes 1179652 | tf_op jit(solution)/shard_map/while
  78.7 2.5 copy-start.7
  109.4 5.8 %copy-start.10 = (pred[80,80]{1,0:T(8,128)(4,1)S(1)}, pred[80,80]{1,0:T(8,128)(4,1)}, u32[]{:S(2)}) copy-start(pred[80,80]{1,0:T(8,128)(4,1)} %copy-done.9) | copy-start | bytes 19204 | tf_op jit(solution)/shard_map/while
  130.5 2.9 copy-start.9
  144.1 7.7 %copy-start.1 = (bf16[48,64,64]{2,1,0:T(8,128)(2,1)S(1)}, bf16[48,64,64]{2,1,0:T(8,128)(2,1)}, u32[]{:S(2)}) copy-start(bf16[48,64,64]{2,1,0:T(8,128)(2,1)} %get-tuple-element.354) | copy-start | bytes 1179652 | tf_op jit(solution)/shard_map/while
  185.4 5.8 %copy-start.10 = (pred[80,80]{1,0:T(8,128)(4,1)S(1)}, pred[80,80]{1,0:T(8,128)(4,1)}, u32[]{:S(2)}) copy-start(pred[80,80]{1,0:T(8,128)(4,1)} %copy-done.9) | copy-start | bytes 19204 | tf_op jit(solution)/shard_map/while
  206.4 2.9 copy-start.9
  220.0 7.7 %copy-start.1 = (bf16[48,64,64]{2,1,0:T(8,128)(2,1)S(1)}, bf16[48,64,64]{2,1,0:T(8,128)(2,1)}, u32[]{:S(2)}) copy-start(bf16[48,64,64]{2,1,0:T(8,128)(2,1)} %get-tuple-element.354) | copy-start | bytes 1179652 | tf_op jit(solution)/shard_map/while
  230.5 2.5 copy-start.7
  261.3 5.8 %copy-start.10 = (pred[80,80]{1,0:T(8,128)(4,1)S(1)}, pred[80,80]{1,0:T(8,128)(4,1)}, u32[]{:S(2)}) copy-start(pred[80,80]{1,0:T(8,128)(4,1)} %copy-done.9) | copy-start | bytes 19204 | tf_op jit(solution)/shard_map/while
  282.4 2.9 copy-start.9
  295.9 7.7 %copy-start.1 = (bf16[48,64,64]{2,1,0:T(8,128)(2,1)S(1)}, bf16[48,64,64]{2,1,0:T(8,128)(2,1)}, u32[]{:S(2)}) copy-start(bf16[48,64,64]{2,1,0:T(8,128)(2,1)} %get-tuple-element.354) | copy-start | bytes 1179652 | tf_op jit(solution)/shard_map/while
  337.2 5.8 %copy-start.10 = (pred[80,80]{1,0:T(8,128)(4,1)S(1)}, pred[80,80]{1,0:T(8,128)(4,1)}, u32[]{:S(2)}) copy-start(pred[80,80]{1,0:T(8,128)(4,1)} %copy-done.9) | copy-start | bytes 19204 | tf_op jit(solution)/shard_map/while
  358.3 3.0 copy-start.9
  371.9 7.7 %copy-start.1 = (bf16[48,64,64]{2,1,0:T(8,128)(2,1)S(1)}, bf16[48,64,64]{2,1,0:T(8,128)(2,1)}, u32[]{:S(2)}) copy-start(bf16[48,64,64]{2,1,0:T(8,128)(2,1)} %get-tuple-element.354) | copy-start | bytes 1179652 | tf_op jit(solution)/shard_map/while
  413.2 5.8 %copy-start.10 = (pred[80,80]{1,0:T(8,128)(4,1)S(1)}, pred[80,80]{1,0:T(8,128)(4,1)}, u32[]{:S(2)}) copy-start(pred[80,80]{1,0:T(8,128)(4,1)} %copy-done.9) | copy-start | bytes 19204 | tf_op jit(solution)/shard_map/while
  432.5 2.7 copy-start.13
  432.6 2.9 copy-start.17
  434.2 131.3 %all-reduce.14.cloned.1.call-start = ((), (), s32[]{:S(2)}) async-start(), calls=%async_computation.4 | async-start | bytes 442368 | tf_op jit(solution)/shard_map/psum | solution.py:152
  435.1 132.2 %reduce-scatter.5.cloned.1.call-start = ((), (), s32[]{:S(2)}) async-start(), calls=%async_computation.3 | async-start | bytes 81920 | tf_op jit(solution)/shard_map/reduce_scatter | solution.py:146
  (49 other events, 72.2 us)
Sparse Core Ops, SparseCore 0:
  434.4 63.8 reduce-scatter.2
  500.8 18.4 reduce-scatter.4
Sparse Core Ops, SparseCore 1:
  440.8 124.7 all-reduce.13
where the time goes:
time: 582 us; the launch traced here: 576 us
  local copies, waits for them, and re-layouts  301 us (52%)
  waiting for transfers between devices  87.9 us (15%)
  blocking collectives  79 us (14%)
  other arithmetic  58.3 us (10%)
  matrix products  23.7 us (4%)
  between operations  15.7 us (3%)
  loops' own time  10.9 us (2%)
    reshape x45, local copies, waits for them, and re-layouts, tile_terms(): backed[index * MAP_CHANNELS:(index + 1) * MAP_CHANNELS]  126 us
    reshape x45, local copies, waits for them, and re-layouts, tile_terms(): stacked = jnp.concatenate([relu_act[:, row_shift:row_shift + TILE_BINS, c...  84.3 us
    psum x1, waiting for transfers between devices, body(): lax.psum((conv_acc, head_acc, proj_term), ('row', 'col'))  67.2 us
    psum x1, blocking collectives, body(): lax.psum((conv_acc, head_acc, proj_term), ('row', 'col'))  41 us
    reduce_sum x5, other arithmetic, tile_terms(): grad_cols = 0.5 * jnp.sum(input_gradient, axis=1).T  37.3 us
    all_gather x1, blocking collectives, body(): all_feats = lax.all_gather(band_feats, 'row', axis=0, tiled=True)  31.6 us
    reduce_scatter x1, waiting for transfers between devices, body(): lax.psum_scatter(jnp.einsum('rhtd,cd->rhtc', grad_fold, weights_wide, pre...  20.6 us
    slice x5, local copies, waits for them, and re-layouts, tile_terms(): relu_act[:, row_shift:row_shift + TILE_BINS, column_shift:column_shift +...  18.6 us
  transfers between devices with their start and end apart: 3, of which 2 were waited for; matrix products, arithmetic and copies ran while one was open for 1% of the time, Pallas kernels for 0%

commit v1 on v0

v1 whole, which is shorter than its diff:
```python
import functools
import math

import jax
import jax.numpy as jnp
from jax import lax
from jax.experimental import pallas as pl
from jax.experimental.pallas import tpu as pltpu
from jax.sharding import PartitionSpec as P

DIL = 8
LANES = 128
HALO = 16
F32 = jnp.float32
BF16 = jnp.bfloat16
OUTSIDE = -1e30


def lane_iota(rows):
    return lax.broadcasted_iota(jnp.int32, (rows, LANES), 1)


def split_two(x):
    high = x.astype(BF16).astype(F32)
    return high, x - high


def pad_to(x, rows, cols):
    r, c = x.shape
    if c < cols:
        x = jnp.concatenate([x, jnp.zeros((r, cols - c), x.dtype)], axis=1)
    if r < rows:
        x = jnp.concatenate([x, jnp.zeros((rows - r, cols), x.dtype)], axis=0)
    return x


def column_of(scalars_ref, count):
    sub = lax.broadcasted_iota(jnp.int32, (8, LANES), 0)
    groups = []
    for g in range(count // 8):
        acc = jnp.zeros((8, LANES), F32)
        for k in range(8):
            acc = jnp.where(sub == k, scalars_ref[g * 8 + k], acc)
        groups.append(acc)
    return jnp.concatenate(groups, axis=0)


def tiles_kernel(
    rows_dev,
    slots,
    feats_ref,
    proj_ref,
    conv_ref,
    head_ref,
    table_ref,
    targets_ref,
    out_ref,
    fwin_ref,
    gwin_ref,
    dwin_ref,
    u_ref,
    m_ref,
):
    n_src, _, chunk, c1 = feats_ref.shape
    cols_dev = n_src // rows_dev
    blocks = 2 * rows_dev
    bins = cols_dev * chunk
    ch = proj_ref.shape[1]
    frame = bins + 2 * DIL
    lane = lane_iota(ch)
    lane1 = lane_iota(1)

    def chunks_of(b):
        r, half = (b, 0) if b < rows_dev else (blocks - 1 - b, 1)
        return [feats_ref[r * cols_dev + c, half] for c in range(cols_dev)]

    proj_t = jnp.transpose(pad_to(proj_ref[...].astype(F32), LANES, LANES))[:ch, :c1].astype(BF16)
    zero_halo = jnp.zeros((HALO, c1), BF16)
    for b in range(blocks):
        before = chunks_of(b - 1)[-1][chunk - HALO :] if b > 0 else zero_halo
        after = chunks_of(b + 1)[0][:HALO] if b < blocks - 1 else zero_halo
        tail = jnp.zeros((LANES - bins - 2 * HALO, c1), BF16)
        window = jnp.concatenate([before] + chunks_of(b) + [after, tail], axis=0)
        fwin_ref[b] = window
        g = lax.dot_general(proj_t, window, (((1,), (1,)), ((), ())), preferred_element_type=F32)
        g = 0.5 * g.astype(BF16).astype(F32)
        if b == 0:
            g = jnp.where(lane < HALO, OUTSIDE, g)
        if b == blocks - 1:
            g = jnp.where(lane >= HALO + bins, OUTSIDE, g)
        gwin_ref[b] = g
        dwin_ref[b] = jnp.zeros((ch, LANES), F32)

    taps = jnp.zeros((9, ch), F32)
    for o in range(ch):
        taps = taps + head_ref[o] * conv_ref[o].astype(F32)
    taps_hi, taps_lo = split_two(taps)
    forward_rows, backward_rows = [], []
    for dy in range(3):
        hi, lo = taps_hi[3 * dy : 3 * dy + 3], taps_lo[3 * dy : 3 * dy + 3]
        forward_rows.append(
            jnp.concatenate([hi, lo, jnp.zeros((10, ch), F32)], axis=0).astype(BF16)
        )
        backward_rows.append(jnp.concatenate([hi, hi, lo, jnp.zeros((7, ch), F32)], axis=0))
    forward_taps = jnp.concatenate(forward_rows, axis=1)
    backward_taps = jnp.transpose(pad_to(jnp.concatenate(backward_rows, axis=0), LANES, LANES))[
        :ch, :48
    ].astype(BF16)
    head_col = column_of(head_ref, ch)

    group = 8 * LANES
    pad_cols = 2 * group
    m_ref[:, :pad_cols] = jnp.zeros((16, pad_cols), BF16)
    m_ref[:, pad_cols + bins * LANES :] = jnp.zeros((16, pad_cols), BF16)
    row8 = lax.broadcasted_iota(jnp.int32, (8, LANES), 0)
    row16 = lax.broadcasted_iota(jnp.int32, (16, LANES), 0)
    inner = (lane1 >= HALO) & (lane1 < HALO + bins)
    low_row = (row16 >= 3) & (row16 < 6)

    def slot(s, carry):
        v_acc, x_acc = carry
        a, b, live = table_ref[0, 0, s, 0], table_ref[0, 0, s, 1], table_ref[0, 0, s, 2]
        weight = jnp.where(inner, live.astype(F32), 0.0)
        gr, gc = gwin_ref[a], gwin_ref[b]
        for i in range(frame):
            at = HALO - DIL + i
            x = gr[:, at : at + 1] + gc
            u_ref[:, i * LANES : (i + 1) * LANES] = jnp.maximum(x, 0.0).astype(BF16)
        pred_r = jnp.sum(jnp.where(lane < HALO + bins, head_col * gr, 0.0), axis=0, keepdims=True)
        pred_c = jnp.sum(jnp.where(lane < HALO + bins, head_col * gc, 0.0), axis=0, keepdims=True)
        m_rows = jnp.zeros((1, LANES), F32)
        m_cols = jnp.zeros((1, LANES), F32)
        for c in range(bins // 8):
            u3 = jnp.concatenate(
                [u_ref[:, (c + dy) * group : (c + dy + 1) * group] for dy in range(3)], axis=0
            )
            z = jnp.dot(forward_taps, u3, preferred_element_type=F32)[:8]
            goal = targets_ref[0, 0, s, c * 8 : (c + 1) * 8, :]
            goal = jnp.concatenate(
                [jnp.zeros((8, HALO), F32), goal, jnp.zeros((8, LANES - HALO - bins), F32)], axis=1
            )
            for k in range(8):
                i = c * 8 + k
                zi = z[:, k * LANES : (k + 1) * LANES]
                shifted = jnp.where(
                    row8 % 3 == 0,
                    pltpu.roll(zi, DIL, 1),
                    jnp.where(row8 % 3 == 2, pltpu.roll(zi, LANES - DIL, 1), zi),
                )
                conv = jnp.sum(jnp.where(row8 < 6, shifted, 0.0), axis=0, keepdims=True)
                at = HALO + i
                m = (conv + pred_c + pred_r[:, at : at + 1] - goal[k : k + 1]) * weight
                m = jnp.where(inner, m, 0.0)
                m_cols = m_cols + m
                m_rows = jnp.where(lane1 == at, jnp.sum(m, axis=1, keepdims=True), m_rows)
                m8 = jnp.broadcast_to(m, (8, LANES))
                left, right = pltpu.roll(m8, LANES - DIL, 1), pltpu.roll(m8, DIL, 1)
                spread = jnp.where(
                    row16 % 3 == 0,
                    jnp.concatenate([left, left], axis=0),
                    jnp.where(
                        row16 % 3 == 2,
                        jnp.concatenate([right, right], axis=0),
                        jnp.concatenate([m8, m8], axis=0),
                    ),
                )
                hi, lo = split_two(spread)
                m_ref[:, pad_cols + i * LANES : pad_cols + (i + 1) * LANES] = jnp.where(
                    low_row, lo, hi
                ).astype(BF16)
        d_rows = jnp.zeros((ch, LANES), F32)
        d_cols = jnp.zeros((ch, LANES), F32)
        for c in range(frame // 8):
            m3 = jnp.concatenate(
                [m_ref[:, (c + 2 - dy) * group : (c + 3 - dy) * group] for dy in range(3)], axis=0
            )
            u = u_ref[:, c * group : (c + 1) * group]
            v_acc = v_acc + lax.dot_general(
                u, m3, (((1,), (1,)), ((), ())), preferred_element_type=F32
            )
            up = jnp.dot(backward_taps, m3, preferred_element_type=F32)
            grad = jnp.where(u.astype(F32) > 0.0, up, 0.0)
            for k in range(8):
                part = grad[:, k * LANES : (k + 1) * LANES]
                d_cols = d_cols + part
                d_rows = jnp.where(
                    lane == HALO - DIL + c * 8 + k, jnp.sum(part, axis=1, keepdims=True), d_rows
                )
        d_rows = 0.5 * (d_rows + head_col * m_rows)
        d_cols = 0.5 * (d_cols + head_col * m_cols)
        dwin_ref[a] = dwin_ref[a] + d_rows
        dwin_ref[b] = dwin_ref[b] + d_cols
        return v_acc, x_acc + jnp.where(m_rows != 0.0, gr * m_rows, 0.0) + jnp.where(
            m_cols != 0.0, gc * m_cols, 0.0
        )

    v_acc, x_acc = lax.fori_loop(
        0, slots, slot, (jnp.zeros((ch, 48), F32), jnp.zeros((ch, LANES), F32))
    )

    proj_acc = jnp.zeros((2 * ch, c1), F32)
    for b in range(blocks):
        hi, lo = split_two(dwin_ref[b])
        both = jnp.concatenate([hi, lo], axis=0).astype(BF16)
        proj_acc = proj_acc + jnp.dot(both, fwin_ref[b], preferred_element_type=F32)
    proj_acc = pad_to(proj_acc[:ch] + proj_acc[ch:], ch, LANES)

    v_pad = pad_to(v_acc, ch, LANES)
    v_pad = v_pad + pltpu.roll(v_pad, LANES - 3, 1)
    sums = jnp.zeros((ch, LANES), F32)
    for dy in range(3):
        first = 2 * ch + 3 * dy
        moved = pltpu.roll(v_pad, 2 * ch - 13 * dy, 1)
        sums = jnp.where((lane >= first) & (lane < first + 3), moved, sums)
    sums = jnp.where(lane == 2 * ch + 9, jnp.sum(x_acc, axis=1, keepdims=True), sums)
    sums_hi, sums_lo = split_two(sums)
    sums = sums_hi + pltpu.roll(sums_lo, 10, 1)
    shared = [
        jnp.where(lane < 2 * ch, half, sums) for half in (pltpu.roll(proj_acc, ch, 1), proj_acc)
    ]

    def block_gradient(b):
        own = jnp.where((lane >= HALO) & (lane < HALO + bins), dwin_ref[b], 0.0)
        if b > 0:
            before = pltpu.roll(dwin_ref[b - 1], LANES - bins, 1)
            own = own + jnp.where((lane >= HALO) & (lane < HALO + DIL), before, 0.0)
        if b < blocks - 1:
            after = pltpu.roll(dwin_ref[b + 1], bins, 1)
            own = own + jnp.where((lane >= HALO + bins - DIL) & (lane < HALO + bins), after, 0.0)
        return jnp.transpose(pad_to(own, LANES, LANES))[HALO : HALO + bins]

    part = bins // (out_ref.shape[0] // rows_dev)
    lane_part = lane_iota(part)
    for r in range(rows_dev):
        both = (block_gradient(r), block_gradient(blocks - 1 - r))
        for c in range(bins // part):
            dest = r * (bins // part) + c
            base = shared[c % 2]
            for half in range(2):
                rows = slice(half * part, (half + 1) * part)
                piece = jnp.where(
                    lane_part < ch, both[half][c * part : (c + 1) * part], base[rows]
                )
                out_ref[dest, rows] = piece.astype(BF16)
            out_ref[dest, 2 * part :] = base[2 * part :].astype(BF16)


def finish_kernel(
    scale, root, got_ref, proj_ref, conv_ref, head_ref, feat_ref, conv_out_ref, head_out_ref, half_ref
):
    n_src, ch, _ = got_ref.shape
    c1 = proj_ref.shape[0]
    part = feat_ref.shape[2]
    total = got_ref[0].astype(F32)
    for d in range(1, n_src):
        total = total + got_ref[d].astype(F32)
    whole_t = jnp.transpose(pad_to(total, LANES, LANES))
    half_ref[...] = whole_t[ch : 2 * ch, :ch] * scale

    proj_t = jnp.transpose(pad_to(proj_ref[...].astype(F32), LANES, LANES))[:ch, :c1].astype(BF16)
    hi, lo = split_two(total[: 2 * part, :ch])
    feat = jnp.dot(hi.astype(BF16), proj_t, preferred_element_type=F32) + jnp.dot(
        lo.astype(BF16), proj_t, preferred_element_type=F32
    )
    feat = feat * root
    for half in range(2):
        feat_ref[0, half] = feat[half * part : (half + 1) * part]

    sums = whole_t[2 * ch : 2 * ch + 10, :ch] + whole_t[2 * ch + 10 : 2 * ch + 20, :ch]
    v = sums[:9]
    sub = lax.broadcasted_iota(jnp.int32, (8, ch), 0)
    groups = []
    for g in range(ch // 8):
        acc = jnp.zeros((8, ch), F32)
        for k in range(8):
            o = g * 8 + k
            conv_out_ref[o] = v * (head_ref[o] * scale)
            product = jnp.sum(conv_ref[o].astype(F32) * v, axis=0, keepdims=True)
            acc = jnp.where(sub == k, product, acc)
        groups.append(acc)
    products = pad_to(jnp.concatenate(groups, axis=0), LANES, LANES)
    head_sum = jnp.sum(jnp.transpose(products), axis=0, keepdims=True)[:, :ch]
    head_out_ref[...] = (sums[9:10] + head_sum) * scale


def body(feats, proj_weight, conv_weight, head_weight, tile_table, targets):
    rows_dev, cols_dev = lax.axis_size("row"), lax.axis_size("col")
    devices = rows_dev * cols_dev
    _, halves, part, c1 = feats.shape
    ch = proj_weight.shape[1]
    bins = part * cols_dev
    blocks = halves * rows_dev
    sequence_length = blocks * bins
    slots = tile_table.shape[2]
    scale = 1.0 / (sequence_length * bins)
    frame = bins + 2 * DIL

    all_feats = lax.all_to_all(
        jnp.broadcast_to(feats, (devices,) + feats.shape[1:]), ("row", "col"), 0, 0, tiled=True
    )
    if part % 16:
        all_feats = (
            all_feats.reshape(rows_dev, cols_dev, halves, part, c1)
            .transpose(0, 2, 1, 3, 4)
            .reshape(rows_dev, halves, bins, c1)
        )
    vmem = pl.BlockSpec(memory_space=pltpu.VMEM)
    smem = pl.BlockSpec(memory_space=pltpu.SMEM)
    params = pltpu.CompilerParams(vmem_limit_bytes=48 * 1024 * 1024)
    partial = pl.pallas_call(
        functools.partial(tiles_kernel, rows_dev, slots),
        out_shape=jax.ShapeDtypeStruct((devices, ch, LANES), BF16),
        in_specs=[vmem, vmem, vmem, smem, smem, vmem],
        out_specs=vmem,
        scratch_shapes=[
            pltpu.VMEM((blocks, LANES, c1), BF16),
            pltpu.VMEM((blocks, ch, LANES), F32),
            pltpu.VMEM((blocks, ch, LANES), F32),
            pltpu.VMEM((ch, frame * LANES), BF16),
            pltpu.VMEM((16, (bins + 32) * LANES), BF16),
        ],
        compiler_params=params,
        name="tiles",
    )(all_feats, proj_weight, conv_weight, head_weight, tile_table, targets)
    got = lax.all_to_all(partial, ("row", "col"), 0, 0, tiled=True)
    feat_grad, conv_grad, head_grad, mine = pl.pallas_call(
        functools.partial(finish_kernel, scale, 1.0 / math.sqrt(sequence_length)),
        out_shape=(
            jax.ShapeDtypeStruct(feats.shape, F32),
            jax.ShapeDtypeStruct(conv_weight.shape, F32),
            jax.ShapeDtypeStruct((1, ch), F32),
            jax.ShapeDtypeStruct((ch, ch), F32),
        ),
        in_specs=[vmem, vmem, vmem, smem],
        out_specs=(vmem, vmem, vmem, vmem),
        compiler_params=params,
        name="finish",
    )(got, proj_weight, conv_weight, head_weight)
    other = lax.ppermute(mine, "col", [(c, c ^ 1) for c in range(cols_dev)])
    odd = lax.axis_index("col") % 2 == 1
    proj_grad = jnp.concatenate(
        [jnp.where(odd, other, mine), jnp.where(odd, mine, other)], axis=0
    )
    return feat_grad, proj_grad, conv_grad, head_grad.reshape(ch)


def solution(mesh):
    return jax.shard_map(
        body,
        mesh=mesh,
        in_specs=(
            P("row", None, "col", None),
            P(),
            P(),
            P(),
            P("row", "col", None, None),
            P("row", "col", None, None, None),
        ),
        out_specs=(P("row", None, "col", None), P(), P(), P()),
        check_vma=False,
    )
```

time: 582 us -> 78.8 us (0.14)
  local copies, waits for them, and re-layouts: 301 us -> 3.74 us
  waiting for transfers between devices: 87.9 us -> 10.1 us
  blocking collectives: 79 us -> 15.4 us
  other arithmetic: 58.3 us -> 0.02 us
  Pallas kernels: 0 us -> 41.2 us
  matrix products: 23.7 us -> 0 us
  between operations: 15.7 us -> 0.69 us
  loops' own time: 10.9 us -> 0 us
  starting transfers between devices: 0.12 us -> 7.3 us
    reshape x101 -> x0, local copies, waits for them, and re-layouts: 221 us -> none  [the longest x45 126 us: tile_terms(): backed[index * MAP_CHANNELS:(index + 1) * MAP_CHANNELS]]
    psum x1 -> x0, waiting for transfers between devices: 67.2 us -> none  [body(): lax.psum((conv_acc, head_acc, proj_term), ('row', 'col'))]
    pallas_call x0 -> x2, Pallas kernels: none -> 41.2 us  [the longest x1 39.7 us: body(): pl.pallas_call(functools.partial(tiles_kernel, rows_dev, slots), out_shap...]
    psum x1 -> x0, blocking collectives: 41 us -> none  [body(): lax.psum((conv_acc, head_acc, proj_term), ('row', 'col'))]
    slice x23 -> x0, local copies, waits for them, and re-layouts: 39.5 us -> none  [the longest x5 18.6 us: tile_terms(): relu_act[:, row_shift:row_shift + TILE_BINS, column_shift:column_shift +...]
    all_gather x2 -> x0, blocking collectives: 38 us -> none  [the longest x1 31.6 us: body(): all_feats = lax.all_gather(band_feats, 'row', axis=0, tiled=True)]
    reduce_sum x5 -> x0, other arithmetic: 37.3 us -> none  [tile_terms(): grad_cols = 0.5 * jnp.sum(input_gradient, axis=1).T]
    dot_general x28 -> x0, matrix products: 23.7 us -> none  [the longest x5 5.77 us: tile_terms(): lax.dot_general(dy_half, stacked, (((1,), (1,)), ((), ())), preferred_ele...]
  transfers between devices with their start and end apart: 3 -> 2, of which waited for: 2 -> 2; matrix products, arithmetic and copies ran while one was open for 1% -> 1% of each run, Pallas kernels for 0% -> 0%
where the time goes in v1:
time: 78.8 us; the launch traced here: 78.4 us
  Pallas kernels  41.2 us (52%)
  blocking collectives  15.4 us (20%)
  waiting for transfers between devices  10.1 us (13%)
  starting transfers between devices  7.3 us (9%)
  local copies, waits for them, and re-layouts  3.74 us (5%)
    pallas_call x1, Pallas kernels, body(): pl.pallas_call(functools.partial(tiles_kernel, rows_dev, slots), out_shap...  39.7 us
    all_to_all x1, blocking collectives, body(): got = lax.all_to_all(partial, ('row', 'col'), 0, 0, tiled=True)  15.4 us
    all_to_all x1, waiting for transfers between devices, body(): lax.all_to_all(jnp.broadcast_to(feats, (devices,) + feats.shape[1:]), ('r...  9.69 us
    all_to_all x1, starting transfers between devices, body(): lax.all_to_all(jnp.broadcast_to(feats, (devices,) + feats.shape[1:]), ('r...  7.3 us
    unnamed x15, local copies, waits for them, and re-layouts  2.31 us
  transfers between devices with their start and end apart: 2, of which 2 were waited for; matrix products, arithmetic and copies ran while one was open for 1% of the time, Pallas kernels for 0%

profile of v1, /device:TPU:0, one launch (start us, length us, event | category | flops | bytes accessed | tf_op | source)
XLA Modules:
  0.0 78.4 jit_solution(1518708429836944061)
XLA Ops:
  0.6 1.4 %broadcast_in_dim.8 = bf16[32,2,16,96]{3,2,1,0:T(8,128)(2,1)} broadcast(bf16[2,16,96]{2,1,0:T(8,128)(2,1)} %bitcast.2), dimensions={1,2,3} | broadcast | bytes 202752 | tf_op jit(solution)/shard_map/broadcast_in_dim | solution.py:299
  2.1 0.0 copy-start.3
  2.1 0.0 copy-start.2
  2.1 7.3 %all-to-all-start = ((bf16[32,2,16,96]{3,2,1,0:T(8,128)(2,1)}), bf16[32,2,16,96]{3,2,1,0:T(8,128)(2,1)S(1)}, u32[]{:S(2)}, u32[]{:S(2)}) async-start(bf16[32,2,16,96]{3,2,1,0:T(8,128)(2,1)} %broadcast_in_dim.8), calls=%async_computation | async-start | bytes 524288 | tf_op jit(solution)/shard_map/all_to_all | solution.py:298
  9.4 0.0 copy-done.3
  9.4 0.1 copy.10.proj_ref
  9.5 0.0 copy-done.2
  9.5 0.0 copy-start.4
  9.5 0.0 copy-start
  9.6 0.6 copy-done.4
  10.2 0.0 copy-start.1
  10.2 0.1 copy.12.table_ref
  10.3 9.7 %all-to-all-done.feats_ref = bf16[32,2,16,96]{3,2,1,0:T(8,128)(2,1)S(1)} async-done(((bf16[32,2,16,96]{3,2,1,0:T(8,128)(2,1)}), bf16[32,2,16,96]{3,2,1,0:T(8,128)(2,1)S(1)}, u32[]{:S(2)}, u32[]{:S(2)}) %all-to-all-start) | async-done | bytes 196640 | tf_op jit(solution)/shard_map/all_to_all | solution.py:298
  20.0 0.0 copy-done
  20.0 0.0 copy-done.1
  20.0 39.7 %tiles.1 = bf16[32,48,128]{2,1,0:T(8,128)(2,1)S(1)} custom-call(bf16[32,2,16,96]{3,2,1,0:T(8,128)(2,1)S(1)} %all-to-all-done.feats_ref, bf16[96,48]{1,0:T(8,128)(2,1)S(1)} %copy.10.proj_ref, bf16[48,9,48]{2,1,0:T(8,128)(2,1)S(1)} %copy.11.conv_ref, f32[48]{0:T(128)S(1)} %copy-done.1, s32[1,1,5,3]{3,2,1,0:T(8,128)S(1)} %copy.12.table_ref, ...), custom_call_target="tpu_custom_call" | custom-call | tf_op jit(solution)/shard_map/tiles/pallas_call | solution.py:310
  59.7 15.4 %all_to_all.10.got_ref = bf16[32,48,128]{2,1,0:T(8,128)(2,1)S(1)} all-to-all(bf16[32,48,128]{2,1,0:T(8,128)(2,1)S(1)} %tiles.1), channel_id=1, replica_groups=mesh['row'=8,'col'=4] {'row','col'}, dimensions={0} | all-to-all | bytes 786432 | tf_op jit(solution)/shard_map/all_to_all | solution.py:325
  75.1 1.4 %finish.1 = (f32[1,2,16,96]{3,2,1,0:T(8,128)}, f32[48,9,48]{2,1,0:T(8,128)S(1)}, f32[1,48]{1,0:T(1,128)}, f32[48,48]{1,0:T(8,128)S(1)}) custom-call(bf16[32,48,128]{2,1,0:T(8,128)(2,1)S(1)} %all_to_all.10.got_ref, bf16[96,48]{1,0:T(8,128)(2,1)S(1)} %copy.10.proj_ref, bf16[48,9,48]{2,1,0:T(8,128)(2,1)S(1)} %copy.11.conv_ref, f32[48]{0:T(128)S(1)} %copy-done.1), custom_call_target="tpu_custom_call" | custom-call | tf_op jit(solution)/shard_map/finish/pallas_call | solution.py:326
  76.5 0.0 collective-permute-start
  76.5 0.8 copy.16
  77.3 0.4 collective-permute-done
  77.7 0.7 copy.15
  (3 shorter events, 0.1 us)
Async XLA Ops:
  2.1 7.3 %copy-start.3 = (bf16[96,48]{0,1:T(8,128)(2,1)S(1)}, bf16[96,48]{0,1:T(8,128)(2,1)}, u32[]{:S(2)}) copy-start(bf16[96,48]{0,1:T(8,128)(2,1)} %param.7) | copy-start | bytes 27652
  2.1 7.4 %copy-start.2 = (bf16[48,9,48]{2,0,1:T(8,128)(2,1)S(1)}, bf16[48,9,48]{2,0,1:T(8,128)(2,1)}, u32[]{:S(2)}) copy-start(bf16[48,9,48]{2,0,1:T(8,128)(2,1)} %param.8) | copy-start | bytes 124420
  2.1 17.9 %all-to-all-start = ((bf16[32,2,16,96]{3,2,1,0:T(8,128)(2,1)}), bf16[32,2,16,96]{3,2,1,0:T(8,128)(2,1)S(1)}, u32[]{:S(2)}, u32[]{:S(2)}) async-start(bf16[32,2,16,96]{3,2,1,0:T(8,128)(2,1)} %broadcast_in_dim.8), calls=%async_computation | async-start | bytes 524288 | tf_op jit(solution)/shard_map/all_to_all | solution.py:298
  9.5 0.7 copy-start.4
  9.5 10.5 %copy-start = (f32[1,1,5,64,64]{4,3,2,1,0:T(8,128)S(1)}, f32[1,1,5,64,64]{4,3,2,1,0:T(8,128)}, u32[]{:S(2)}) copy-start(f32[1,1,5,64,64]{4,3,2,1,0:T(8,128)} %targets_ref.1) | copy-start | bytes 245764
  10.2 9.8 %copy-start.1 = (f32[48]{0:T(128)S(1)}, f32[48]{0:T(128)}, u32[]{:S(2)}) copy-start(f32[48]{0:T(128)} %head_ref.3) | copy-start | bytes 580
  76.5 1.2 %collective-permute-start = (f32[48,48]{1,0:T(8,128)S(1)}, f32[48,48]{1,0:T(8,128)S(1)}, u32[]{:S(2)}, u32[]{:S(2)}) collective-permute-start(f32[48,48]{1,0:T(8,128)S(1)} %get-tuple-element.9), channel_id=1, source_target_pairs={{0,1},{1,0},{2,3},{3,2},{4,5},{5,4},{6,7},{7,6},{8,9},{9,8},{10,11... | collective-permute-start | bytes 27656 | tf_op jit(solution)/shard_map/ppermute | solution.py:339

commit v2 on v1

--- a/solution.py
+++ b/solution.py
@@ -60,13 +60,15 @@
     dwin_ref,
     u_ref,
     m_ref,
+    v_ref,
+    forward_ref,
+    backward_ref,
 ):
     n_src, _, chunk, c1 = feats_ref.shape
     cols_dev = n_src // rows_dev
     blocks = 2 * rows_dev
     bins = cols_dev * chunk
     ch = proj_ref.shape[1]
-    frame = bins + 2 * DIL
     lane = lane_iota(ch)
     lane1 = lane_iota(1)
 
@@ -94,109 +96,115 @@
     taps = jnp.zeros((9, ch), F32)
     for o in range(ch):
         taps = taps + head_ref[o] * conv_ref[o].astype(F32)
-    taps_hi, taps_lo = split_two(taps)
+    wide = (8, 8 * ch)
+    diagonal = lax.broadcasted_iota(jnp.int32, wide, 1) // ch == lax.broadcasted_iota(
+        jnp.int32, wide, 0
+    )
+    hi_tiles, lo_tiles = [
+        [
+            jnp.where(diagonal, jnp.broadcast_to(row, wide), 0.0)
+            for row in jnp.split(jnp.concatenate([values] * 8, axis=1), 9, axis=0)
+        ]
+        for values in split_two(taps)
+    ]
     forward_rows, backward_rows = [], []
     for dy in range(3):
-        hi, lo = taps_hi[3 * dy : 3 * dy + 3], taps_lo[3 * dy : 3 * dy + 3]
-        forward_rows.append(
-            jnp.concatenate([hi, lo, jnp.zeros((10, ch), F32)], axis=0).astype(BF16)
-        )
-        backward_rows.append(jnp.concatenate([hi, hi, lo, jnp.zeros((7, ch), F32)], axis=0))
-    forward_taps = jnp.concatenate(forward_rows, axis=1)
-    backward_taps = jnp.transpose(pad_to(jnp.concatenate(backward_rows, axis=0), LANES, LANES))[
-        :ch, :48
-    ].astype(BF16)
+        hi, lo = hi_tiles[3 * dy : 3 * dy + 3], lo_tiles[3 * dy : 3 * dy + 3]
+        forward_rows += hi + lo
+        backward_rows += hi + hi + lo + [jnp.zeros(wide, F32)]
+    forward_taps = jnp.concatenate(forward_rows, axis=0).astype(BF16)
+    backward_taps = jnp.transpose(
+        jnp.concatenate(backward_rows + [jnp.zeros((16, 8 * ch), F32)], axis=0)
+    )[:, :240].astype(BF16)
+    forward_ref[...] = forward_taps
+    backward_ref[...] = backward_taps
     head_col = column_of(head_ref, ch)
 
-    group = 8 * LANES
-    pad_cols = 2 * group
-    m_ref[:, :pad_cols] = jnp.zeros((16, pad_cols), BF16)
-    m_ref[:, pad_cols + bins * LANES :] = jnp.zeros((16, pad_cols), BF16)
-    row8 = lax.broadcasted_iota(jnp.int32, (8, LANES), 0)
-    row16 = lax.broadcasted_iota(jnp.int32, (16, LANES), 0)
+    groups = bins // 8
+    m_ref[:, : 2 * LANES] = jnp.zeros((80, 2 * LANES), BF16)
+    m_ref[:, (groups + 2) * LANES :] = jnp.zeros((80, 2 * LANES), BF16)
+    v_ref[...] = jnp.zeros(v_ref.shape, F32)
     inner = (lane1 >= HALO) & (lane1 < HALO + bins)
-    low_row = (row16 >= 3) & (row16 < 6)
-
-    def slot(s, carry):
-        v_acc, x_acc = carry
+
+    def slot(s, x_acc):
         a, b, live = table_ref[0, 0, s, 0], table_ref[0, 0, s, 1], table_ref[0, 0, s, 2]
         weight = jnp.where(inner, live.astype(F32), 0.0)
         gr, gc = gwin_ref[a], gwin_ref[b]
-        for i in range(frame):
-            at = HALO - DIL + i
-            x = gr[:, at : at + 1] + gc
-            u_ref[:, i * LANES : (i + 1) * LANES] = jnp.maximum(x, 0.0).astype(BF16)
+        for g in range(groups + 2):
+            for k in range(8):
+                at = HALO - DIL + g * 8 + k
+                x = gr[:, at : at + 1] + gc
+                u_ref[k * ch : (k + 1) * ch, g * LANES : (g + 1) * LANES] = jnp.maximum(
+                    x, 0.0
+                ).astype(BF16)
         pred_r = jnp.sum(jnp.where(lane < HALO + bins, head_col * gr, 0.0), axis=0, keepdims=True)
         pred_c = jnp.sum(jnp.where(lane < HALO + bins, head_col * gc, 0.0), axis=0, keepdims=True)
-        m_rows = jnp.zeros((1, LANES), F32)
-        m_cols = jnp.zeros((1, LANES), F32)
-        for c in range(bins // 8):
-            u3 = jnp.concatenate(
-                [u_ref[:, (c + dy) * group : (c + dy + 1) * group] for dy in range(3)], axis=0
-            )
-            z = jnp.dot(forward_taps, u3, preferred_element_type=F32)[:8]
+        pred_r = jnp.transpose(jnp.broadcast_to(pred_r, (LANES, LANES)))
+        z = jnp.dot(forward_ref[...], u_ref[...], preferred_element_type=F32)
+        m_cols = jnp.zeros((8, LANES), F32)
+        row_sums = [jnp.zeros((HALO, LANES), F32)]
+        for c in range(groups):
+            terms = []
+            for dx in range(3):
+                tiles = [
+                    z[
+                        48 * dy + 24 * p + 8 * dx : 48 * dy + 24 * p + 8 * dx + 8,
+                        (c + dy) * LANES : (c + dy + 1) * LANES,
+                    ]
+                    for dy in range(3)
+                    for p in range(2)
+                ]
+                while len(tiles) > 1:
+                    tiles = [sum(tiles[i : i + 2]) for i in range(0, len(tiles), 2)]
+                terms.append(tiles[0])
+            conv = pltpu.roll(terms[0], DIL, 1) + terms[1] + pltpu.roll(terms[2], LANES - DIL, 1)
             goal = targets_ref[0, 0, s, c * 8 : (c + 1) * 8, :]
             goal = jnp.concatenate(
                 [jnp.zeros((8, HALO), F32), goal, jnp.zeros((8, LANES - HALO - bins), F32)], axis=1
             )
-            for k in range(8):
-                i = c * 8 + k
-                zi = z[:, k * LANES : (k + 1) * LANES]
-                shifted = jnp.where(
-                    row8 % 3 == 0,
-                    pltpu.roll(zi, DIL, 1),
-                    jnp.where(row8 % 3 == 2, pltpu.roll(zi, LANES - DIL, 1), zi),
-                )
-                conv = jnp.sum(jnp.where(row8 < 6, shifted, 0.0), axis=0, keepdims=True)
-                at = HALO + i
-                m = (conv + pred_c + pred_r[:, at : at + 1] - goal[k : k + 1]) * weight
-                m = jnp.where(inner, m, 0.0)
-                m_cols = m_cols + m
-                m_rows = jnp.where(lane1 == at, jnp.sum(m, axis=1, keepdims=True), m_rows)
-                m8 = jnp.broadcast_to(m, (8, LANES))
-                left, right = pltpu.roll(m8, LANES - DIL, 1), pltpu.roll(m8, DIL, 1)
-                spread = jnp.where(
-                    row16 % 3 == 0,
-                    jnp.concatenate([left, left], axis=0),
-                    jnp.where(
-                        row16 % 3 == 2,
-                        jnp.concatenate([right, right], axis=0),
-                        jnp.concatenate([m8, m8], axis=0),
-                    ),
-                )
-                hi, lo = split_two(spread)
-                m_ref[:, pad_cols + i * LANES : pad_cols + (i + 1) * LANES] = jnp.where(
-                    low_row, lo, hi
-                ).astype(BF16)
+            at = HALO + c * 8
+            m = jnp.where(inner, (conv + pred_c + pred_r[at : at + 8] - goal) * weight, 0.0)
+            m_cols = m_cols + m
+            row_sums.append(jnp.broadcast_to(jnp.sum(m, axis=1, keepdims=True), (8, LANES)))
+            his, los = [], []
+            for moved in (pltpu.roll(m, LANES - DIL, 1), m, pltpu.roll(m, DIL, 1)):
+                hi, lo = split_two(moved)
+                his.append(hi)
+                los.append(lo)
+            m_ref[:, (c + 2) * LANES : (c + 3) * LANES] = jnp.concatenate(
+                his + los + his + [jnp.zeros((8, LANES), F32)], axis=0
+            ).astype(BF16)
+        row_sums.append(jnp.zeros((LANES - HALO - bins, LANES), F32))
+        m_rows = jnp.transpose(jnp.concatenate(row_sums, axis=0))[:1]
+        m_cols = jnp.sum(m_cols, axis=0, keepdims=True)
         d_rows = jnp.zeros((ch, LANES), F32)
         d_cols = jnp.zeros((ch, LANES), F32)
-        for c in range(frame // 8):
-            m3 = jnp.concatenate(
-                [m_ref[:, (c + 2 - dy) * group : (c + 3 - dy) * group] for dy in range(3)], axis=0
-            )
-            u = u_ref[:, c * group : (c + 1) * group]
-            v_acc = v_acc + lax.dot_general(
-                u, m3, (((1,), (1,)), ((), ())), preferred_element_type=F32
-            )
-            up = jnp.dot(backward_taps, m3, preferred_element_type=F32)
-            grad = jnp.where(u.astype(F32) > 0.0, up, 0.0)
+        frame_cols = (groups + 2) * LANES
+        m3 = jnp.concatenate(
+            [m_ref[:, (2 - dy) * LANES : (2 - dy) * LANES + frame_cols] for dy in range(3)], axis=0
+        )
+        v_ref[...] += lax.dot_general(
+            u_ref[...], m3, (((1,), (1,)), ((), ())), preferred_element_type=F32
+        )
+        for g in range(groups + 2):
+            cols = slice(g * LANES, (g + 1) * LANES)
+            up = jnp.dot(backward_ref[...], m3[:, cols], preferred_element_type=F32)
+            grad = jnp.where(u_ref[:, cols].astype(F32) > 0.0, up, 0.0)
             for k in range(8):
-                part = grad[:, k * LANES : (k + 1) * LANES]
+                part = grad[k * ch : (k + 1) * ch]
                 d_cols = d_cols + part
                 d_rows = jnp.where(
-                    lane == HALO - DIL + c * 8 + k, jnp.sum(part, axis=1, keepdims=True), d_rows
+                    lane == HALO - DIL + g * 8 + k, jnp.sum(part, axis=1, keepdims=True), d_rows
                 )
         d_rows = 0.5 * (d_rows + head_col * m_rows)
         d_cols = 0.5 * (d_cols + head_col * m_cols)
         dwin_ref[a] = dwin_ref[a] + d_rows
         dwin_ref[b] = dwin_ref[b] + d_cols
-        return v_acc, x_acc + jnp.where(m_rows != 0.0, gr * m_rows, 0.0) + jnp.where(
+        return x_acc + jnp.where(m_rows != 0.0, gr * m_rows, 0.0) + jnp.where(
             m_cols != 0.0, gc * m_cols, 0.0
         )
 
-    v_acc, x_acc = lax.fori_loop(
-        0, slots, slot, (jnp.zeros((ch, 48), F32), jnp.zeros((ch, LANES), F32))
-    )
+    x_acc = lax.fori_loop(0, slots, slot, jnp.zeros((ch, LANES), F32))
 
     proj_acc = jnp.zeros((2 * ch, c1), F32)
     for b in range(blocks):
@@ -205,13 +213,20 @@
         proj_acc = proj_acc + jnp.dot(both, fwin_ref[b], preferred_element_type=F32)
     proj_acc = pad_to(proj_acc[:ch] + proj_acc[ch:], ch, LANES)
 
-    v_pad = pad_to(v_acc, ch, LANES)
-    v_pad = v_pad + pltpu.roll(v_pad, LANES - 3, 1)
-    sums = jnp.zeros((ch, LANES), F32)
-    for dy in range(3):
-        first = 2 * ch + 3 * dy
-        moved = pltpu.roll(v_pad, 2 * ch - 13 * dy, 1)
-        sums = jnp.where((lane >= first) & (lane < first + 3), moved, sums)
+    wide = lax.broadcasted_iota(jnp.int32, (ch, 240), 1)
+    v_sum = jnp.zeros((ch, 240), F32)
+    for k in range(8):
+        v_sum = v_sum + jnp.where(wide % 8 == k, v_ref[k * ch : (k + 1) * ch], 0.0)
+    hi, lo = split_two(v_sum)
+    source = lax.broadcasted_iota(jnp.int32, (240, LANES), 0)
+    place = 2 * ch + 3 * (source // 80) + source % 80 % 24 // 8
+    select = (source % 80 < 48) & (lax.broadcasted_iota(jnp.int32, (240, LANES), 1) == place)
+    sums = jnp.dot(
+        jnp.concatenate([hi, lo], axis=0).astype(BF16),
+        select.astype(F32).astype(BF16),
+        preferred_element_type=F32,
+    )
+    sums = sums[:ch] + sums[ch:]
     sums = jnp.where(lane == 2 * ch + 9, jnp.sum(x_acc, axis=1, keepdims=True), sums)
     sums_hi, sums_lo = split_two(sums)
     sums = sums_hi + pltpu.roll(sums_lo, 10, 1)
@@ -293,7 +308,6 @@
     sequence_length = blocks * bins
     slots = tile_table.shape[2]
     scale = 1.0 / (sequence_length * bins)
-    frame = bins + 2 * DIL
 
     all_feats = lax.all_to_all(
         jnp.broadcast_to(feats, (devices,) + feats.shape[1:]), ("row", "col"), 0, 0, tiled=True
@@ -316,8 +330,11 @@
             pltpu.VMEM((blocks, LANES, c1), BF16),
             pltpu.VMEM((blocks, ch, LANES), F32),
             pltpu.VMEM((blocks, ch, LANES), F32),
-            pltpu.VMEM((ch, frame * LANES), BF16),
-            pltpu.VMEM((16, (bins + 32) * LANES), BF16),
+            pltpu.VMEM((8 * ch, (bins // 8 + 2) * LANES), BF16),
+            pltpu.VMEM((80, (bins // 8 + 4) * LANES), BF16),
+            pltpu.VMEM((8 * ch, 240), F32),
+            pltpu.VMEM((144, 8 * ch), BF16),
+            pltpu.VMEM((8 * ch, 240), BF16),
         ],
         compiler_params=params,
         name="tiles",

time: 78.8 us -> 51.4 us (0.65)
  Pallas kernels: 41.2 us -> 13.8 us
    pallas_call x1, Pallas kernels: 39.7 us -> 12.4 us  [body(): pl.pallas_call(functools.partial(tiles_kernel, rows_dev, slots), out_shap...]
  transfers between devices with their start and end apart: 2 -> 2, of which waited for: 2 -> 2; matrix products, arithmetic and copies ran while one was open for 1% -> 2% of each run, Pallas kernels for 0% -> 0%
where the time goes in v2:
time: 51.4 us; the launch traced here: 51.1 us
  blocking collectives  15.4 us (30%)
  Pallas kernels  13.8 us (27%)
  waiting for transfers between devices  10.1 us (20%)
  starting transfers between devices  7.3 us (14%)
  local copies, waits for them, and re-layouts  3.74 us (7%)
  between operations  0.69 us (1%)
    all_to_all x1, blocking collectives, body(): got = lax.all_to_all(partial, ('row', 'col'), 0, 0, tiled=True)  15.4 us
    pallas_call x1, Pallas kernels, body(): pl.pallas_call(functools.partial(tiles_kernel, rows_dev, slots), out_shap...  12.4 us
    all_to_all x1, waiting for transfers between devices, body(): lax.all_to_all(jnp.broadcast_to(feats, (devices,) + feats.shape[1:]), ('r...  9.69 us
    all_to_all x1, starting transfers between devices, body(): lax.all_to_all(jnp.broadcast_to(feats, (devices,) + feats.shape[1:]), ('r...  7.3 us
    unnamed x15, local copies, waits for them, and re-layouts  2.31 us
    broadcast_in_dim x1, local copies, waits for them, and re-layouts, body(): jnp.broadcast_to(feats, (devices,) + feats.shape[1:])  1.43 us
    pallas_call x1, Pallas kernels, body(): pl.pallas_call(functools.partial(finish_kernel, scale, 1.0 / math.sqrt(se...  1.42 us
  transfers between devices with their start and end apart: 2, of which 2 were waited for; matrix products, arithmetic and copies ran while one was open for 2% of the time, Pallas kernels for 0%

profile of v2, /device:TPU:0, one launch (start us, length us, event | category | flops | bytes accessed | tf_op | source)
XLA Modules:
  0.0 51.1 jit_solution(4623726295753624798)
XLA Ops:
  0.6 1.4 %broadcast_in_dim.8 = bf16[32,2,16,96]{3,2,1,0:T(8,128)(2,1)} broadcast(bf16[2,16,96]{2,1,0:T(8,128)(2,1)} %bitcast.2), dimensions={1,2,3} | broadcast | bytes 202752 | tf_op jit(solution)/shard_map/broadcast_in_dim | solution.py:313
  2.1 0.0 copy-start.3
  2.1 0.0 copy-start.2
  2.1 7.3 %all-to-all-start = ((bf16[32,2,16,96]{3,2,1,0:T(8,128)(2,1)}), bf16[32,2,16,96]{3,2,1,0:T(8,128)(2,1)S(1)}, u32[]{:S(2)}, u32[]{:S(2)}) async-start(bf16[32,2,16,96]{3,2,1,0:T(8,128)(2,1)} %broadcast_in_dim.8), calls=%async_computation | async-start | bytes 524288 | tf_op jit(solution)/shard_map/all_to_all | solution.py:312
  9.4 0.0 copy-done.3
  9.4 0.1 copy.10.proj_ref
  9.5 0.0 copy-done.2
  9.5 0.0 copy-start.4
  9.5 0.0 copy-start
  9.6 0.6 %copy-done.4 = s32[1,1,5,3]{2,1,3,0:T(1,128)S(1)} copy-done((s32[1,1,5,3]{2,1,3,0:T(1,128)S(1)}, s32[1,1,5,3]{2,1,3,0:T(1,128)}, u32[]{:S(2)}) %copy-start.4) | copy-done | bytes 84
  10.2 0.0 copy-start.1
  10.2 0.1 copy.12.table_ref
  10.3 9.7 %all-to-all-done.feats_ref = bf16[32,2,16,96]{3,2,1,0:T(8,128)(2,1)S(1)} async-done(((bf16[32,2,16,96]{3,2,1,0:T(8,128)(2,1)}), bf16[32,2,16,96]{3,2,1,0:T(8,128)(2,1)S(1)}, u32[]{:S(2)}, u32[]{:S(2)}) %all-to-all-start) | async-done | bytes 196640 | tf_op jit(solution)/shard_map/all_to_all | solution.py:312
  20.0 0.0 copy-done
  20.0 0.0 copy-done.1
  20.0 12.4 %tiles.1 = bf16[32,48,128]{2,1,0:T(8,128)(2,1)S(1)} custom-call(bf16[32,2,16,96]{3,2,1,0:T(8,128)(2,1)S(1)} %all-to-all-done.feats_ref, bf16[96,48]{1,0:T(8,128)(2,1)S(1)} %copy.10.proj_ref, bf16[48,9,48]{2,1,0:T(8,128)(2,1)S(1)} %copy.11.conv_ref, f32[48]{0:T(128)S(1)} %copy-done.1, s32[1,1,5,3]{3,2,1,0:T(8,128)S(1)} %copy.12.table_ref, ...), custom_call_target="tpu_custom_call" | custom-call | tf_op jit(solution)/shard_map/tiles/pallas_call | solution.py:324
  32.4 15.4 %all_to_all.10.got_ref = bf16[32,48,128]{2,1,0:T(8,128)(2,1)S(1)} all-to-all(bf16[32,48,128]{2,1,0:T(8,128)(2,1)S(1)} %tiles.1), channel_id=1, replica_groups=mesh['row'=8,'col'=4] {'row','col'}, dimensions={0} | all-to-all | bytes 786432 | tf_op jit(solution)/shard_map/all_to_all | solution.py:342
  47.8 1.4 %finish.1 = (f32[1,2,16,96]{3,2,1,0:T(8,128)}, f32[48,9,48]{2,1,0:T(8,128)S(1)}, f32[1,48]{1,0:T(1,128)}, f32[48,48]{1,0:T(8,128)S(1)}) custom-call(bf16[32,48,128]{2,1,0:T(8,128)(2,1)S(1)} %all_to_all.10.got_ref, bf16[96,48]{1,0:T(8,128)(2,1)S(1)} %copy.10.proj_ref, bf16[48,9,48]{2,1,0:T(8,128)(2,1)S(1)} %copy.11.conv_ref, f32[48]{0:T(128)S(1)} %copy-done.1), custom_call_target="tpu_custom_call" | custom-call | tf_op jit(solution)/shard_map/finish/pallas_call | solution.py:343
  49.2 0.0 collective-permute-start
  49.2 0.8 %copy.16 = f32[48,9,48]{2,0,1:T(8,128)} copy(f32[48,9,48]{2,1,0:T(8,128)S(1)} %get-tuple-element.14) | data formatting | bytes 165888
  50.0 0.4 collective-permute-done
  50.4 0.7 %copy.15 = f32[96,48]{0,1:T(8,128)} copy(f32[96,48]{1,0:T(8,128)S(1)} %pad_maximum_fusion) | data formatting | bytes 36864
  (3 shorter events, 0.1 us)
Async XLA Ops:
  2.1 7.3 %copy-start.3 = (bf16[96,48]{0,1:T(8,128)(2,1)S(1)}, bf16[96,48]{0,1:T(8,128)(2,1)}, u32[]{:S(2)}) copy-start(bf16[96,48]{0,1:T(8,128)(2,1)} %param.7) | copy-start | bytes 27652
  2.1 7.4 %copy-start.2 = (bf16[48,9,48]{2,0,1:T(8,128)(2,1)S(1)}, bf16[48,9,48]{2,0,1:T(8,128)(2,1)}, u32[]{:S(2)}) copy-start(bf16[48,9,48]{2,0,1:T(8,128)(2,1)} %param.8) | copy-start | bytes 124420
  2.1 17.9 %all-to-all-start = ((bf16[32,2,16,96]{3,2,1,0:T(8,128)(2,1)}), bf16[32,2,16,96]{3,2,1,0:T(8,128)(2,1)S(1)}, u32[]{:S(2)}, u32[]{:S(2)}) async-start(bf16[32,2,16,96]{3,2,1,0:T(8,128)(2,1)} %broadcast_in_dim.8), calls=%async_computation | async-start | bytes 524288 | tf_op jit(solution)/shard_map/all_to_all | solution.py:312
  9.5 0.7 %copy-start.4 = (s32[1,1,5,3]{2,1,3,0:T(1,128)S(1)}, s32[1,1,5,3]{2,1,3,0:T(1,128)}, u32[]{:S(2)}) copy-start(s32[1,1,5,3]{2,1,3,0:T(1,128)} %param.10) | copy-start | bytes 184
  9.5 10.5 %copy-start = (f32[1,1,5,64,64]{4,3,2,1,0:T(8,128)S(1)}, f32[1,1,5,64,64]{4,3,2,1,0:T(8,128)}, u32[]{:S(2)}) copy-start(f32[1,1,5,64,64]{4,3,2,1,0:T(8,128)} %targets_ref.1) | copy-start | bytes 245764
  10.2 9.8 %copy-start.1 = (f32[48]{0:T(128)S(1)}, f32[48]{0:T(128)}, u32[]{:S(2)}) copy-start(f32[48]{0:T(128)} %head_ref.3) | copy-start | bytes 580
  49.2 1.2 %collective-permute-start = (f32[48,48]{1,0:T(8,128)S(1)}, f32[48,48]{1,0:T(8,128)S(1)}, u32[]{:S(2)}, u32[]{:S(2)}) collective-permute-start(f32[48,48]{1,0:T(8,128)S(1)} %get-tuple-element.9), channel_id=1, source_target_pairs={{0,1},{1,0},{2,3},{3,2},{4,5},{5,4},{6,7},{7,6},{8,9},{9,8},{10,11... | collective-permute-start | bytes 27656 | tf_op jit(solution)/shard_map/ppermute | solution.py:356

commit v3 on v2

--- a/solution.py
+++ b/solution.py
@@ -45,67 +45,26 @@
     return jnp.concatenate(groups, axis=0)
 
 
-def tiles_kernel(
-    rows_dev,
-    slots,
-    feats_ref,
-    proj_ref,
-    conv_ref,
-    head_ref,
-    table_ref,
-    targets_ref,
-    out_ref,
-    fwin_ref,
-    gwin_ref,
-    dwin_ref,
-    u_ref,
-    m_ref,
-    v_ref,
-    forward_ref,
-    backward_ref,
-):
-    n_src, _, chunk, c1 = feats_ref.shape
-    cols_dev = n_src // rows_dev
-    blocks = 2 * rows_dev
-    bins = cols_dev * chunk
-    ch = proj_ref.shape[1]
-    lane = lane_iota(ch)
-    lane1 = lane_iota(1)
-
-    def chunks_of(b):
-        r, half = (b, 0) if b < rows_dev else (blocks - 1 - b, 1)
-        return [feats_ref[r * cols_dev + c, half] for c in range(cols_dev)]
-
-    proj_t = jnp.transpose(pad_to(proj_ref[...].astype(F32), LANES, LANES))[:ch, :c1].astype(BF16)
-    zero_halo = jnp.zeros((HALO, c1), BF16)
-    for b in range(blocks):
-        before = chunks_of(b - 1)[-1][chunk - HALO :] if b > 0 else zero_halo
-        after = chunks_of(b + 1)[0][:HALO] if b < blocks - 1 else zero_halo
-        tail = jnp.zeros((LANES - bins - 2 * HALO, c1), BF16)
-        window = jnp.concatenate([before] + chunks_of(b) + [after, tail], axis=0)
-        fwin_ref[b] = window
-        g = lax.dot_general(proj_t, window, (((1,), (1,)), ((), ())), preferred_element_type=F32)
-        g = 0.5 * g.astype(BF16).astype(F32)
-        if b == 0:
-            g = jnp.where(lane < HALO, OUTSIDE, g)
-        if b == blocks - 1:
-            g = jnp.where(lane >= HALO + bins, OUTSIDE, g)
-        gwin_ref[b] = g
-        dwin_ref[b] = jnp.zeros((ch, LANES), F32)
-
-    taps = jnp.zeros((9, ch), F32)
-    for o in range(ch):
-        taps = taps + head_ref[o] * conv_ref[o].astype(F32)
+def taps_kernel(conv_ref, head_ref, table_ref, forward_ref, backward_ref, entries_ref):
+    ch = conv_ref.shape[1]
+    for s in range(table_ref.shape[3]):
+        for k in range(3):
+            entries_ref[k, s] = table_ref[0, k, 0, s]
+    head_col = column_of(head_ref, ch)
+    taps = [
+        jnp.sum(head_col[:, :ch] * conv_ref[t].astype(F32), axis=0, keepdims=True)
+        for t in range(9)
+    ]
     wide = (8, 8 * ch)
     diagonal = lax.broadcasted_iota(jnp.int32, wide, 1) // ch == lax.broadcasted_iota(
         jnp.int32, wide, 0
     )
     hi_tiles, lo_tiles = [
         [
-            jnp.where(diagonal, jnp.broadcast_to(row, wide), 0.0)
-            for row in jnp.split(jnp.concatenate([values] * 8, axis=1), 9, axis=0)
+            jnp.where(diagonal, jnp.broadcast_to(jnp.concatenate([row] * 8, axis=1), wide), 0.0)
+            for row in rows
         ]
-        for values in split_two(taps)
+        for rows in zip(*[split_two(row) for row in taps])
     ]
     forward_rows, backward_rows = [], []
     for dy in range(3):
@@ -118,8 +77,55 @@
     )[:, :240].astype(BF16)
     forward_ref[...] = forward_taps
     backward_ref[...] = backward_taps
+
+
+def tiles_kernel(
+    rows_dev,
+    slots,
+    feats_ref,
+    proj_ref,
+    forward_ref,
+    backward_ref,
+    head_ref,
+    table_ref,
+    targets_ref,
+    out_ref,
+    fwin_ref,
+    gwin_ref,
+    dwin_ref,
+    u_ref,
+    m_ref,
+    v_ref,
+):
+    n_src, _, chunk, c1 = feats_ref.shape
+    cols_dev = n_src // rows_dev
+    blocks = 2 * rows_dev
+    bins = cols_dev * chunk
+    ch = proj_ref.shape[0]
+    lane = lane_iota(ch)
+    lane1 = lane_iota(1)
+
+    def chunks_of(b):
+        r, half = (b, 0) if b < rows_dev else (blocks - 1 - b, 1)
+        return [feats_ref[r * cols_dev + c, half] for c in range(cols_dev)]
+
+    zero_halo = jnp.zeros((HALO, c1), BF16)
+    for b in range(blocks):
+        before = chunks_of(b - 1)[-1][chunk - HALO :] if b > 0 else zero_halo
+        after = chunks_of(b + 1)[0][:HALO] if b < blocks - 1 else zero_halo
+        tail = jnp.zeros((LANES - bins - 2 * HALO, c1), BF16)
+        window = jnp.concatenate([before] + chunks_of(b) + [after, tail], axis=0)
+        fwin_ref[b] = window
+        g = lax.dot_general(proj_ref[...], window, (((1,), (1,)), ((), ())), preferred_element_type=F32)
+        g = 0.5 * g.astype(BF16).astype(F32)
+        if b == 0:
+            g = jnp.where(lane < HALO, OUTSIDE, g)
+        if b == blocks - 1:
+            g = jnp.where(lane >= HALO + bins, OUTSIDE, g)
+        gwin_ref[b] = g.astype(BF16)
+        dwin_ref[b] = jnp.zeros((ch, LANES), F32)
+
     head_col = column_of(head_ref, ch)
-
     groups = bins // 8
     m_ref[:, : 2 * LANES] = jnp.zeros((80, 2 * LANES), BF16)
     m_ref[:, (groups + 2) * LANES :] = jnp.zeros((80, 2 * LANES), BF16)
@@ -127,30 +133,31 @@
     inner = (lane1 >= HALO) & (lane1 < HALO + bins)
 
     def slot(s, x_acc):
-        a, b, live = table_ref[0, 0, s, 0], table_ref[0, 0, s, 1], table_ref[0, 0, s, 2]
+        a, b, live = table_ref[0, s], table_ref[1, s], table_ref[2, s]
         weight = jnp.where(inner, live.astype(F32), 0.0)
-        gr, gc = gwin_ref[a], gwin_ref[b]
-        for g in range(groups + 2):
+        gr, gc = gwin_ref[a].astype(F32), gwin_ref[b].astype(F32)
+        pred_r = jnp.sum(jnp.where(lane < HALO + bins, head_col * gr, 0.0), axis=0, keepdims=True)
+        pred_c = jnp.sum(jnp.where(lane < HALO + bins, head_col * gc, 0.0), axis=0, keepdims=True)
+        pred_r = jnp.transpose(jnp.broadcast_to(pred_r, (LANES, LANES)))
+
+        def activations(g):
             for k in range(8):
                 at = HALO - DIL + g * 8 + k
                 x = gr[:, at : at + 1] + gc
                 u_ref[k * ch : (k + 1) * ch, g * LANES : (g + 1) * LANES] = jnp.maximum(
                     x, 0.0
                 ).astype(BF16)
-        pred_r = jnp.sum(jnp.where(lane < HALO + bins, head_col * gr, 0.0), axis=0, keepdims=True)
-        pred_c = jnp.sum(jnp.where(lane < HALO + bins, head_col * gc, 0.0), axis=0, keepdims=True)
-        pred_r = jnp.transpose(jnp.broadcast_to(pred_r, (LANES, LANES)))
-        z = jnp.dot(forward_ref[...], u_ref[...], preferred_element_type=F32)
-        m_cols = jnp.zeros((8, LANES), F32)
-        row_sums = [jnp.zeros((HALO, LANES), F32)]
-        for c in range(groups):
+            return jnp.dot(
+                forward_ref[...],
+                u_ref[:, g * LANES : (g + 1) * LANES],
+                preferred_element_type=F32,
+            )
+
+        def misfit(c, z):
             terms = []
             for dx in range(3):
                 tiles = [
-                    z[
-                        48 * dy + 24 * p + 8 * dx : 48 * dy + 24 * p + 8 * dx + 8,
-                        (c + dy) * LANES : (c + dy + 1) * LANES,
-                    ]
+                    z[c + dy][48 * dy + 24 * p + 8 * dx : 48 * dy + 24 * p + 8 * dx + 8]
                     for dy in range(3)
                     for p in range(2)
                 ]
@@ -164,8 +171,6 @@
             )
             at = HALO + c * 8
             m = jnp.where(inner, (conv + pred_c + pred_r[at : at + 8] - goal) * weight, 0.0)
-            m_cols = m_cols + m
-            row_sums.append(jnp.broadcast_to(jnp.sum(m, axis=1, keepdims=True), (8, LANES)))
             his, los = [], []
             for moved in (pltpu.roll(m, LANES - DIL, 1), m, pltpu.roll(m, DIL, 1)):
                 hi, lo = split_two(moved)
@@ -174,11 +179,36 @@
             m_ref[:, (c + 2) * LANES : (c + 3) * LANES] = jnp.concatenate(
                 his + los + his + [jnp.zeros((8, LANES), F32)], axis=0
             ).astype(BF16)
+            return m
+
+        def gradients(g, d_rows, d_cols):
+            cols = slice(g * LANES, (g + 1) * LANES)
+            m3 = jnp.concatenate(
+                [m_ref[:, (g + 2 - dy) * LANES : (g + 3 - dy) * LANES] for dy in range(3)], axis=0
+            )
+            up = jnp.dot(backward_ref[...], m3, preferred_element_type=F32)
+            grad = jnp.where(u_ref[:, cols].astype(F32) > 0.0, up, 0.0)
+            for k in range(8):
+                part = grad[k * ch : (k + 1) * ch]
+                d_cols = d_cols + part
+                d_rows = jnp.where(
+                    lane == HALO - DIL + g * 8 + k, jnp.sum(part, axis=1, keepdims=True), d_rows
+                )
+            return d_rows, d_cols
+
+        z, m_cols, row_sums = [], jnp.zeros((8, LANES), F32), [jnp.zeros((HALO, LANES), F32)]
+        d_rows = d_cols = jnp.zeros((ch, LANES), F32)
+        for g in range(groups + 2):
+            z.append(activations(g))
+            if g >= 2:
+                m = misfit(g - 2, z)
+                m_cols = m_cols + m
+                row_sums.append(jnp.broadcast_to(jnp.sum(m, axis=1, keepdims=True), (8, LANES)))
+        for g in range(groups + 2):
+            d_rows, d_cols = gradients(g, d_rows, d_cols)
         row_sums.append(jnp.zeros((LANES - HALO - bins, LANES), F32))
         m_rows = jnp.transpose(jnp.concatenate(row_sums, axis=0))[:1]
         m_cols = jnp.sum(m_cols, axis=0, keepdims=True)
-        d_rows = jnp.zeros((ch, LANES), F32)
-        d_cols = jnp.zeros((ch, LANES), F32)
         frame_cols = (groups + 2) * LANES
         m3 = jnp.concatenate(
             [m_ref[:, (2 - dy) * LANES : (2 - dy) * LANES + frame_cols] for dy in range(3)], axis=0
@@ -186,16 +216,6 @@
         v_ref[...] += lax.dot_general(
             u_ref[...], m3, (((1,), (1,)), ((), ())), preferred_element_type=F32
         )
-        for g in range(groups + 2):
-            cols = slice(g * LANES, (g + 1) * LANES)
-            up = jnp.dot(backward_ref[...], m3[:, cols], preferred_element_type=F32)
-            grad = jnp.where(u_ref[:, cols].astype(F32) > 0.0, up, 0.0)
-            for k in range(8):
-                part = grad[k * ch : (k + 1) * ch]
-                d_cols = d_cols + part
-                d_rows = jnp.where(
-                    lane == HALO - DIL + g * 8 + k, jnp.sum(part, axis=1, keepdims=True), d_rows
-                )
         d_rows = 0.5 * (d_rows + head_col * m_rows)
         d_cols = 0.5 * (d_cols + head_col * m_cols)
         dwin_ref[a] = dwin_ref[a] + d_rows
@@ -264,15 +284,13 @@
     scale, root, got_ref, proj_ref, conv_ref, head_ref, feat_ref, conv_out_ref, head_out_ref, half_ref
 ):
     n_src, ch, _ = got_ref.shape
-    c1 = proj_ref.shape[0]
     part = feat_ref.shape[2]
     total = got_ref[0].astype(F32)
     for d in range(1, n_src):
         total = total + got_ref[d].astype(F32)
+    half_ref[...] = total[:, ch : 2 * ch] * scale
     whole_t = jnp.transpose(pad_to(total, LANES, LANES))
-    half_ref[...] = whole_t[ch : 2 * ch, :ch] * scale
-
-    proj_t = jnp.transpose(pad_to(proj_ref[...].astype(F32), LANES, LANES))[:ch, :c1].astype(BF16)
+    proj_t = proj_ref[...]
     hi, lo = split_two(total[: 2 * part, :ch])
     feat = jnp.dot(hi.astype(BF16), proj_t, preferred_element_type=F32) + jnp.dot(
         lo.astype(BF16), proj_t, preferred_element_type=F32
@@ -282,19 +300,13 @@
         feat_ref[0, half] = feat[half * part : (half + 1) * part]
 
     sums = whole_t[2 * ch : 2 * ch + 10, :ch] + whole_t[2 * ch + 10 : 2 * ch + 20, :ch]
-    v = sums[:9]
-    sub = lax.broadcasted_iota(jnp.int32, (8, ch), 0)
-    groups = []
-    for g in range(ch // 8):
-        acc = jnp.zeros((8, ch), F32)
-        for k in range(8):
-            o = g * 8 + k
-            conv_out_ref[o] = v * (head_ref[o] * scale)
-            product = jnp.sum(conv_ref[o].astype(F32) * v, axis=0, keepdims=True)
-            acc = jnp.where(sub == k, product, acc)
-        groups.append(acc)
-    products = pad_to(jnp.concatenate(groups, axis=0), LANES, LANES)
-    head_sum = jnp.sum(jnp.transpose(products), axis=0, keepdims=True)[:, :ch]
+    head_col = column_of(head_ref, ch)[:, :ch] * scale
+    products = jnp.zeros((ch, ch), F32)
+    for t in range(9):
+        v = sums[t : t + 1]
+        conv_out_ref[t] = head_col * v
+        products = products + conv_ref[t].astype(F32) * v
+    head_sum = jnp.sum(jnp.transpose(pad_to(products, LANES, LANES)), axis=0, keepdims=True)[:, :ch]
     head_out_ref[...] = (sums[9:10] + head_sum) * scale
 
 
@@ -303,6 +315,7 @@
     devices = rows_dev * cols_dev
     _, halves, part, c1 = feats.shape
     ch = proj_weight.shape[1]
+    proj_t, conv_t = proj_weight.T, conv_weight.transpose(1, 0, 2)
     bins = part * cols_dev
     blocks = halves * rows_dev
     sequence_length = blocks * bins
@@ -321,30 +334,41 @@
     vmem = pl.BlockSpec(memory_space=pltpu.VMEM)
     smem = pl.BlockSpec(memory_space=pltpu.SMEM)
     params = pltpu.CompilerParams(vmem_limit_bytes=48 * 1024 * 1024)
+    forward, backward, entries = pl.pallas_call(
+        taps_kernel,
+        out_shape=(
+            jax.ShapeDtypeStruct((144, 8 * ch), BF16),
+            jax.ShapeDtypeStruct((8 * ch, 240), BF16),
+            jax.ShapeDtypeStruct((3, slots), jnp.int32),
+        ),
+        in_specs=[vmem, smem, smem],
+        out_specs=(vmem, vmem, smem),
+        compiler_params=params,
+        cost_estimate=pl.CostEstimate(flops=10**7, bytes_accessed=10**6, transcendentals=0),
+        name="taps",
+    )(conv_t, head_weight, tile_table.transpose(0, 3, 1, 2))
     partial = pl.pallas_call(
         functools.partial(tiles_kernel, rows_dev, slots),
         out_shape=jax.ShapeDtypeStruct((devices, ch, LANES), BF16),
-        in_specs=[vmem, vmem, vmem, smem, smem, vmem],
+        in_specs=[vmem, vmem, vmem, vmem, smem, smem, vmem],
         out_specs=vmem,
         scratch_shapes=[
             pltpu.VMEM((blocks, LANES, c1), BF16),
-            pltpu.VMEM((blocks, ch, LANES), F32),
+            pltpu.VMEM((blocks, ch, LANES), BF16),
             pltpu.VMEM((blocks, ch, LANES), F32),
             pltpu.VMEM((8 * ch, (bins // 8 + 2) * LANES), BF16),
             pltpu.VMEM((80, (bins // 8 + 4) * LANES), BF16),
             pltpu.VMEM((8 * ch, 240), F32),
-            pltpu.VMEM((144, 8 * ch), BF16),
-            pltpu.VMEM((8 * ch, 240), BF16),
         ],
         compiler_params=params,
         name="tiles",
-    )(all_feats, proj_weight, conv_weight, head_weight, tile_table, targets)
+    )(all_feats, proj_t, forward, backward, head_weight, entries, targets)
     got = lax.all_to_all(partial, ("row", "col"), 0, 0, tiled=True)
     feat_grad, conv_grad, head_grad, mine = pl.pallas_call(
         functools.partial(finish_kernel, scale, 1.0 / math.sqrt(sequence_length)),
         out_shape=(
             jax.ShapeDtypeStruct(feats.shape, F32),
-            jax.ShapeDtypeStruct(conv_weight.shape, F32),
+            jax.ShapeDtypeStruct(conv_t.shape, F32),
             jax.ShapeDtypeStruct((1, ch), F32),
             jax.ShapeDtypeStruct((ch, ch), F32),
         ),
@@ -352,13 +376,13 @@
         out_specs=(vmem, vmem, vmem, vmem),
         compiler_params=params,
         name="finish",
-    )(got, proj_weight, conv_weight, head_weight)
+    )(got, proj_t, conv_t, head_weight)
     other = lax.ppermute(mine, "col", [(c, c ^ 1) for c in range(cols_dev)])
     odd = lax.axis_index("col") % 2 == 1
     proj_grad = jnp.concatenate(
-        [jnp.where(odd, other, mine), jnp.where(odd, mine, other)], axis=0
-    )
-    return feat_grad, proj_grad, conv_grad, head_grad.reshape(ch)
+        [jnp.where(odd, other, mine), jnp.where(odd, mine, other)], axis=1
+    )
+    return feat_grad, proj_grad.T, conv_grad.transpose(1, 0, 2), head_grad.reshape(ch)
 
 
 def solution(mesh):

time: 51.4 us -> 50.2 us (0.977)
  local copies, waits for them, and re-layouts: 3.74 us -> 2.11 us
  other arithmetic: 0.02 us -> 0.69 us
    unnamed x15 -> x10, local copies, waits for them, and re-layouts: 2.31 us -> 0.67 us
    pallas_call x0 -> x1, Pallas kernels: none -> 1.39 us  [body(): pl.pallas_call(taps_kernel, out_shape=(jax.ShapeDtypeStruct((144, 8 * ch)...]
    all_to_all x1, waiting for transfers between devices: 9.69 us -> 8.51 us  [body(): lax.all_to_all(jnp.broadcast_to(feats, (devices,) + feats.shape[1:]), ('r...]
    pallas_call x1, Pallas kernels: 12.4 us -> 11.2 us  [body(): pl.pallas_call(functools.partial(tiles_kernel, rows_dev, slots), out_shap...]
    ppermute x1, waiting for transfers between devices: 0.44 us -> 1.19 us  [body(): other = lax.ppermute(mine, 'col', [(c, c ^ 1) for c in range(cols_dev)])]
    transpose x0 -> x1, other arithmetic: none -> 0.69 us  [body(): return (feat_grad, proj_grad.T, conv_grad.transpose(1, 0, 2), head_grad.r...]
  transfers between devices with their start and end apart: 2 -> 2, of which waited for: 2 -> 2; matrix products, arithmetic and copies ran while one was open for 2% -> 0% of each run, Pallas kernels for 0% -> 3%
where the time goes in v3:
time: 50.2 us; the launch traced here: 49.9 us
  blocking collectives  15.4 us (31%)
  Pallas kernels  14 us (28%)
  waiting for transfers between devices  9.71 us (19%)
  starting transfers between devices  7.3 us (15%)
  local copies, waits for them, and re-layouts  2.11 us (4%)
  other arithmetic  0.69 us (1%)
  between operations  0.68 us (1%)
    all_to_all x1, blocking collectives, body(): got = lax.all_to_all(partial, ('row', 'col'), 0, 0, tiled=True)  15.4 us
    pallas_call x1, Pallas kernels, body(): pl.pallas_call(functools.partial(tiles_kernel, rows_dev, slots), out_shap...  11.2 us
    all_to_all x1, waiting for transfers between devices, body(): lax.all_to_all(jnp.broadcast_to(feats, (devices,) + feats.shape[1:]), ('r...  8.51 us
    all_to_all x1, starting transfers between devices, body(): lax.all_to_all(jnp.broadcast_to(feats, (devices,) + feats.shape[1:]), ('r...  7.3 us
    broadcast_in_dim x1, local copies, waits for them, and re-layouts, body(): jnp.broadcast_to(feats, (devices,) + feats.shape[1:])  1.44 us
    pallas_call x1, Pallas kernels, body(): pl.pallas_call(functools.partial(finish_kernel, scale, 1.0 / math.sqrt(se...  1.4 us
    pallas_call x1, Pallas kernels, body(): pl.pallas_call(taps_kernel, out_shape=(jax.ShapeDtypeStruct((144, 8 * ch)...  1.39 us
    ppermute x1, waiting for transfers between devices, body(): other = lax.ppermute(mine, 'col', [(c, c ^ 1) for c in range(cols_dev)])  1.19 us
  transfers between devices with their start and end apart: 2, of which 2 were waited for; matrix products, arithmetic and copies ran while one was open for 0% of the time, Pallas kernels for 3%

profile of v3, /device:TPU:0, one launch (start us, length us, event | category | flops | bytes accessed | tf_op | source)
XLA Modules:
  0.0 49.9 jit_solution(12197631702479982075)
XLA Ops:
  0.6 1.4 %broadcast_in_dim.8 = bf16[32,2,16,96]{3,2,1,0:T(8,128)(2,1)} broadcast(bf16[2,16,96]{2,1,0:T(8,128)(2,1)} %bitcast.13), dimensions={1,2,3} | broadcast | bytes 202752 | tf_op jit(solution)/shard_map/broadcast_in_dim | solution.py:326
  2.1 0.0 copy-start
  2.1 0.0 copy-start.1
  2.1 7.3 %all-to-all-start = ((bf16[32,2,16,96]{3,2,1,0:T(8,128)(2,1)}), bf16[32,2,16,96]{3,2,1,0:T(8,128)(2,1)S(1)}, u32[]{:S(2)}, u32[]{:S(2)}) async-start(bf16[32,2,16,96]{3,2,1,0:T(8,128)(2,1)} %broadcast_in_dim.8), calls=%async_computation | async-start | bytes 524288 | tf_op jit(solution)/shard_map/all_to_all | solution.py:325
  9.4 0.0 copy-start.4
  9.4 0.0 copy-start.3
  9.4 0.0 copy-done
  9.4 0.6 %copy-done.4 = s32[1,1,5,3]{2,1,3,0:T(1,128)S(1)} copy-done((s32[1,1,5,3]{2,1,3,0:T(1,128)S(1)}, s32[1,1,5,3]{2,1,3,0:T(1,128)}, u32[]{:S(2)}) %copy-start.4) | copy-done | bytes 84
  10.1 0.0 copy-done.3
  10.1 0.0 copy-start.2
  10.1 1.4 %taps.1 = (bf16[144,384]{1,0:T(8,128)(2,1)S(1)}, bf16[384,240]{1,0:T(8,128)(2,1)S(1)}, s32[3,5]{1,0:T(4,128)S(1)}) custom-call(bf16[9,48,48]{2,1,0:T(8,128)(2,1)S(1)} %bitcast.8, f32[48]{0:T(128)S(1)} %copy-done.3, s32[1,3,1,5]{3,2,1,0:T(1,128)S(1)} %bitcast.12), custom_call_target="tpu_custom_call" | custom-call | flops 10000000 | bytes 1000000 | tf_op jit(solution)/shard_map/taps/pallas_call | solution.py:337
  11.5 8.5 %all-to-all-done.feats_ref = bf16[32,2,16,96]{3,2,1,0:T(8,128)(2,1)S(1)} async-done(((bf16[32,2,16,96]{3,2,1,0:T(8,128)(2,1)}), bf16[32,2,16,96]{3,2,1,0:T(8,128)(2,1)S(1)}, u32[]{:S(2)}, u32[]{:S(2)}) %all-to-all-start) | async-done | bytes 196640 | tf_op jit(solution)/shard_map/all_to_all | solution.py:325
  20.0 0.0 copy-done.1
  20.0 0.0 copy-done.2
  20.0 11.2 %tiles.1 = bf16[32,48,128]{2,1,0:T(8,128)(2,1)S(1)} custom-call(bf16[32,2,16,96]{3,2,1,0:T(8,128)(2,1)S(1)} %all-to-all-done.feats_ref, bf16[48,96]{1,0:T(8,128)(2,1)S(1)} %bitcast.10, bf16[144,384]{1,0:T(8,128)(2,1)S(1)} %get-tuple-element.11.forward_ref, bf16[384,240]{1,0:T(8,128)(2,1)S(1)} %get-tuple-element.12.backward_ref, f32[48]{0:T(128)S(1)} %copy-done.3, ...), custom_call_target="tpu_custom_call" | custom-call | tf_op jit(solution)/shard_map/tiles/pallas_call | solution.py:350
  31.2 15.4 %all_to_all.10.got_ref = bf16[32,48,128]{2,1,0:T(8,128)(2,1)S(1)} all-to-all(bf16[32,48,128]{2,1,0:T(8,128)(2,1)S(1)} %tiles.1), channel_id=1, replica_groups=mesh['row'=8,'col'=4] {'row','col'}, dimensions={0} | all-to-all | bytes 786432 | tf_op jit(solution)/shard_map/all_to_all | solution.py:366
  46.6 1.4 %finish.1 = (f32[1,2,16,96]{3,2,1,0:T(8,128)}, f32[9,48,48]{2,1,0:T(8,128)}, f32[1,48]{1,0:T(1,128)}, f32[48,48]{1,0:T(8,128)S(1)}) custom-call(bf16[32,48,128]{2,1,0:T(8,128)(2,1)S(1)} %all_to_all.10.got_ref, bf16[48,96]{1,0:T(8,128)(2,1)S(1)} %bitcast.11, bf16[9,48,48]{2,1,0:T(8,128)(2,1)S(1)} %bitcast.9, f32[48]{0:T(128)S(1)} %copy-done.3), custom_call_target="tpu_custom_call" | custom-call | tf_op jit(solution)/shard_map/finish/pallas_call | solution.py:367
  48.0 0.0 collective-permute-start
  48.0 1.2 %collective-permute-done = f32[48,48]{1,0:T(8,128)S(1)} collective-permute-done((f32[48,48]{1,0:T(8,128)S(1)}, f32[48,48]{1,0:T(8,128)S(1)}, u32[]{:S(2)}, u32[]{:S(2)}) %collective-permute-start) | collective-permute-done | bytes 9248 | tf_op jit(solution)/shard_map/ppermute | solution.py:380
  49.2 0.7 %maximum_bitcast_fusion = f32[96,48]{0,1:T(8,128)} fusion(f32[48,48]{1,0:T(8,128)S(1)} %get-tuple-element.19, f32[48,48]{1,0:T(8,128)S(1)} %get-tuple-element.18), kind=kLoop, calls=%fused_computation | loop fusion | flops 4608 | bytes 36864 | tf_op jit(solution)/shard_map/transpose | solution.py:385
  (1 shorter events, 0.0 us)
Async XLA Ops:
  2.1 7.3 %copy-start = (bf16[48,9,48]{2,0,1:T(8,128)(2,1)S(1)}, bf16[48,9,48]{2,0,1:T(8,128)(2,1)}, u32[]{:S(2)}) copy-start(bf16[48,9,48]{2,0,1:T(8,128)(2,1)} %param.8) | copy-start | bytes 124420
  2.1 17.9 %copy-start.1 = (f32[1,1,5,64,64]{4,3,2,1,0:T(8,128)S(1)}, f32[1,1,5,64,64]{4,3,2,1,0:T(8,128)}, u32[]{:S(2)}) copy-start(f32[1,1,5,64,64]{4,3,2,1,0:T(8,128)} %targets_ref.1) | copy-start | bytes 245764
  2.1 17.9 %all-to-all-start = ((bf16[32,2,16,96]{3,2,1,0:T(8,128)(2,1)}), bf16[32,2,16,96]{3,2,1,0:T(8,128)(2,1)S(1)}, u32[]{:S(2)}, u32[]{:S(2)}) async-start(bf16[32,2,16,96]{3,2,1,0:T(8,128)(2,1)} %broadcast_in_dim.8), calls=%async_computation | async-start | bytes 524288 | tf_op jit(solution)/shard_map/all_to_all | solution.py:325
  9.4 0.7 %copy-start.4 = (s32[1,1,5,3]{2,1,3,0:T(1,128)S(1)}, s32[1,1,5,3]{2,1,3,0:T(1,128)}, u32[]{:S(2)}) copy-start(s32[1,1,5,3]{2,1,3,0:T(1,128)} %param.10) | copy-start | bytes 184
  9.4 0.7 %copy-start.3 = (f32[48]{0:T(128)S(1)}, f32[48]{0:T(128)}, u32[]{:S(2)}) copy-start(f32[48]{0:T(128)} %head_ref.5) | copy-start | bytes 580
  10.1 9.9 %copy-start.2 = (bf16[96,48]{0,1:T(8,128)(2,1)S(1)}, bf16[96,48]{0,1:T(8,128)(2,1)}, u32[]{:S(2)}) copy-start(bf16[96,48]{0,1:T(8,128)(2,1)} %param.7) | copy-start | bytes 27652
  48.0 1.2 %collective-permute-start = (f32[48,48]{1,0:T(8,128)S(1)}, f32[48,48]{1,0:T(8,128)S(1)}, u32[]{:S(2)}, u32[]{:S(2)}) collective-permute-start(f32[48,48]{1,0:T(8,128)S(1)} %get-tuple-element.15), channel_id=1, source_target_pairs={{0,1},{1,0},{2,3},{3,2},{4,5},{5,4},{6,7},{7,6},{8,9},{9,8},{10,11... | collective-permute-start | bytes 27656 | tf_op jit(solution)/shard_map/ppermute | solution.py:380

commit v4 on v3

--- a/solution.py
+++ b/solution.py
@@ -82,7 +82,8 @@
 def tiles_kernel(
     rows_dev,
     slots,
-    feats_ref,
+    mine_ref,
+    other_ref,
     proj_ref,
     forward_ref,
     backward_ref,
@@ -97,7 +98,8 @@
     m_ref,
     v_ref,
 ):
-    n_src, _, chunk, c1 = feats_ref.shape
+    n_src, chunk, c1 = mine_ref.shape
+    odd = lax.axis_index("col") % 2 == 1
     cols_dev = n_src // rows_dev
     blocks = 2 * rows_dev
     bins = cols_dev * chunk
@@ -107,7 +109,11 @@
 
     def chunks_of(b):
         r, half = (b, 0) if b < rows_dev else (blocks - 1 - b, 1)
-        return [feats_ref[r * cols_dev + c, half] for c in range(cols_dev)]
+        first, second = (mine_ref, other_ref) if half == 0 else (other_ref, mine_ref)
+        return [
+            jnp.where(odd, second[r * cols_dev + c], first[r * cols_dev + c])
+            for c in range(cols_dev)
+        ]
 
     zero_halo = jnp.zeros((HALO, c1), BF16)
     for b in range(blocks):
@@ -322,15 +328,17 @@
     slots = tile_table.shape[2]
     scale = 1.0 / (sequence_length * bins)
 
-    all_feats = lax.all_to_all(
-        jnp.broadcast_to(feats, (devices,) + feats.shape[1:]), ("row", "col"), 0, 0, tiled=True
-    )
+    mine = lax.all_to_all(
+        jnp.broadcast_to(feats, (devices // halves,) + feats.shape[1:]).reshape(devices, part, c1),
+        ("row", "col"),
+        0,
+        0,
+        tiled=True,
+    )
+    cores = [(c, c ^ 1) for c in range(cols_dev)]
+    other = lax.ppermute(mine, "col", cores)
     if part % 16:
-        all_feats = (
-            all_feats.reshape(rows_dev, cols_dev, halves, part, c1)
-            .transpose(0, 2, 1, 3, 4)
-            .reshape(rows_dev, halves, bins, c1)
-        )
+        mine, other = mine.reshape(rows_dev, bins, c1), other.reshape(rows_dev, bins, c1)
     vmem = pl.BlockSpec(memory_space=pltpu.VMEM)
     smem = pl.BlockSpec(memory_space=pltpu.SMEM)
     params = pltpu.CompilerParams(vmem_limit_bytes=48 * 1024 * 1024)
@@ -350,7 +358,7 @@
     partial = pl.pallas_call(
         functools.partial(tiles_kernel, rows_dev, slots),
         out_shape=jax.ShapeDtypeStruct((devices, ch, LANES), BF16),
-        in_specs=[vmem, vmem, vmem, vmem, smem, smem, vmem],
+        in_specs=[vmem, vmem, vmem, vmem, vmem, smem, smem, vmem],
         out_specs=vmem,
         scratch_shapes=[
             pltpu.VMEM((blocks, LANES, c1), BF16),
@@ -362,9 +370,9 @@
         ],
         compiler_params=params,
         name="tiles",
-    )(all_feats, proj_t, forward, backward, head_weight, entries, targets)
+    )(mine, other, proj_t, forward, backward, head_weight, entries, targets)
     got = lax.all_to_all(partial, ("row", "col"), 0, 0, tiled=True)
-    feat_grad, conv_grad, head_grad, mine = pl.pallas_call(
+    feat_grad, conv_grad, head_grad, own_part = pl.pallas_call(
         functools.partial(finish_kernel, scale, 1.0 / math.sqrt(sequence_length)),
         out_shape=(
             jax.ShapeDtypeStruct(feats.shape, F32),
@@ -377,10 +385,10 @@
         compiler_params=params,
         name="finish",
     )(got, proj_t, conv_t, head_weight)
-    other = lax.ppermute(mine, "col", [(c, c ^ 1) for c in range(cols_dev)])
+    other_part = lax.ppermute(own_part, "col", cores)
     odd = lax.axis_index("col") % 2 == 1
     proj_grad = jnp.concatenate(
-        [jnp.where(odd, other, mine), jnp.where(odd, mine, other)], axis=1
+        [jnp.where(odd, other_part, own_part), jnp.where(odd, own_part, other_part)], axis=1
     )
     return feat_grad, proj_grad.T, conv_grad.transpose(1, 0, 2), head_grad.reshape(ch)
 

time: 50.2 us -> 48 us (0.956)
  blocking collectives: 15.4 us -> 30.2 us
  waiting for transfers between devices: 9.71 us -> 1.2 us
  starting transfers between devices: 7.3 us -> 0.22 us
  local copies, waits for them, and re-layouts: 2.11 us -> 0.75 us
    all_to_all x0 -> x1, blocking collectives: none -> 15.3 us  [body(): lax.all_to_all(jnp.broadcast_to(feats, (devices // halves,) + feats.shape...]
    all_to_all x1 -> x0, waiting for transfers between devices: 8.51 us -> none  [body(): lax.all_to_all(jnp.broadcast_to(feats, (devices,) + feats.shape[1:]), ('r...]
    all_to_all x1 -> x0, starting transfers between devices: 7.3 us -> none  [body(): lax.all_to_all(jnp.broadcast_to(feats, (devices,) + feats.shape[1:]), ('r...]
    broadcast_in_dim x1, local copies, waits for them, and re-layouts: 1.44 us -> 0.72 us  [body(): jnp.broadcast_to(feats, (devices // halves,) + feats.shape[1:])]
    unnamed x10, local copies, waits for them, and re-layouts: 0.67 us -> 0.03 us
    all_to_all x1, blocking collectives: 15.4 us -> 14.9 us  [body(): got = lax.all_to_all(partial, ('row', 'col'), 0, 0, tiled=True)]
    ppermute x1 -> x2, waiting for transfers between devices: 1.19 us -> 1.2 us  [the longest x1 1.19 us: body(): other_part = lax.ppermute(own_part, 'col', cores)]
  transfers between devices with their start and end apart: 2 -> 2, of which waited for: 2 -> 1; matrix products, arithmetic and copies ran while one was open for 0% -> 0% of each run, Pallas kernels for 3% -> 3%
where the time goes in v4:
time: 48 us; the launch traced here: 47.8 us
  blocking collectives  30.2 us (63%)
  Pallas kernels  14 us (29%)
  waiting for transfers between devices  1.2 us (2%)
  local copies, waits for them, and re-layouts  0.75 us (2%)
  between operations  0.72 us (2%)
  other arithmetic  0.69 us (1%)
    all_to_all x1, blocking collectives, body(): lax.all_to_all(jnp.broadcast_to(feats, (devices // halves,) + feats.shape...  15.3 us
    all_to_all x1, blocking collectives, body(): got = lax.all_to_all(partial, ('row', 'col'), 0, 0, tiled=True)  14.9 us
    pallas_call x1, Pallas kernels, body(): pl.pallas_call(functools.partial(tiles_kernel, rows_dev, slots), out_shap...  11.2 us
    pallas_call x1, Pallas kernels, body(): pl.pallas_call(functools.partial(finish_kernel, scale, 1.0 / math.sqrt(se...  1.4 us
    pallas_call x1, Pallas kernels, body(): pl.pallas_call(taps_kernel, out_shape=(jax.ShapeDtypeStruct((144, 8 * ch)...  1.39 us
    ppermute x1, waiting for transfers between devices, body(): other_part = lax.ppermute(own_part, 'col', cores)  1.19 us
  transfers between devices with their start and end apart: 2, of which 1 were waited for; matrix products, arithmetic and copies ran while one was open for 0% of the time, Pallas kernels for 3%

profile of v4, /device:TPU:0, one launch (start us, length us, event | category | flops | bytes accessed | tf_op | source)
XLA Modules:
  0.0 47.8 jit_solution(16120537036604729770)
XLA Ops:
  0.6 0.0 copy-start.3
  0.6 0.7 %broadcast_in_dim.8 = bf16[16,2,16,96]{3,2,1,0:T(8,128)(2,1)S(1)} broadcast(bf16[2,16,96]{2,1,0:T(8,128)(2,1)} %bitcast.15), dimensions={1,2,3} | broadcast | bytes 104448 | tf_op jit(solution)/shard_map/broadcast_in_dim | solution.py:332
  1.4 0.0 copy-start.4
  1.4 0.0 copy-start
  1.4 0.0 copy-start.1
  1.4 15.3 %all_to_all.10.mine_ref = bf16[32,16,96]{2,1,0:T(8,128)(2,1)S(1)} all-to-all(bf16[32,16,96]{2,1,0:T(8,128)(2,1)S(1)} %bitcast.14), channel_id=1, replica_groups=mesh['row'=8,'col'=4] {'row','col'}, dimensions={0} | all-to-all | bytes 196608 | tf_op jit(solution)/shard_map/all_to_all | solution.py:331
  16.7 0.2 collective-permute-start
  16.9 0.0 copy-done.3
  17.0 0.0 copy-done.4
  17.0 0.0 copy-done
  17.0 0.0 copy-start.2
  17.0 1.4 %taps.1 = (bf16[144,384]{1,0:T(8,128)(2,1)S(1)}, bf16[384,240]{1,0:T(8,128)(2,1)S(1)}, s32[3,5]{1,0:T(4,128)S(1)}) custom-call(bf16[9,48,48]{2,1,0:T(8,128)(2,1)S(1)} %bitcast.9, f32[48]{0:T(128)S(1)} %copy-done.3, s32[1,3,1,5]{3,2,1,0:T(1,128)S(1)} %bitcast.13), custom_call_target="tpu_custom_call" | custom-call | flops 10000000 | bytes 1000000 | tf_op jit(solution)/shard_map/taps/pallas_call | solution.py:345
  18.4 0.0 collective-permute-done.other_ref
  18.4 0.0 copy-done.1
  18.4 0.0 copy-done.2
  18.4 11.2 %tiles.1 = bf16[32,48,128]{2,1,0:T(8,128)(2,1)S(1)} custom-call(bf16[32,16,96]{2,1,0:T(8,128)(2,1)S(1)} %all_to_all.10.mine_ref, bf16[32,16,96]{2,1,0:T(8,128)(2,1)S(1)} %collective-permute-done.other_ref, bf16[48,96]{1,0:T(8,128)(2,1)S(1)} %bitcast.11, bf16[144,384]{1,0:T(8,128)(2,1)S(1)} %get-tuple-element.11.forward_ref, ...), custom_call_target="tpu_custom_call" | custom-call | tf_op jit(solution)/shard_map/tiles/pallas_call | solution.py:358
  29.6 14.9 %all_to_all.11.got_ref = bf16[32,48,128]{2,1,0:T(8,128)(2,1)S(1)} all-to-all(bf16[32,48,128]{2,1,0:T(8,128)(2,1)S(1)} %tiles.1), channel_id=1, replica_groups=mesh['row'=8,'col'=4] {'row','col'}, dimensions={0} | all-to-all | bytes 786432 | tf_op jit(solution)/shard_map/all_to_all | solution.py:374
  44.5 1.4 %finish.1 = (f32[1,2,16,96]{3,2,1,0:T(8,128)}, f32[9,48,48]{2,1,0:T(8,128)}, f32[1,48]{1,0:T(1,128)}, f32[48,48]{1,0:T(8,128)S(1)}) custom-call(bf16[32,48,128]{2,1,0:T(8,128)(2,1)S(1)} %all_to_all.11.got_ref, bf16[48,96]{1,0:T(8,128)(2,1)S(1)} %bitcast.12, bf16[9,48,48]{2,1,0:T(8,128)(2,1)S(1)} %bitcast.10, f32[48]{0:T(128)S(1)} %copy-done.3), custom_call_target="tpu_custom_call" | custom-call | tf_op jit(solution)/shard_map/finish/pallas_call | solution.py:375
  45.9 0.0 collective-permute-start.1
  45.9 1.2 %collective-permute-done.1 = f32[48,48]{1,0:T(8,128)S(1)} collective-permute-done((f32[48,48]{1,0:T(8,128)S(1)}, f32[48,48]{1,0:T(8,128)S(1)}, u32[]{:S(2)}, u32[]{:S(2)}) %collective-permute-start.1) | collective-permute-done | bytes 9248 | tf_op jit(solution)/shard_map/ppermute | solution.py:388
  47.1 0.7 %maximum_bitcast_fusion = f32[96,48]{0,1:T(8,128)} fusion(f32[48,48]{1,0:T(8,128)S(1)} %get-tuple-element.19, f32[48,48]{1,0:T(8,128)S(1)} %get-tuple-element.18), kind=kLoop, calls=%fused_computation | loop fusion | flops 4608 | bytes 36864 | tf_op jit(solution)/shard_map/transpose | solution.py:393
  (1 shorter events, 0.0 us)
Async XLA Ops:
  0.6 16.3 %copy-start.3 = (f32[48]{0:T(128)S(1)}, f32[48]{0:T(128)}, u32[]{:S(2)}) copy-start(f32[48]{0:T(128)} %head_ref.5) | copy-start | bytes 580
  1.4 15.6 %copy-start.4 = (s32[1,1,5,3]{2,1,3,0:T(1,128)S(1)}, s32[1,1,5,3]{2,1,3,0:T(1,128)}, u32[]{:S(2)}) copy-start(s32[1,1,5,3]{2,1,3,0:T(1,128)} %param.10) | copy-start | bytes 184
  1.4 15.6 %copy-start = (bf16[48,9,48]{2,0,1:T(8,128)(2,1)S(1)}, bf16[48,9,48]{2,0,1:T(8,128)(2,1)}, u32[]{:S(2)}) copy-start(bf16[48,9,48]{2,0,1:T(8,128)(2,1)} %param.8) | copy-start | bytes 124420
  1.4 17.0 %copy-start.1 = (f32[1,1,5,64,64]{4,3,2,1,0:T(8,128)S(1)}, f32[1,1,5,64,64]{4,3,2,1,0:T(8,128)}, u32[]{:S(2)}) copy-start(f32[1,1,5,64,64]{4,3,2,1,0:T(8,128)} %targets_ref.1) | copy-start | bytes 245764
  16.7 1.6 %collective-permute-start = (bf16[32,16,96]{2,1,0:T(8,128)(2,1)S(1)}, bf16[32,16,96]{2,1,0:T(8,128)(2,1)S(1)}, u32[]{:S(2)}, u32[]{:S(2)}) collective-permute-start(bf16[32,16,96]{2,1,0:T(8,128)(2,1)S(1)} %all_to_all.10.mine_ref), channel_id=1, source_target_pairs={{0,1},{1,0},{2,3},{3,2},{4,5},{5,4},{6,7},{7,6},{8,9},{9,8},{10,11... | collective-permute-start | bytes 294920 | tf_op jit(solution)/shard_map/ppermute | solution.py:339
  17.0 1.4 %copy-start.2 = (bf16[96,48]{0,1:T(8,128)(2,1)S(1)}, bf16[96,48]{0,1:T(8,128)(2,1)}, u32[]{:S(2)}) copy-start(bf16[96,48]{0,1:T(8,128)(2,1)} %param.7) | copy-start | bytes 27652
  45.9 1.2 %collective-permute-start.1 = (f32[48,48]{1,0:T(8,128)S(1)}, f32[48,48]{1,0:T(8,128)S(1)}, u32[]{:S(2)}, u32[]{:S(2)}) collective-permute-start(f32[48,48]{1,0:T(8,128)S(1)} %get-tuple-element.15), channel_id=1, source_target_pairs={{0,1},{1,0},{2,3},{3,2},{4,5},{5,4},{6,7},{7,6},{8,9},{9,8},{10,11... | collective-permute-start | bytes 27656 | tf_op jit(solution)/shard_map/ppermute | solution.py:388

commit v5 on v4

--- a/solution.py
+++ b/solution.py
@@ -254,11 +254,24 @@
     )
     sums = sums[:ch] + sums[ch:]
     sums = jnp.where(lane == 2 * ch + 9, jnp.sum(x_acc, axis=1, keepdims=True), sums)
-    sums_hi, sums_lo = split_two(sums)
-    sums = sums_hi + pltpu.roll(sums_lo, 10, 1)
-    shared = [
-        jnp.where(lane < 2 * ch, half, sums) for half in (pltpu.roll(proj_acc, ch, 1), proj_acc)
-    ]
+    shared = []
+    lane32, low16 = lane_iota(32), slice(32, 48)
+    for k in range(2):
+        half = pltpu.roll(proj_acc, ch - ch * k, 1) if k == 0 else proj_acc
+        tail = jnp.concatenate(
+            [pltpu.roll(half[low16], 48, 1), pltpu.roll(half[low16], 24, 1)], axis=0
+        )
+        v_head = pltpu.roll(sums[:32], 24 - 5 * k, 1)
+        v_tail = jnp.concatenate(
+            [pltpu.roll(sums[low16], 29 - 5 * k, 1), pltpu.roll(sums[low16], 26 - 5 * k, 1)], axis=0
+        )
+        shared.append(
+            jnp.where(
+                lane32 < 96,
+                half[:32],
+                jnp.where(lane32 < 120, tail, jnp.where(lane32 < 125, v_head, v_tail)),
+            )
+        )
 
     def block_gradient(b):
         own = jnp.where((lane >= HALO) & (lane < HALO + bins), dwin_ref[b], 0.0)
@@ -283,29 +296,55 @@
                     lane_part < ch, both[half][c * part : (c + 1) * part], base[rows]
                 )
                 out_ref[dest, rows] = piece.astype(BF16)
-            out_ref[dest, 2 * part :] = base[2 * part :].astype(BF16)
-
-
-def finish_kernel(
-    scale, root, got_ref, proj_ref, conv_ref, head_ref, feat_ref, conv_out_ref, head_out_ref, half_ref
-):
-    n_src, ch, _ = got_ref.shape
+            if 2 * part < 32:
+                out_ref[dest, 2 * part :] = base[2 * part :].astype(BF16)
+
+
+def total_kernel(root, got_ref, proj_ref, feat_ref, total_ref):
+    n_src = got_ref.shape[0]
+    ch = proj_ref.shape[0]
     part = feat_ref.shape[2]
-    total = got_ref[0].astype(F32)
-    for d in range(1, n_src):
-        total = total + got_ref[d].astype(F32)
-    half_ref[...] = total[:, ch : 2 * ch] * scale
-    whole_t = jnp.transpose(pad_to(total, LANES, LANES))
-    proj_t = proj_ref[...]
+    totals = [got_ref[d].astype(F32) for d in range(4)]
+    for d in range(4, n_src):
+        totals[d % 4] = totals[d % 4] + got_ref[d].astype(F32)
+    total = (totals[0] + totals[1]) + (totals[2] + totals[3])
+    total_ref[...] = total
     hi, lo = split_two(total[: 2 * part, :ch])
-    feat = jnp.dot(hi.astype(BF16), proj_t, preferred_element_type=F32) + jnp.dot(
-        lo.astype(BF16), proj_t, preferred_element_type=F32
-    )
-    feat = feat * root
+    feat = jnp.dot(
+        jnp.concatenate([hi, lo], axis=0).astype(BF16), proj_ref[...], preferred_element_type=F32
+    )
     for half in range(2):
-        feat_ref[0, half] = feat[half * part : (half + 1) * part]
-
-    sums = whole_t[2 * ch : 2 * ch + 10, :ch] + whole_t[2 * ch + 10 : 2 * ch + 20, :ch]
+        rows = slice(half * part, (half + 1) * part)
+        feat_ref[0, half] = (feat[: 2 * part][rows] + feat[2 * part :][rows]) * root
+
+
+def weights_kernel(scale, mine_ref, other_ref, conv_ref, head_ref, proj_out_ref, conv_out_ref, head_out_ref):
+    ch = conv_ref.shape[1]
+    odd = lax.axis_index("col") % 2 == 1
+    mine, other = mine_ref[...], other_ref[...]
+    lane16, lane32 = lane_iota(16), lane_iota(32)
+
+    heads, tails, v_heads, v_tails = [], [], [], []
+    for k, part in enumerate((jnp.where(odd, other, mine), jnp.where(odd, mine, other))):
+        heads.append(pltpu.roll(part, 80, 1) if k == 0 else part)
+        tails.append([pltpu.roll(part[:16], 32 + 48 * k, 1), pltpu.roll(part[16:], 56 + 48 * k, 1)])
+        v_heads.append(pltpu.roll(part, 8 + 5 * k, 1))
+        v_tails.append([pltpu.roll(part[:16], 3 + 5 * k, 1), pltpu.roll(part[16:], 6 + 5 * k, 1)])
+    head = jnp.where(lane32 < 48, heads[0], heads[1])
+    tail = jnp.where(
+        lane16 < 48,
+        jnp.where(lane16 < 24, tails[0][0], tails[0][1]),
+        jnp.where(lane16 < 72, tails[1][0], tails[1][1]),
+    )
+    proj_out_ref[...] = jnp.concatenate([head, tail], axis=0)[:, : 2 * ch] * scale
+    v_head = jnp.where(lane32 < 5, v_heads[0], v_heads[1])
+    v_tail = jnp.where(
+        lane16 < 5,
+        jnp.where(lane16 < 3, v_tails[0][0], v_tails[0][1]),
+        jnp.where(lane16 < 8, v_tails[1][0], v_tails[1][1]),
+    )
+    sums = jnp.concatenate([v_head, v_tail], axis=0)
+    sums = jnp.transpose(pad_to(sums, LANES, LANES))[:10, :ch]
     head_col = column_of(head_ref, ch)[:, :ch] * scale
     products = jnp.zeros((ch, ch), F32)
     for t in range(9):
@@ -357,7 +396,7 @@
     )(conv_t, head_weight, tile_table.transpose(0, 3, 1, 2))
     partial = pl.pallas_call(
         functools.partial(tiles_kernel, rows_dev, slots),
-        out_shape=jax.ShapeDtypeStruct((devices, ch, LANES), BF16),
+        out_shape=jax.ShapeDtypeStruct((devices, 32, LANES), BF16),
         in_specs=[vmem, vmem, vmem, vmem, vmem, smem, smem, vmem],
         out_specs=vmem,
         scratch_shapes=[
@@ -372,24 +411,30 @@
         name="tiles",
     )(mine, other, proj_t, forward, backward, head_weight, entries, targets)
     got = lax.all_to_all(partial, ("row", "col"), 0, 0, tiled=True)
-    feat_grad, conv_grad, head_grad, own_part = pl.pallas_call(
-        functools.partial(finish_kernel, scale, 1.0 / math.sqrt(sequence_length)),
+    feat_grad, own_total = pl.pallas_call(
+        functools.partial(total_kernel, 1.0 / math.sqrt(sequence_length)),
         out_shape=(
             jax.ShapeDtypeStruct(feats.shape, F32),
+            jax.ShapeDtypeStruct((32, LANES), F32),
+        ),
+        in_specs=[vmem, vmem],
+        out_specs=(vmem, vmem),
+        compiler_params=params,
+        name="total",
+    )(got, proj_t)
+    other_total = lax.ppermute(own_total, "col", cores)
+    proj_grad, conv_grad, head_grad = pl.pallas_call(
+        functools.partial(weights_kernel, scale),
+        out_shape=(
+            jax.ShapeDtypeStruct(proj_t.shape, F32),
             jax.ShapeDtypeStruct(conv_t.shape, F32),
             jax.ShapeDtypeStruct((1, ch), F32),
-            jax.ShapeDtypeStruct((ch, ch), F32),
         ),
         in_specs=[vmem, vmem, vmem, smem],
-        out_specs=(vmem, vmem, vmem, vmem),
+        out_specs=(vmem, vmem, vmem),
         compiler_params=params,
-        name="finish",
-    )(got, proj_t, conv_t, head_weight)
-    other_part = lax.ppermute(own_part, "col", cores)
-    odd = lax.axis_index("col") % 2 == 1
-    proj_grad = jnp.concatenate(
-        [jnp.where(odd, other_part, own_part), jnp.where(odd, own_part, other_part)], axis=1
-    )
+        name="weights",
+    )(own_total, other_total, conv_t, head_weight)
     return feat_grad, proj_grad.T, conv_grad.transpose(1, 0, 2), head_grad.reshape(ch)
 
 

time: 48 us -> 45.6 us (0.950)
  blocking collectives: 30.2 us -> 27.6 us
  Pallas kernels: 14 us -> 14.8 us
  other arithmetic: 0.69 us -> 0 us
    all_to_all x1, blocking collectives: 14.9 us -> 12.3 us  [body(): got = lax.all_to_all(partial, ('row', 'col'), 0, 0, tiled=True)]
    pallas_call x1 -> x2, Pallas kernels: 1.4 us -> 2.21 us  [the longest x1 1.45 us: body(): pl.pallas_call(functools.partial(weights_kernel, scale), out_shape=(jax.S...]
    transpose x1 -> x0, other arithmetic: 0.69 us -> none  [body(): return (feat_grad, proj_grad.T, conv_grad.transpose(1, 0, 2), head_grad.r...]
where the time goes in v5:
time: 45.6 us; the launch traced here: 45.3 us
  blocking collectives  27.6 us (61%)
  Pallas kernels  14.8 us (32%)
  waiting for transfers between devices  1.18 us (3%)
  local copies, waits for them, and re-layouts  0.75 us (2%)
  between operations  0.71 us (2%)
    all_to_all x1, blocking collectives, body(): lax.all_to_all(jnp.broadcast_to(feats, (devices // halves,) + feats.shape...  15.3 us
    all_to_all x1, blocking collectives, body(): got = lax.all_to_all(partial, ('row', 'col'), 0, 0, tiled=True)  12.3 us
    pallas_call x1, Pallas kernels, body(): pl.pallas_call(functools.partial(tiles_kernel, rows_dev, slots), out_shap...  11.2 us
    pallas_call x1, Pallas kernels, body(): pl.pallas_call(functools.partial(weights_kernel, scale), out_shape=(jax.S...  1.45 us
    pallas_call x1, Pallas kernels, body(): pl.pallas_call(taps_kernel, out_shape=(jax.ShapeDtypeStruct((144, 8 * ch)...  1.39 us
    ppermute x1, waiting for transfers between devices, body(): other_total = lax.ppermute(own_total, 'col', cores)  1.18 us
  transfers between devices with their start and end apart: 2, of which 1 were waited for; matrix products, arithmetic and copies ran while one was open for 0% of the time, Pallas kernels for 3%

profile of v5, /device:TPU:0, one launch (start us, length us, event | category | flops | bytes accessed | tf_op | source)
XLA Modules:
  0.0 45.3 jit_solution(4281053498559988154)
XLA Ops:
  0.6 0.0 copy-start.3
  0.6 0.7 %broadcast_in_dim.8 = bf16[16,2,16,96]{3,2,1,0:T(8,128)(2,1)S(1)} broadcast(bf16[2,16,96]{2,1,0:T(8,128)(2,1)} %bitcast.14), dimensions={1,2,3} | broadcast | bytes 104448 | tf_op jit(solution)/shard_map/broadcast_in_dim | solution.py:371
  1.4 0.0 copy-start.4
  1.4 0.0 copy-start
  1.4 0.0 copy-start.1
  1.4 15.3 %all_to_all.10.mine_ref = bf16[32,16,96]{2,1,0:T(8,128)(2,1)S(1)} all-to-all(bf16[32,16,96]{2,1,0:T(8,128)(2,1)S(1)} %bitcast.13), channel_id=1, replica_groups=mesh['row'=8,'col'=4] {'row','col'}, dimensions={0} | all-to-all | bytes 196608 | tf_op jit(solution)/shard_map/all_to_all | solution.py:370
  16.7 0.2 collective-permute-start
  16.9 0.0 copy-done.3
  17.0 0.0 copy-done.4
  17.0 0.0 copy-done
  17.0 0.0 copy-start.2
  17.0 1.4 %taps.1 = (bf16[144,384]{1,0:T(8,128)(2,1)S(1)}, bf16[384,240]{1,0:T(8,128)(2,1)S(1)}, s32[3,5]{1,0:T(4,128)S(1)}) custom-call(bf16[9,48,48]{2,1,0:T(8,128)(2,1)S(1)} %bitcast.8, f32[48]{0:T(128)S(1)} %copy-done.3, s32[1,3,1,5]{3,2,1,0:T(1,128)S(1)} %bitcast.12), custom_call_target="tpu_custom_call" | custom-call | flops 10000000 | bytes 1000000 | tf_op jit(solution)/shard_map/taps/pallas_call | solution.py:384
  18.4 0.0 collective-permute-done.other_ref
  18.4 0.0 copy-done.1
  18.4 0.0 copy-done.2
  18.4 11.2 %tiles.1 = bf16[32,32,128]{2,1,0:T(8,128)(2,1)S(1)} custom-call(bf16[32,16,96]{2,1,0:T(8,128)(2,1)S(1)} %all_to_all.10.mine_ref, bf16[32,16,96]{2,1,0:T(8,128)(2,1)S(1)} %collective-permute-done.other_ref, bf16[48,96]{1,0:T(8,128)(2,1)S(1)} %bitcast.10, bf16[144,384]{1,0:T(8,128)(2,1)S(1)} %get-tuple-element.12.forward_ref, ...), custom_call_target="tpu_custom_call" | custom-call | tf_op jit(solution)/shard_map/tiles/pallas_call | solution.py:397
  29.6 12.3 %all_to_all.11.got_ref = bf16[32,32,128]{2,1,0:T(8,128)(2,1)S(1)} all-to-all(bf16[32,32,128]{2,1,0:T(8,128)(2,1)S(1)} %tiles.1), channel_id=1, replica_groups=mesh['row'=8,'col'=4] {'row','col'}, dimensions={0} | all-to-all | bytes 524288 | tf_op jit(solution)/shard_map/all_to_all | solution.py:413
  41.9 0.8 %total.1 = (f32[1,2,16,96]{3,2,1,0:T(8,128)}, f32[32,128]{1,0:T(8,128)S(1)}) custom-call(bf16[32,32,128]{2,1,0:T(8,128)(2,1)S(1)} %all_to_all.11.got_ref, bf16[48,96]{1,0:T(8,128)(2,1)S(1)} %bitcast.11), custom_call_target="tpu_custom_call" | custom-call | tf_op jit(solution)/shard_map/total/pallas_call | solution.py:414
  42.7 0.0 collective-permute-start.1
  42.7 1.2 %collective-permute-done.1.other_ref = f32[32,128]{1,0:T(8,128)S(1)} collective-permute-done((f32[32,128]{1,0:T(8,128)S(1)}, f32[32,128]{1,0:T(8,128)S(1)}, u32[]{:S(2)}, u32[]{:S(2)}) %collective-permute-start.1) | collective-permute-done | bytes 16416 | tf_op jit(solution)/shard_map/ppermute | solution.py:425
  43.9 1.4 %weights.1 = (f32[48,96]{1,0:T(8,128)}, f32[9,48,48]{2,1,0:T(8,128)}, f32[1,48]{1,0:T(1,128)}) custom-call(f32[32,128]{1,0:T(8,128)S(1)} %get-tuple-element.16.mine_ref, f32[32,128]{1,0:T(8,128)S(1)} %collective-permute-done.1.other_ref, bf16[9,48,48]{2,1,0:T(8,128)(2,1)S(1)} %bitcast.9, f32[48]{0:T(128)S(1)} %copy-done.3), custom_call_target="tpu_custom_call" | custom-call | tf_op jit(solution)/shard_map/weights/pallas_call | solution.py:426
Async XLA Ops:
  0.6 16.3 %copy-start.3 = (f32[48]{0:T(128)S(1)}, f32[48]{0:T(128)}, u32[]{:S(2)}) copy-start(f32[48]{0:T(128)} %head_ref.5) | copy-start | bytes 580
  1.4 15.6 %copy-start.4 = (s32[1,1,5,3]{2,1,3,0:T(1,128)S(1)}, s32[1,1,5,3]{2,1,3,0:T(1,128)}, u32[]{:S(2)}) copy-start(s32[1,1,5,3]{2,1,3,0:T(1,128)} %param.10) | copy-start | bytes 184
  1.4 15.6 %copy-start = (bf16[48,9,48]{2,0,1:T(8,128)(2,1)S(1)}, bf16[48,9,48]{2,0,1:T(8,128)(2,1)}, u32[]{:S(2)}) copy-start(bf16[48,9,48]{2,0,1:T(8,128)(2,1)} %param.8) | copy-start | bytes 124420
  1.4 17.0 %copy-start.1 = (f32[1,1,5,64,64]{4,3,2,1,0:T(8,128)S(1)}, f32[1,1,5,64,64]{4,3,2,1,0:T(8,128)}, u32[]{:S(2)}) copy-start(f32[1,1,5,64,64]{4,3,2,1,0:T(8,128)} %targets_ref.1) | copy-start | bytes 245764
  16.7 1.6 %collective-permute-start = (bf16[32,16,96]{2,1,0:T(8,128)(2,1)S(1)}, bf16[32,16,96]{2,1,0:T(8,128)(2,1)S(1)}, u32[]{:S(2)}, u32[]{:S(2)}) collective-permute-start(bf16[32,16,96]{2,1,0:T(8,128)(2,1)S(1)} %all_to_all.10.mine_ref), channel_id=1, source_target_pairs={{0,1},{1,0},{2,3},{3,2},{4,5},{5,4},{6,7},{7,6},{8,9},{9,8},{10,11... | collective-permute-start | bytes 294920 | tf_op jit(solution)/shard_map/ppermute | solution.py:378
  17.0 1.4 %copy-start.2 = (bf16[96,48]{0,1:T(8,128)(2,1)S(1)}, bf16[96,48]{0,1:T(8,128)(2,1)}, u32[]{:S(2)}) copy-start(bf16[96,48]{0,1:T(8,128)(2,1)} %param.7) | copy-start | bytes 27652
  42.7 1.2 %collective-permute-start.1 = (f32[32,128]{1,0:T(8,128)S(1)}, f32[32,128]{1,0:T(8,128)S(1)}, u32[]{:S(2)}, u32[]{:S(2)}) collective-permute-start(f32[32,128]{1,0:T(8,128)S(1)} %get-tuple-element.16.mine_ref), channel_id=1, source_target_pairs={{0,1},{1,0},{2,3},{3,2},{4,5},{5,4},{6,7},{7,6},{8,9},{9,8},{10,11... | collective-permute-start | bytes 49160 | tf_op jit(solution)/shard_map/ppermute | solution.py:425

commit v6 on v4

--- a/solution.py
+++ b/solution.py
@@ -45,7 +45,7 @@
     return jnp.concatenate(groups, axis=0)
 
 
-def taps_kernel(conv_ref, head_ref, table_ref, forward_ref, backward_ref, entries_ref):
+def taps_kernel(conv_ref, head_ref, table_ref, forward_ref, backward_ref, column_ref, entries_ref):
     ch = conv_ref.shape[1]
     for s in range(table_ref.shape[3]):
         for k in range(3):
@@ -70,13 +70,13 @@
     for dy in range(3):
         hi, lo = hi_tiles[3 * dy : 3 * dy + 3], lo_tiles[3 * dy : 3 * dy + 3]
         forward_rows += hi + lo
-        backward_rows += hi + hi + lo + [jnp.zeros(wide, F32)]
+        backward_rows += hi + lo
     forward_taps = jnp.concatenate(forward_rows, axis=0).astype(BF16)
-    backward_taps = jnp.transpose(
-        jnp.concatenate(backward_rows + [jnp.zeros((16, 8 * ch), F32)], axis=0)
-    )[:, :240].astype(BF16)
+    pad = [jnp.zeros((112, 8 * ch), F32)]
+    backward_taps = jnp.transpose(jnp.concatenate(backward_rows + pad, axis=0))[:, :144].astype(BF16)
     forward_ref[...] = forward_taps
     backward_ref[...] = backward_taps
+    column_ref[...] = head_col
 
 
 def tiles_kernel(
@@ -87,10 +87,11 @@
     proj_ref,
     forward_ref,
     backward_ref,
-    head_ref,
+    column_ref,
     table_ref,
     targets_ref,
-    out_ref,
+    keep_ref,
+    give_ref,
     fwin_ref,
     gwin_ref,
     dwin_ref,
@@ -131,10 +132,10 @@
         gwin_ref[b] = g.astype(BF16)
         dwin_ref[b] = jnp.zeros((ch, LANES), F32)
 
-    head_col = column_of(head_ref, ch)
+    head_col = column_ref[...]
     groups = bins // 8
-    m_ref[:, : 2 * LANES] = jnp.zeros((80, 2 * LANES), BF16)
-    m_ref[:, (groups + 2) * LANES :] = jnp.zeros((80, 2 * LANES), BF16)
+    m_ref[:, : 2 * LANES] = jnp.zeros((48, 2 * LANES), BF16)
+    m_ref[:, (groups + 2) * LANES :] = jnp.zeros((48, 2 * LANES), BF16)
     v_ref[...] = jnp.zeros(v_ref.shape, F32)
     inner = (lane1 >= HALO) & (lane1 < HALO + bins)
 
@@ -177,25 +178,22 @@
             )
             at = HALO + c * 8
             m = jnp.where(inner, (conv + pred_c + pred_r[at : at + 8] - goal) * weight, 0.0)
-            his, los = [], []
-            for moved in (pltpu.roll(m, LANES - DIL, 1), m, pltpu.roll(m, DIL, 1)):
-                hi, lo = split_two(moved)
-                his.append(hi)
-                los.append(lo)
+            moved = [pltpu.roll(m, LANES - DIL, 1), m, pltpu.roll(m, DIL, 1)]
             m_ref[:, (c + 2) * LANES : (c + 3) * LANES] = jnp.concatenate(
-                his + los + his + [jnp.zeros((8, LANES), F32)], axis=0
+                moved + moved, axis=0
             ).astype(BF16)
             return m
 
         def gradients(g, d_rows, d_cols):
-            cols = slice(g * LANES, (g + 1) * LANES)
+            cols = slice(g * LANES, (g + 2) * LANES)
             m3 = jnp.concatenate(
-                [m_ref[:, (g + 2 - dy) * LANES : (g + 3 - dy) * LANES] for dy in range(3)], axis=0
+                [m_ref[:, (g + 2 - dy) * LANES : (g + 4 - dy) * LANES] for dy in range(3)], axis=0
             )
             up = jnp.dot(backward_ref[...], m3, preferred_element_type=F32)
             grad = jnp.where(u_ref[:, cols].astype(F32) > 0.0, up, 0.0)
-            for k in range(8):
-                part = grad[k * ch : (k + 1) * ch]
+            for k in range(16):
+                at = slice(k // 8 * LANES, (k // 8 + 1) * LANES)
+                part = grad[k % 8 * ch : (k % 8 + 1) * ch, at]
                 d_cols = d_cols + part
                 d_rows = jnp.where(
                     lane == HALO - DIL + g * 8 + k, jnp.sum(part, axis=1, keepdims=True), d_rows
@@ -210,17 +208,17 @@
                 m = misfit(g - 2, z)
                 m_cols = m_cols + m
                 row_sums.append(jnp.broadcast_to(jnp.sum(m, axis=1, keepdims=True), (8, LANES)))
-        for g in range(groups + 2):
+        for g in range(0, groups + 2, 2):
             d_rows, d_cols = gradients(g, d_rows, d_cols)
         row_sums.append(jnp.zeros((LANES - HALO - bins, LANES), F32))
         m_rows = jnp.transpose(jnp.concatenate(row_sums, axis=0))[:1]
         m_cols = jnp.sum(m_cols, axis=0, keepdims=True)
         frame_cols = (groups + 2) * LANES
         m3 = jnp.concatenate(
-            [m_ref[:, (2 - dy) * LANES : (2 - dy) * LANES + frame_cols] for dy in range(3)], axis=0
+            [m_ref[:32, (2 - dy) * LANES : (2 - dy) * LANES + frame_cols] for dy in range(3)], axis=0
         )
         v_ref[...] += lax.dot_general(
-            u_ref[...], m3, (((1,), (1,)), ((), ())), preferred_element_type=F32
+            m3, u_ref[...], (((1,), (1,)), ((), ())), preferred_element_type=F32
         )
         d_rows = 0.5 * (d_rows + head_col * m_rows)
         d_cols = 0.5 * (d_cols + head_col * m_cols)
@@ -239,74 +237,130 @@
         proj_acc = proj_acc + jnp.dot(both, fwin_ref[b], preferred_element_type=F32)
     proj_acc = pad_to(proj_acc[:ch] + proj_acc[ch:], ch, LANES)
 
-    wide = lax.broadcasted_iota(jnp.int32, (ch, 240), 1)
-    v_sum = jnp.zeros((ch, 240), F32)
-    for k in range(8):
-        v_sum = v_sum + jnp.where(wide % 8 == k, v_ref[k * ch : (k + 1) * ch], 0.0)
-    hi, lo = split_two(v_sum)
-    source = lax.broadcasted_iota(jnp.int32, (240, LANES), 0)
-    place = 2 * ch + 3 * (source // 80) + source % 80 % 24 // 8
-    select = (source % 80 < 48) & (lax.broadcasted_iota(jnp.int32, (240, LANES), 1) == place)
-    sums = jnp.dot(
-        jnp.concatenate([hi, lo], axis=0).astype(BF16),
-        select.astype(F32).astype(BF16),
-        preferred_element_type=F32,
-    )
-    sums = sums[:ch] + sums[ch:]
+    wide = (96, 8 * ch)
+    own_row = lax.broadcasted_iota(jnp.int32, wide, 0) % 8 == (
+        lax.broadcasted_iota(jnp.int32, wide, 1) // ch
+    )
+    hi, lo = split_two(jnp.where(own_row, v_ref[...], 0.0))
+    source = lax.broadcasted_iota(jnp.int32, (16, 96), 1)
+    place = 3 * (source // 32) + source % 32 // 8
+    select = (source % 32 < 24) & (lax.broadcasted_iota(jnp.int32, (16, 96), 0) == place)
+    select = select.astype(F32).astype(BF16)
+    v_rows = jnp.dot(select, hi.astype(BF16), preferred_element_type=F32) + jnp.dot(
+        select, lo.astype(BF16), preferred_element_type=F32
+    )
+    v_sum = v_rows[:, :ch]
+    for k in range(1, 8):
+        v_sum = v_sum + v_rows[:, k * ch : (k + 1) * ch]
+    sums = pltpu.roll(jnp.transpose(pad_to(v_sum, LANES, LANES))[:ch], 2 * ch, 1)
     sums = jnp.where(lane == 2 * ch + 9, jnp.sum(x_acc, axis=1, keepdims=True), sums)
-    sums_hi, sums_lo = split_two(sums)
-    sums = sums_hi + pltpu.roll(sums_lo, 10, 1)
-    shared = [
-        jnp.where(lane < 2 * ch, half, sums) for half in (pltpu.roll(proj_acc, ch, 1), proj_acc)
-    ]
-
     def block_gradient(b):
-        own = jnp.where((lane >= HALO) & (lane < HALO + bins), dwin_ref[b], 0.0)
+        own = dwin_ref[b]
+        at_start, at_end = lane < HALO + DIL, lane >= HALO + bins - DIL
         if b > 0:
-            before = pltpu.roll(dwin_ref[b - 1], LANES - bins, 1)
-            own = own + jnp.where((lane >= HALO) & (lane < HALO + DIL), before, 0.0)
+            own = own + jnp.where(at_start, pltpu.roll(dwin_ref[b - 1], LANES - bins, 1), 0.0)
         if b < blocks - 1:
-            after = pltpu.roll(dwin_ref[b + 1], bins, 1)
-            own = own + jnp.where((lane >= HALO + bins - DIL) & (lane < HALO + bins), after, 0.0)
-        return jnp.transpose(pad_to(own, LANES, LANES))[HALO : HALO + bins]
-
-    part = bins // (out_ref.shape[0] // rows_dev)
+            own = own + jnp.where(at_end, pltpu.roll(dwin_ref[b + 1], bins, 1), 0.0)
+        return own
+
+    for j in range(rows_dev // 2):
+        packs = []
+        for half in range(2):
+            b0, b1 = [r if half == 0 else blocks - 1 - r for r in (2 * j, 2 * j + 1)]
+            first = pltpu.roll(block_gradient(b0), LANES - HALO, 1)
+            second = pltpu.roll(block_gradient(b1), bins - HALO, 1)
+            packs.append(jnp.where(lane < bins, first, second))
+        keep_ref[j] = jnp.where(odd, packs[1], packs[0])
+        give_ref[j] = jnp.where(odd, packs[0], packs[1])
+    weights = jnp.where(lane < 2 * ch, proj_acc, sums)
+    keep_ref[rows_dev // 2] = weights
+    give_ref[rows_dev // 2] = weights
+
+
+def pair_kernel(keep_ref, took_ref, out_ref):
+    pairs, ch = keep_ref.shape[0] - 1, keep_ref.shape[1]
+    odd = lax.axis_index("col") % 2 == 1
+    bins = LANES // 2
+    cols_dev = out_ref.shape[0] // (2 * pairs)
+    part = bins // cols_dev
+    weights = keep_ref[pairs] + took_ref[pairs]
+    chunks = [weights[16 * q : 16 * q + 16] for q in range(3)]
+    lane16 = lane_iota(16)
+
+    def share(dest, k):
+        first = 48 * dest + 24 * k
+        moved = [pltpu.roll(chunks[q], (48 + 24 * q - first) % LANES, 1) for q in range(3)]
+        v_own = pltpu.roll(chunks[2 * k], 24 - 5 * dest, 1)
+        v_middle = pltpu.roll(chunks[1], 29 - 5 * dest - 3 * k, 1)
+        out = jnp.where(lane16 < 125, v_own, v_middle)
+        for q in (2, 1, 0):
+            out = jnp.where(lane16 < 72 + 24 * q, moved[q], out)
+        return out
+
+    shares = [jnp.where(odd, share(dest, 1), share(dest, 0)) for dest in range(2)]
     lane_part = lane_iota(part)
-    for r in range(rows_dev):
-        both = (block_gradient(r), block_gradient(blocks - 1 - r))
-        for c in range(bins // part):
-            dest = r * (bins // part) + c
-            base = shared[c % 2]
-            for half in range(2):
-                rows = slice(half * part, (half + 1) * part)
-                piece = jnp.where(
-                    lane_part < ch, both[half][c * part : (c + 1) * part], base[rows]
-                )
-                out_ref[dest, rows] = piece.astype(BF16)
-            out_ref[dest, 2 * part :] = base[2 * part :].astype(BF16)
-
-
-def finish_kernel(
-    scale, root, got_ref, proj_ref, conv_ref, head_ref, feat_ref, conv_out_ref, head_out_ref, half_ref
-):
-    n_src, ch, _ = got_ref.shape
+    for j in range(pairs):
+        both = jnp.transpose(pad_to(keep_ref[j] + took_ref[j], LANES, LANES))
+        for i in range(2 * cols_dev):
+            dest = 2 * j * cols_dev + i
+            base = shares[i % 2]
+            rows = both[i * part : (i + 1) * part]
+            out_ref[dest, :part] = jnp.where(lane_part < ch, rows, base[:part]).astype(BF16)
+            if part < 16:
+                out_ref[dest, part:] = base[part:].astype(BF16)
+
+
+def total_kernel(got_ref, total_ref):
+    totals = [got_ref[d].astype(F32) for d in range(4)]
+    for d in range(4, got_ref.shape[0]):
+        totals[d % 4] = totals[d % 4] + got_ref[d].astype(F32)
+    total_ref[:16] = totals[0] + totals[2]
+    total_ref[16:] = totals[1] + totals[3]
+
+
+def features_kernel(root, total_ref, proj_ref, feat_ref):
+    ch = proj_ref.shape[0]
     part = feat_ref.shape[2]
-    total = got_ref[0].astype(F32)
-    for d in range(1, n_src):
-        total = total + got_ref[d].astype(F32)
-    half_ref[...] = total[:, ch : 2 * ch] * scale
-    whole_t = jnp.transpose(pad_to(total, LANES, LANES))
-    proj_t = proj_ref[...]
-    hi, lo = split_two(total[: 2 * part, :ch])
-    feat = jnp.dot(hi.astype(BF16), proj_t, preferred_element_type=F32) + jnp.dot(
-        lo.astype(BF16), proj_t, preferred_element_type=F32
-    )
-    feat = feat * root
+    rows = [total_ref[16 * half : 16 * half + part, :ch] for half in range(2)]
+    hi, lo = split_two(jnp.concatenate(rows, axis=0))
+    feat = jnp.dot(
+        jnp.concatenate([hi, lo], axis=0).astype(BF16), proj_ref[...], preferred_element_type=F32
+    )
     for half in range(2):
-        feat_ref[0, half] = feat[half * part : (half + 1) * part]
-
-    sums = whole_t[2 * ch : 2 * ch + 10, :ch] + whole_t[2 * ch + 10 : 2 * ch + 20, :ch]
-    head_col = column_of(head_ref, ch)[:, :ch] * scale
+        at = half * part
+        feat_ref[0, half] = (feat[at : at + part] + feat[2 * part + at : 3 * part + at]) * root
+
+
+def weights_kernel(scale, mine_ref, other_ref, conv_ref, column_ref, proj_out_ref, conv_out_ref, head_out_ref):
+    ch = conv_ref.shape[1]
+    odd = lax.axis_index("col") % 2 == 1
+    mine, other = mine_ref[...], other_ref[...]
+    lane16 = lane_iota(16)
+    parts = (jnp.where(odd, other, mine), jnp.where(odd, mine, other))
+
+    def sent(dest, k, shift):
+        return pltpu.roll(parts[dest][16 * k : 16 * k + 16], shift % LANES, 1)
+
+    proj_rows = []
+    for q in range(3):
+        rows = sent(1, 1, 72 - 48 - 24 * q)
+        for n in (2, 1, 0):
+            rows = jnp.where(lane16 < 24 * n + 24, sent(n // 2, n % 2, 24 * n - 48 - 24 * q), rows)
+        proj_rows.append(rows)
+    proj_out_ref[...] = jnp.concatenate(proj_rows, axis=0)[:, : 2 * ch] * scale
+    v_rows = []
+    for q in range(3):
+        by_dest = []
+        for dest in range(2):
+            if q == 1:
+                first, second = sent(dest, 0, 5 * dest - 125), sent(dest, 1, 5 * dest + 3 - 125)
+                by_dest.append(jnp.where(lane16 < 5 * dest + 3, first, second))
+            else:
+                by_dest.append(sent(dest, q // 2, 5 * dest - 120))
+        v_rows.append(jnp.where(lane16 < 5, by_dest[0], by_dest[1]))
+    sums = jnp.concatenate(v_rows, axis=0)
+    sums = jnp.transpose(pad_to(sums, LANES, LANES))[:10, :ch]
+    head_col = column_ref[:, :ch] * scale
     products = jnp.zeros((ch, ch), F32)
     for t in range(9):
         v = sums[t : t + 1]
@@ -342,54 +396,76 @@
     vmem = pl.BlockSpec(memory_space=pltpu.VMEM)
     smem = pl.BlockSpec(memory_space=pltpu.SMEM)
     params = pltpu.CompilerParams(vmem_limit_bytes=48 * 1024 * 1024)
-    forward, backward, entries = pl.pallas_call(
+    forward, backward, head_column, entries = pl.pallas_call(
         taps_kernel,
         out_shape=(
             jax.ShapeDtypeStruct((144, 8 * ch), BF16),
-            jax.ShapeDtypeStruct((8 * ch, 240), BF16),
+            jax.ShapeDtypeStruct((8 * ch, 144), BF16),
+            jax.ShapeDtypeStruct((ch, LANES), F32),
             jax.ShapeDtypeStruct((3, slots), jnp.int32),
         ),
         in_specs=[vmem, smem, smem],
-        out_specs=(vmem, vmem, smem),
+        out_specs=(vmem, vmem, vmem, smem),
         compiler_params=params,
         cost_estimate=pl.CostEstimate(flops=10**7, bytes_accessed=10**6, transcendentals=0),
         name="taps",
     )(conv_t, head_weight, tile_table.transpose(0, 3, 1, 2))
-    partial = pl.pallas_call(
+    keep, give = pl.pallas_call(
         functools.partial(tiles_kernel, rows_dev, slots),
-        out_shape=jax.ShapeDtypeStruct((devices, ch, LANES), BF16),
-        in_specs=[vmem, vmem, vmem, vmem, vmem, smem, smem, vmem],
-        out_specs=vmem,
+        out_shape=(jax.ShapeDtypeStruct((rows_dev // 2 + 1, ch, LANES), F32),) * 2,
+        in_specs=[vmem, vmem, vmem, vmem, vmem, vmem, smem, vmem],
+        out_specs=(vmem, vmem),
         scratch_shapes=[
             pltpu.VMEM((blocks, LANES, c1), BF16),
             pltpu.VMEM((blocks, ch, LANES), BF16),
             pltpu.VMEM((blocks, ch, LANES), F32),
             pltpu.VMEM((8 * ch, (bins // 8 + 2) * LANES), BF16),
-            pltpu.VMEM((80, (bins // 8 + 4) * LANES), BF16),
-            pltpu.VMEM((8 * ch, 240), F32),
+            pltpu.VMEM((48, (bins // 8 + 4) * LANES), BF16),
+            pltpu.VMEM((96, 8 * ch), F32),
         ],
         compiler_params=params,
         name="tiles",
-    )(mine, other, proj_t, forward, backward, head_weight, entries, targets)
+    )(mine, other, proj_t, forward, backward, head_column, entries, targets)
+    took = lax.ppermute(give, "col", cores)
+    partial = pl.pallas_call(
+        pair_kernel,
+        out_shape=jax.ShapeDtypeStruct((devices, 16, LANES), BF16),
+        in_specs=[vmem, vmem],
+        out_specs=vmem,
+        compiler_params=params,
+        name="pair",
+    )(keep, took)
     got = lax.all_to_all(partial, ("row", "col"), 0, 0, tiled=True)
-    feat_grad, conv_grad, head_grad, own_part = pl.pallas_call(
-        functools.partial(finish_kernel, scale, 1.0 / math.sqrt(sequence_length)),
+    own_total = pl.pallas_call(
+        total_kernel,
+        out_shape=jax.ShapeDtypeStruct((32, LANES), F32),
+        in_specs=[vmem],
+        out_specs=vmem,
+        compiler_params=params,
+        name="total",
+    )(got)
+    other_total = lax.ppermute(own_total, "col", cores)
+    feat_grad = pl.pallas_call(
+        functools.partial(features_kernel, 1.0 / math.sqrt(sequence_length)),
+        out_shape=jax.ShapeDtypeStruct(feats.shape, F32),
+        in_specs=[vmem, vmem],
+        out_specs=vmem,
+        compiler_params=params,
+        cost_estimate=pl.CostEstimate(flops=10**7, bytes_accessed=10**6, transcendentals=0),
+        name="features",
+    )(own_total, proj_t)
+    proj_grad, conv_grad, head_grad = pl.pallas_call(
+        functools.partial(weights_kernel, scale),
         out_shape=(
-            jax.ShapeDtypeStruct(feats.shape, F32),
+            jax.ShapeDtypeStruct(proj_t.shape, F32),
             jax.ShapeDtypeStruct(conv_t.shape, F32),
             jax.ShapeDtypeStruct((1, ch), F32),
-            jax.ShapeDtypeStruct((ch, ch), F32),
         ),
-        in_specs=[vmem, vmem, vmem, smem],
-        out_specs=(vmem, vmem, vmem, vmem),
-        compiler_params=params,
-        name="finish",
-    )(got, proj_t, conv_t, head_weight)
-    other_part = lax.ppermute(own_part, "col", cores)
-    odd = lax.axis_index("col") % 2 == 1
-    proj_grad = jnp.concatenate(
-        [jnp.where(odd, other_part, own_part), jnp.where(odd, own_part, other_part)], axis=1
-    )
+        in_specs=[vmem, vmem, vmem, vmem],
+        out_specs=(vmem, vmem, vmem),
+        compiler_params=params,
+        name="weights",
+    )(own_total, other_total, conv_t, head_column)
     return feat_grad, proj_grad.T, conv_grad.transpose(1, 0, 2), head_grad.reshape(ch)
 
 

time: 48 us -> 43.2 us (0.900)
  blocking collectives: 30.2 us -> 25.3 us
  other arithmetic: 0.69 us -> 0 us
  starting transfers between devices: 0.22 us -> 0.85 us
    all_to_all x1, blocking collectives: 14.9 us -> 9.95 us  [body(): got = lax.all_to_all(partial, ('row', 'col'), 0, 0, tiled=True)]
    transpose x1 -> x0, other arithmetic: 0.69 us -> none  [body(): return (feat_grad, proj_grad.T, conv_grad.transpose(1, 0, 2), head_grad.r...]
    ppermute x1 -> x2, starting transfers between devices: 0.01 us -> 0.64 us  [the longest x1 0.36 us: body(): took = lax.ppermute(give, 'col', cores)]
    pallas_call x1 -> x4, Pallas kernels: 1.4 us -> 1.79 us  [the longest x1 0.9 us: body(): pl.pallas_call(functools.partial(weights_kernel, scale), out_shape=(jax.S...]
    ppermute x1 -> x2, waiting for transfers between devices: 1.19 us -> 1.28 us  [the longest x1 1.04 us: body(): took = lax.ppermute(give, 'col', cores)]
  transfers between devices with their start and end apart: 2 -> 3, of which waited for: 1 -> 2; matrix products, arithmetic and copies ran while one was open for 0% -> 0% of each run, Pallas kernels for 3% -> 5%
where the time goes in v6:
time: 43.2 us; the launch traced here: 43 us
  blocking collectives  25.3 us (59%)
  Pallas kernels  14.1 us (33%)
  waiting for transfers between devices  1.29 us (3%)
  starting transfers between devices  0.85 us (2%)
  local copies, waits for them, and re-layouts  0.75 us (2%)
  between operations  0.73 us (2%)
    all_to_all x1, blocking collectives, body(): lax.all_to_all(jnp.broadcast_to(feats, (devices // halves,) + feats.shape...  15.3 us
    pallas_call x1, Pallas kernels, body(): pl.pallas_call(functools.partial(tiles_kernel, rows_dev, slots), out_shap...  10.9 us
    all_to_all x1, blocking collectives, body(): got = lax.all_to_all(partial, ('row', 'col'), 0, 0, tiled=True)  9.95 us
    pallas_call x1, Pallas kernels, body(): pl.pallas_call(taps_kernel, out_shape=(jax.ShapeDtypeStruct((144, 8 * ch)...  1.39 us
    ppermute x1, waiting for transfers between devices, body(): took = lax.ppermute(give, 'col', cores)  1.04 us
    pallas_call x1, Pallas kernels, body(): pl.pallas_call(functools.partial(weights_kernel, scale), out_shape=(jax.S...  0.9 us
  transfers between devices with their start and end apart: 3, of which 2 were waited for; matrix products, arithmetic and copies ran while one was open for 0% of the time, Pallas kernels for 5%

profile of v6, /device:TPU:0, one launch (start us, length us, event | category | flops | bytes accessed | tf_op | source)
XLA Modules:
  0.0 43.0 jit_solution(6103591724911961095)
XLA Ops:
  0.6 0.0 copy-start.4
  0.6 0.7 %broadcast_in_dim.8 = bf16[16,2,16,96]{3,2,1,0:T(8,128)(2,1)S(1)} broadcast(bf16[2,16,96]{2,1,0:T(8,128)(2,1)} %bitcast.14), dimensions={1,2,3} | broadcast | bytes 104448 | tf_op jit(solution)/shard_map/broadcast_in_dim | solution.py:386
  1.4 0.0 copy-start.3
  1.4 0.0 copy-start
  1.4 0.0 copy-start.1
  1.4 15.3 %all_to_all.10.mine_ref = bf16[32,16,96]{2,1,0:T(8,128)(2,1)S(1)} all-to-all(bf16[32,16,96]{2,1,0:T(8,128)(2,1)S(1)} %bitcast.13), channel_id=1, replica_groups=mesh['row'=8,'col'=4] {'row','col'}, dimensions={0} | all-to-all | bytes 196608 | tf_op jit(solution)/shard_map/all_to_all | solution.py:385
  16.7 0.2 collective-permute-start
  16.9 0.0 copy-done.4
  17.0 0.0 copy-done.3
  17.0 0.0 copy-done
  17.0 0.0 copy-start.2
  17.0 1.4 %taps.1 = (bf16[144,384]{1,0:T(8,128)(2,1)S(1)}, bf16[384,144]{1,0:T(8,128)(2,1)S(1)}, f32[48,128]{1,0:T(8,128)S(1)}, s32[3,5]{1,0:T(4,128)S(1)}) custom-call(bf16[9,48,48]{2,1,0:T(8,128)(2,1)S(1)} %bitcast.8, f32[48]{0:T(128)S(1)} %copy-done.4, s32[1,3,1,5]{3,2,1,0:T(1,128)S(1)} %bitcast.12), custom_call_target="tpu_custom_call" | custom-call | flops 10000000 | bytes 1000000 | tf_op jit(solution)/shard_map/taps/pallas_call | solution.py:399
  18.4 0.0 collective-permute-done.other_ref
  18.4 0.0 copy-done.1
  18.4 0.0 copy-done.2
  18.4 10.9 %tiles.1 = (f32[5,48,128]{2,1,0:T(8,128)S(1)}, f32[5,48,128]{2,1,0:T(8,128)S(1)}) custom-call(bf16[32,16,96]{2,1,0:T(8,128)(2,1)S(1)} %all_to_all.10.mine_ref, bf16[32,16,96]{2,1,0:T(8,128)(2,1)S(1)} %collective-permute-done.other_ref, bf16[48,96]{1,0:T(8,128)(2,1)S(1)} %bitcast.10, bf16[144,384]{1,0:T(8,128)(2,1)S(1)} %get-tuple-element.13.forward_ref, ...), custom_call_target="tpu_custom_call" | custom-call | tf_op jit(solution)/shard_map/tiles/pallas_call | solution.py:413
  29.3 0.4 collective-permute-start.1
  29.7 1.0 %collective-permute-done.1.took_ref = f32[5,48,128]{2,1,0:T(8,128)S(1)} collective-permute-done((f32[5,48,128]{2,1,0:T(8,128)S(1)}, f32[5,48,128]{2,1,0:T(8,128)S(1)}, u32[]{:S(2)}, u32[]{:S(2)}) %collective-permute-start.1) | collective-permute-done | bytes 122912 | tf_op jit(solution)/shard_map/ppermute | solution.py:429
  30.7 0.1 pair.1
  30.9 9.9 %all_to_all.11.got_ref = bf16[32,16,128]{2,1,0:T(8,128)(2,1)S(1)} all-to-all(bf16[32,16,128]{2,1,0:T(8,128)(2,1)S(1)} %pair.1), channel_id=1, replica_groups=mesh['row'=8,'col'=4] {'row','col'}, dimensions={0} | all-to-all | bytes 262144 | tf_op jit(solution)/shard_map/all_to_all | solution.py:438
  40.8 0.3 collective-permute-start.2
  41.1 0.7 %features.1 = f32[1,2,16,96]{3,2,1,0:T(8,128)} custom-call(f32[32,128]{1,0:T(8,128)S(1)} %total.1.total_ref.mine_ref, bf16[48,96]{1,0:T(8,128)(2,1)S(1)} %bitcast.11), custom_call_target="tpu_custom_call" | custom-call | flops 10000000 | bytes 1000000 | tf_op jit(solution)/shard_map/features/pallas_call | solution.py:448
  41.9 0.2 collective-permute-done.2.other_ref
  42.1 0.9 %weights.1 = (f32[48,96]{1,0:T(8,128)}, f32[9,48,48]{2,1,0:T(8,128)}, f32[1,48]{1,0:T(1,128)}) custom-call(f32[32,128]{1,0:T(8,128)S(1)} %total.1.total_ref.mine_ref, f32[32,128]{1,0:T(8,128)S(1)} %collective-permute-done.2.other_ref, bf16[9,48,48]{2,1,0:T(8,128)(2,1)S(1)} %bitcast.9, f32[48,128]{1,0:T(8,128)S(1)} %get-tuple-element.15.column_ref), custom_call_target="tpu_custom_call" | custom-call | tf_op jit(solution)/shard_map/weights/pallas_call | solution.py:457
  (1 shorter events, 0.0 us)
Async XLA Ops:
  0.6 16.3 %copy-start.4 = (f32[48]{0:T(128)S(1)}, f32[48]{0:T(128)}, u32[]{:S(2)}) copy-start(f32[48]{0:T(128)} %head_ref.1) | copy-start | bytes 580
  1.4 15.6 %copy-start.3 = (s32[1,1,5,3]{2,1,3,0:T(1,128)S(1)}, s32[1,1,5,3]{2,1,3,0:T(1,128)}, u32[]{:S(2)}) copy-start(s32[1,1,5,3]{2,1,3,0:T(1,128)} %param.10) | copy-start | bytes 184
  1.4 15.6 %copy-start = (bf16[48,9,48]{2,0,1:T(8,128)(2,1)S(1)}, bf16[48,9,48]{2,0,1:T(8,128)(2,1)}, u32[]{:S(2)}) copy-start(bf16[48,9,48]{2,0,1:T(8,128)(2,1)} %param.8) | copy-start | bytes 124420
  1.4 17.0 %copy-start.1 = (f32[1,1,5,64,64]{4,3,2,1,0:T(8,128)S(1)}, f32[1,1,5,64,64]{4,3,2,1,0:T(8,128)}, u32[]{:S(2)}) copy-start(f32[1,1,5,64,64]{4,3,2,1,0:T(8,128)} %targets_ref.1) | copy-start | bytes 245764
  16.7 1.6 %collective-permute-start = (bf16[32,16,96]{2,1,0:T(8,128)(2,1)S(1)}, bf16[32,16,96]{2,1,0:T(8,128)(2,1)S(1)}, u32[]{:S(2)}, u32[]{:S(2)}) collective-permute-start(bf16[32,16,96]{2,1,0:T(8,128)(2,1)S(1)} %all_to_all.10.mine_ref), channel_id=1, source_target_pairs={{0,1},{1,0},{2,3},{3,2},{4,5},{5,4},{6,7},{7,6},{8,9},{9,8},{10,11... | collective-permute-start | bytes 294920 | tf_op jit(solution)/shard_map/ppermute | solution.py:393
  17.0 1.4 %copy-start.2 = (bf16[96,48]{0,1:T(8,128)(2,1)S(1)}, bf16[96,48]{0,1:T(8,128)(2,1)}, u32[]{:S(2)}) copy-start(bf16[96,48]{0,1:T(8,128)(2,1)} %param.7) | copy-start | bytes 27652
  29.3 1.4 %collective-permute-start.1 = (f32[5,48,128]{2,1,0:T(8,128)S(1)}, f32[5,48,128]{2,1,0:T(8,128)S(1)}, u32[]{:S(2)}, u32[]{:S(2)}) collective-permute-start(f32[5,48,128]{2,1,0:T(8,128)S(1)} %get-tuple-element.18), channel_id=1, source_target_pairs={{0,1},{1,0},{2,3},{3,2},{4,5},{5,4},{6,7},{7,6},{8,9},{9,8},{10,11... | collective-permute-start | bytes 368648 | tf_op jit(solution)/shard_map/ppermute | solution.py:429
  40.8 1.2 %collective-permute-start.2 = (f32[32,128]{1,0:T(8,128)S(1)}, f32[32,128]{1,0:T(8,128)S(1)}, u32[]{:S(2)}, u32[]{:S(2)}) collective-permute-start(f32[32,128]{1,0:T(8,128)S(1)} %total.1.total_ref.mine_ref), channel_id=1, source_target_pairs={{0,1},{1,0},{2,3},{3,2},{4,5},{5,4},{6,7},{7,6},{8,9},{9,8},{10,11... | collective-permute-start | bytes 49160 | tf_op jit(solution)/shard_map/ppermute | solution.py:447

commit v7 on v6

--- a/solution.py
+++ b/solution.py
@@ -34,23 +34,10 @@
     return x
 
 
-def column_of(scalars_ref, count):
-    sub = lax.broadcasted_iota(jnp.int32, (8, LANES), 0)
-    groups = []
-    for g in range(count // 8):
-        acc = jnp.zeros((8, LANES), F32)
-        for k in range(8):
-            acc = jnp.where(sub == k, scalars_ref[g * 8 + k], acc)
-        groups.append(acc)
-    return jnp.concatenate(groups, axis=0)
-
-
 def taps_kernel(conv_ref, head_ref, table_ref, forward_ref, backward_ref, column_ref, entries_ref):
     ch = conv_ref.shape[1]
-    for s in range(table_ref.shape[3]):
-        for k in range(3):
-            entries_ref[k, s] = table_ref[0, k, 0, s]
-    head_col = column_of(head_ref, ch)
+    entries_ref[...] = pad_to(table_ref[0, :, 0, :], 8, LANES)
+    head_col = jnp.transpose(jnp.broadcast_to(pad_to(head_ref[...], 1, LANES), (LANES, LANES)))[:ch]
     taps = [
         jnp.sum(head_col[:, :ch] * conv_ref[t].astype(F32), axis=0, keepdims=True)
         for t in range(9)
@@ -88,7 +75,7 @@
     forward_ref,
     backward_ref,
     column_ref,
-    table_ref,
+    entries_ref,
     targets_ref,
     keep_ref,
     give_ref,
@@ -98,7 +85,11 @@
     u_ref,
     m_ref,
     v_ref,
+    table_ref,
+    table_sem,
 ):
+    table_copy = pltpu.make_async_copy(entries_ref, table_ref, table_sem)
+    table_copy.start()
     n_src, chunk, c1 = mine_ref.shape
     odd = lax.axis_index("col") % 2 == 1
     cols_dev = n_src // rows_dev
@@ -154,11 +145,6 @@
                 u_ref[k * ch : (k + 1) * ch, g * LANES : (g + 1) * LANES] = jnp.maximum(
                     x, 0.0
                 ).astype(BF16)
-            return jnp.dot(
-                forward_ref[...],
-                u_ref[:, g * LANES : (g + 1) * LANES],
-                preferred_element_type=F32,
-            )
 
         def misfit(c, z):
             terms = []
@@ -202,24 +188,42 @@
 
         z, m_cols, row_sums = [], jnp.zeros((8, LANES), F32), [jnp.zeros((HALO, LANES), F32)]
         d_rows = d_cols = jnp.zeros((ch, LANES), F32)
-        for g in range(groups + 2):
-            z.append(activations(g))
-            if g >= 2:
-                m = misfit(g - 2, z)
-                m_cols = m_cols + m
-                row_sums.append(jnp.broadcast_to(jnp.sum(m, axis=1, keepdims=True), (8, LANES)))
+        def next_misfit(c, m_cols):
+            m = misfit(c, z)
+            row_sums.append(jnp.broadcast_to(jnp.sum(m, axis=1, keepdims=True), (8, LANES)))
+            return m_cols + m
+
+        def tap_sums(g):
+            m3 = jnp.concatenate(
+                [m_ref[:32, (g + 2 - dy) * LANES : (g + 4 - dy) * LANES] for dy in range(3)], axis=0
+            )
+            v_ref[...] += lax.dot_general(
+                m3,
+                u_ref[:, g * LANES : (g + 2) * LANES],
+                (((1,), (1,)), ((), ())),
+                preferred_element_type=F32,
+            )
+
+        for g in range(0, groups + 2, 2):
+            activations(g)
+            activations(g + 1)
+            pair = jnp.dot(
+                forward_ref[...],
+                u_ref[:, g * LANES : (g + 2) * LANES],
+                preferred_element_type=F32,
+            )
+            z += [pair[:, :LANES], pair[:, LANES:]]
+        for c in range(groups // 2):
+            m_cols = next_misfit(c, m_cols)
         for g in range(0, groups + 2, 2):
             d_rows, d_cols = gradients(g, d_rows, d_cols)
+            tap_sums(g)
+            for c in (groups // 2 + g, groups // 2 + g + 1):
+                if c < groups:
+                    m_cols = next_misfit(c, m_cols)
         row_sums.append(jnp.zeros((LANES - HALO - bins, LANES), F32))
         m_rows = jnp.transpose(jnp.concatenate(row_sums, axis=0))[:1]
         m_cols = jnp.sum(m_cols, axis=0, keepdims=True)
-        frame_cols = (groups + 2) * LANES
-        m3 = jnp.concatenate(
-            [m_ref[:32, (2 - dy) * LANES : (2 - dy) * LANES + frame_cols] for dy in range(3)], axis=0
-        )
-        v_ref[...] += lax.dot_general(
-            m3, u_ref[...], (((1,), (1,)), ((), ())), preferred_element_type=F32
-        )
         d_rows = 0.5 * (d_rows + head_col * m_rows)
         d_cols = 0.5 * (d_cols + head_col * m_cols)
         dwin_ref[a] = dwin_ref[a] + d_rows
@@ -228,6 +232,7 @@
             m_cols != 0.0, gc * m_cols, 0.0
         )
 
+    table_copy.wait()
     x_acc = lax.fori_loop(0, slots, slot, jnp.zeros((ch, LANES), F32))
 
     proj_acc = jnp.zeros((2 * ch, c1), F32)
@@ -394,7 +399,6 @@
     if part % 16:
         mine, other = mine.reshape(rows_dev, bins, c1), other.reshape(rows_dev, bins, c1)
     vmem = pl.BlockSpec(memory_space=pltpu.VMEM)
-    smem = pl.BlockSpec(memory_space=pltpu.SMEM)
     params = pltpu.CompilerParams(vmem_limit_bytes=48 * 1024 * 1024)
     forward, backward, head_column, entries = pl.pallas_call(
         taps_kernel,
@@ -402,18 +406,18 @@
             jax.ShapeDtypeStruct((144, 8 * ch), BF16),
             jax.ShapeDtypeStruct((8 * ch, 144), BF16),
             jax.ShapeDtypeStruct((ch, LANES), F32),
-            jax.ShapeDtypeStruct((3, slots), jnp.int32),
+            jax.ShapeDtypeStruct((8, LANES), jnp.int32),
         ),
-        in_specs=[vmem, smem, smem],
-        out_specs=(vmem, vmem, vmem, smem),
+        in_specs=[vmem, vmem, vmem],
+        out_specs=(vmem, vmem, vmem, vmem),
         compiler_params=params,
         cost_estimate=pl.CostEstimate(flops=10**7, bytes_accessed=10**6, transcendentals=0),
         name="taps",
-    )(conv_t, head_weight, tile_table.transpose(0, 3, 1, 2))
+    )(conv_t, head_weight.reshape(1, ch), tile_table.transpose(0, 3, 1, 2))
     keep, give = pl.pallas_call(
         functools.partial(tiles_kernel, rows_dev, slots),
         out_shape=(jax.ShapeDtypeStruct((rows_dev // 2 + 1, ch, LANES), F32),) * 2,
-        in_specs=[vmem, vmem, vmem, vmem, vmem, vmem, smem, vmem],
+        in_specs=[vmem] * 8,
         out_specs=(vmem, vmem),
         scratch_shapes=[
             pltpu.VMEM((blocks, LANES, c1), BF16),
@@ -422,6 +426,8 @@
             pltpu.VMEM((8 * ch, (bins // 8 + 2) * LANES), BF16),
             pltpu.VMEM((48, (bins // 8 + 4) * LANES), BF16),
             pltpu.VMEM((96, 8 * ch), F32),
+            pltpu.SMEM((8, LANES), jnp.int32),
+            pltpu.SemaphoreType.DMA,
         ],
         compiler_params=params,
         name="tiles",

time: 43.2 us -> 41.6 us (0.963)
  Pallas kernels: 14.1 us -> 11.8 us
  waiting for transfers between devices: 1.29 us -> 2.01 us
    pallas_call x1, Pallas kernels: 10.9 us -> 9.53 us  [body(): pl.pallas_call(functools.partial(tiles_kernel, rows_dev, slots), out_shap...]
    pallas_call x1, Pallas kernels: 1.39 us -> 0.46 us  [body(): pl.pallas_call(taps_kernel, out_shape=(jax.ShapeDtypeStruct((144, 8 * ch)...]
    ppermute x1, waiting for transfers between devices: 0.01 us -> 0.65 us  [body(): other = lax.ppermute(mine, 'col', cores)]
  transfers between devices with their start and end apart: 3 -> 3, of which waited for: 2 -> 3; matrix products, arithmetic and copies ran while one was open for 0% -> 0% of each run, Pallas kernels for 5% -> 3%
where the time goes in v7:
time: 41.6 us; the launch traced here: 41.4 us
  blocking collectives  25.3 us (61%)
  Pallas kernels  11.8 us (28%)
  waiting for transfers between devices  2.01 us (5%)
  starting transfers between devices  0.78 us (2%)
  local copies, waits for them, and re-layouts  0.75 us (2%)
  between operations  0.7 us (2%)
    all_to_all x1, blocking collectives, body(): lax.all_to_all(jnp.broadcast_to(feats, (devices // halves,) + feats.shape...  15.3 us
    all_to_all x1, blocking collectives, body(): got = lax.all_to_all(partial, ('row', 'col'), 0, 0, tiled=True)  10 us
    pallas_call x1, Pallas kernels, body(): pl.pallas_call(functools.partial(tiles_kernel, rows_dev, slots), out_shap...  9.53 us
    ppermute x1, waiting for transfers between devices, body(): took = lax.ppermute(give, 'col', cores)  1.12 us
    pallas_call x1, Pallas kernels, body(): pl.pallas_call(functools.partial(weights_kernel, scale), out_shape=(jax.S...  0.9 us
  transfers between devices with their start and end apart: 3, of which 3 were waited for; matrix products, arithmetic and copies ran while one was open for 0% of the time, Pallas kernels for 3%

profile of v7, /device:TPU:0, one launch (start us, length us, event | category | flops | bytes accessed | tf_op | source)
XLA Modules:
  0.0 41.4 jit_solution(2026532256696036340)
XLA Ops:
  0.6 0.0 copy-start.3
  0.6 0.0 copy-start.4
  0.7 0.7 %broadcast_in_dim.8 = bf16[16,2,16,96]{3,2,1,0:T(8,128)(2,1)S(1)} broadcast(bf16[2,16,96]{2,1,0:T(8,128)(2,1)} %bitcast.16), dimensions={1,2,3} | broadcast | bytes 104448 | tf_op jit(solution)/shard_map/broadcast_in_dim | solution.py:391
  1.4 0.0 copy-start
  1.4 0.0 copy-start.1
  1.4 15.3 %all_to_all.10.mine_ref = bf16[32,16,96]{2,1,0:T(8,128)(2,1)S(1)} all-to-all(bf16[32,16,96]{2,1,0:T(8,128)(2,1)S(1)} %bitcast.15), channel_id=1, replica_groups=mesh['row'=8,'col'=4] {'row','col'}, dimensions={0} | all-to-all | bytes 196608 | tf_op jit(solution)/shard_map/all_to_all | solution.py:390
  16.7 0.2 collective-permute-start
  17.0 0.0 copy-done.3
  17.0 0.0 copy-done.4
  17.0 0.0 copy-done
  17.0 0.0 copy-start.2
  17.0 0.5 %taps.1 = (bf16[144,384]{1,0:T(8,128)(2,1)S(1)}, bf16[384,144]{1,0:T(8,128)(2,1)S(1)}, f32[48,128]{1,0:T(8,128)S(1)}, s32[8,128]{1,0:T(8,128)S(1)}) custom-call(bf16[9,48,48]{2,1,0:T(8,128)(2,1)S(1)} %bitcast.9, f32[1,48]{1,0:T(1,128)S(1)} %bitcast.14, s32[1,3,1,5]{3,2,1,0:T(1,128)S(1)} %bitcast.13), custom_call_target="tpu_custom_call" | custom-call | flops 10000000 | bytes 1000000 | tf_op jit(solution)/shard_map/taps/pallas_call | solution.py:403
  17.4 0.7 %collective-permute-done.other_ref = bf16[32,16,96]{2,1,0:T(8,128)(2,1)S(1)} collective-permute-done((bf16[32,16,96]{2,1,0:T(8,128)(2,1)S(1)}, bf16[32,16,96]{2,1,0:T(8,128)(2,1)S(1)}, u32[]{:S(2)}, u32[]{:S(2)}) %collective-permute-start) | collective-permute-done | bytes 98336 | tf_op jit(solution)/shard_map/ppermute | solution.py:398
  18.1 0.0 copy-done.1
  18.1 0.0 copy-done.2
  18.1 9.5 %tiles.1 = (f32[5,48,128]{2,1,0:T(8,128)S(1)}, f32[5,48,128]{2,1,0:T(8,128)S(1)}) custom-call(bf16[32,16,96]{2,1,0:T(8,128)(2,1)S(1)} %all_to_all.10.mine_ref, bf16[32,16,96]{2,1,0:T(8,128)(2,1)S(1)} %collective-permute-done.other_ref, bf16[48,96]{1,0:T(8,128)(2,1)S(1)} %bitcast.11, bf16[144,384]{1,0:T(8,128)(2,1)S(1)} %get-tuple-element.13.forward_ref, ...), custom_call_target="tpu_custom_call" | custom-call | tf_op jit(solution)/shard_map/tiles/pallas_call | solution.py:417
  27.6 0.3 collective-permute-start.1
  27.9 1.1 %collective-permute-done.1.took_ref = f32[5,48,128]{2,1,0:T(8,128)S(1)} collective-permute-done((f32[5,48,128]{2,1,0:T(8,128)S(1)}, f32[5,48,128]{2,1,0:T(8,128)S(1)}, u32[]{:S(2)}, u32[]{:S(2)}) %collective-permute-start.1) | collective-permute-done | bytes 122912 | tf_op jit(solution)/shard_map/ppermute | solution.py:435
  29.0 0.1 pair.1
  29.2 10.0 %all_to_all.11.got_ref = bf16[32,16,128]{2,1,0:T(8,128)(2,1)S(1)} all-to-all(bf16[32,16,128]{2,1,0:T(8,128)(2,1)S(1)} %pair.1), channel_id=1, replica_groups=mesh['row'=8,'col'=4] {'row','col'}, dimensions={0} | all-to-all | bytes 262144 | tf_op jit(solution)/shard_map/all_to_all | solution.py:444
  39.2 0.3 collective-permute-start.2
  39.5 0.7 %features.1 = f32[1,2,16,96]{3,2,1,0:T(8,128)} custom-call(f32[32,128]{1,0:T(8,128)S(1)} %total.1.total_ref.mine_ref, bf16[48,96]{1,0:T(8,128)(2,1)S(1)} %bitcast.12), custom_call_target="tpu_custom_call" | custom-call | flops 10000000 | bytes 1000000 | tf_op jit(solution)/shard_map/features/pallas_call | solution.py:454
  40.2 0.2 collective-permute-done.2.other_ref
  40.5 0.9 %weights.1 = (f32[48,96]{1,0:T(8,128)}, f32[9,48,48]{2,1,0:T(8,128)}, f32[1,48]{1,0:T(1,128)}) custom-call(f32[32,128]{1,0:T(8,128)S(1)} %total.1.total_ref.mine_ref, f32[32,128]{1,0:T(8,128)S(1)} %collective-permute-done.2.other_ref, bf16[9,48,48]{2,1,0:T(8,128)(2,1)S(1)} %bitcast.10, f32[48,128]{1,0:T(8,128)S(1)} %get-tuple-element.15.column_ref), custom_call_target="tpu_custom_call" | custom-call | tf_op jit(solution)/shard_map/weights/pallas_call | solution.py:463
  (1 shorter events, 0.0 us)
Async XLA Ops:
  0.6 16.3 %copy-start.3 = (s32[1,1,5,3]{2,1,3,0:T(1,128)S(1)}, s32[1,1,5,3]{2,1,3,0:T(1,128)}, u32[]{:S(2)}) copy-start(s32[1,1,5,3]{2,1,3,0:T(1,128)} %param.10) | copy-start | bytes 184
  0.6 16.3 %copy-start.4 = (f32[48]{0:T(128)S(1)}, f32[48]{0:T(128)}, u32[]{:S(2)}) copy-start(f32[48]{0:T(128)} %param.9) | copy-start | bytes 580
  1.4 15.6 %copy-start = (bf16[48,9,48]{2,0,1:T(8,128)(2,1)S(1)}, bf16[48,9,48]{2,0,1:T(8,128)(2,1)}, u32[]{:S(2)}) copy-start(bf16[48,9,48]{2,0,1:T(8,128)(2,1)} %param.8) | copy-start | bytes 124420
  1.4 16.7 %copy-start.1 = (f32[1,1,5,64,64]{4,3,2,1,0:T(8,128)S(1)}, f32[1,1,5,64,64]{4,3,2,1,0:T(8,128)}, u32[]{:S(2)}) copy-start(f32[1,1,5,64,64]{4,3,2,1,0:T(8,128)} %targets_ref.1) | copy-start | bytes 245764
  16.7 1.3 %collective-permute-start = (bf16[32,16,96]{2,1,0:T(8,128)(2,1)S(1)}, bf16[32,16,96]{2,1,0:T(8,128)(2,1)S(1)}, u32[]{:S(2)}, u32[]{:S(2)}) collective-permute-start(bf16[32,16,96]{2,1,0:T(8,128)(2,1)S(1)} %all_to_all.10.mine_ref), channel_id=1, source_target_pairs={{0,1},{1,0},{2,3},{3,2},{4,5},{5,4},{6,7},{7,6},{8,9},{9,8},{10,11... | collective-permute-start | bytes 294920 | tf_op jit(solution)/shard_map/ppermute | solution.py:398
  17.0 1.1 %copy-start.2 = (bf16[96,48]{0,1:T(8,128)(2,1)S(1)}, bf16[96,48]{0,1:T(8,128)(2,1)}, u32[]{:S(2)}) copy-start(bf16[96,48]{0,1:T(8,128)(2,1)} %param.7) | copy-start | bytes 27652
  27.6 1.4 %collective-permute-start.1 = (f32[5,48,128]{2,1,0:T(8,128)S(1)}, f32[5,48,128]{2,1,0:T(8,128)S(1)}, u32[]{:S(2)}, u32[]{:S(2)}) collective-permute-start(f32[5,48,128]{2,1,0:T(8,128)S(1)} %get-tuple-element.18), channel_id=1, source_target_pairs={{0,1},{1,0},{2,3},{3,2},{4,5},{5,4},{6,7},{7,6},{8,9},{9,8},{10,11... | collective-permute-start | bytes 368648 | tf_op jit(solution)/shard_map/ppermute | solution.py:435
  39.2 1.2 %collective-permute-start.2 = (f32[32,128]{1,0:T(8,128)S(1)}, f32[32,128]{1,0:T(8,128)S(1)}, u32[]{:S(2)}, u32[]{:S(2)}) collective-permute-start(f32[32,128]{1,0:T(8,128)S(1)} %total.1.total_ref.mine_ref), channel_id=1, source_target_pairs={{0,1},{1,0},{2,3},{3,2},{4,5},{5,4},{6,7},{7,6},{8,9},{9,8},{10,11... | collective-permute-start | bytes 49160 | tf_op jit(solution)/shard_map/ppermute | solution.py:453

commit v8 on v7

--- a/solution.py
+++ b/solution.py
@@ -259,36 +259,22 @@
         v_sum = v_sum + v_rows[:, k * ch : (k + 1) * ch]
     sums = pltpu.roll(jnp.transpose(pad_to(v_sum, LANES, LANES))[:ch], 2 * ch, 1)
     sums = jnp.where(lane == 2 * ch + 9, jnp.sum(x_acc, axis=1, keepdims=True), sums)
-    def block_gradient(b):
-        own = dwin_ref[b]
-        at_start, at_end = lane < HALO + DIL, lane >= HALO + bins - DIL
-        if b > 0:
-            own = own + jnp.where(at_start, pltpu.roll(dwin_ref[b - 1], LANES - bins, 1), 0.0)
-        if b < blocks - 1:
-            own = own + jnp.where(at_end, pltpu.roll(dwin_ref[b + 1], bins, 1), 0.0)
-        return own
-
-    for j in range(rows_dev // 2):
-        packs = []
-        for half in range(2):
-            b0, b1 = [r if half == 0 else blocks - 1 - r for r in (2 * j, 2 * j + 1)]
-            first = pltpu.roll(block_gradient(b0), LANES - HALO, 1)
-            second = pltpu.roll(block_gradient(b1), bins - HALO, 1)
-            packs.append(jnp.where(lane < bins, first, second))
-        keep_ref[j] = jnp.where(odd, packs[1], packs[0])
-        give_ref[j] = jnp.where(odd, packs[0], packs[1])
+    for r in range(rows_dev + 1):
+        lower, upper = r, blocks - 1 - r
+        keep_ref[r] = dwin_ref[jnp.where(odd, upper, lower)]
+        give_ref[r] = dwin_ref[jnp.where(odd, lower, upper)]
     weights = jnp.where(lane < 2 * ch, proj_acc, sums)
-    keep_ref[rows_dev // 2] = weights
-    give_ref[rows_dev // 2] = weights
+    keep_ref[rows_dev + 1] = weights
+    give_ref[rows_dev + 1] = weights
 
 
 def pair_kernel(keep_ref, took_ref, out_ref):
-    pairs, ch = keep_ref.shape[0] - 1, keep_ref.shape[1]
+    bands, ch = keep_ref.shape[0] - 2, keep_ref.shape[1]
     odd = lax.axis_index("col") % 2 == 1
     bins = LANES // 2
-    cols_dev = out_ref.shape[0] // (2 * pairs)
+    cols_dev = out_ref.shape[0] // bands
     part = bins // cols_dev
-    weights = keep_ref[pairs] + took_ref[pairs]
+    weights = keep_ref[bands + 1] + took_ref[bands + 1]
     chunks = [weights[16 * q : 16 * q + 16] for q in range(3)]
     lane16 = lane_iota(16)
 
@@ -304,12 +290,28 @@
 
     shares = [jnp.where(odd, share(dest, 1), share(dest, 0)) for dest in range(2)]
     lane_part = lane_iota(part)
-    for j in range(pairs):
-        both = jnp.transpose(pad_to(keep_ref[j] + took_ref[j], LANES, LANES))
-        for i in range(2 * cols_dev):
-            dest = 2 * j * cols_dev + i
-            base = shares[i % 2]
-            rows = both[i * part : (i + 1) * part]
+    windows = [
+        jnp.transpose(pad_to(keep_ref[r] + took_ref[r], LANES, LANES)) for r in range(bands + 1)
+    ]
+    first, end = HALO, HALO + bins
+    for r in range(bands):
+        after = windows[r + 1]
+        before = windows[r - 1] if r > 0 else jnp.zeros((LANES, LANES), F32)
+        at_start = jnp.where(odd, after[end : end + DIL], before[end : end + DIL])
+        at_end = jnp.where(odd, before[first - DIL : first], after[first - DIL : first])
+        own = windows[r]
+        block = jnp.concatenate(
+            [
+                own[first : first + DIL] + at_start,
+                own[first + DIL : end - DIL],
+                own[end - DIL : end] + at_end,
+            ],
+            axis=0,
+        )
+        for c in range(cols_dev):
+            dest = r * cols_dev + c
+            base = shares[c % 2]
+            rows = block[c * part : (c + 1) * part]
             out_ref[dest, :part] = jnp.where(lane_part < ch, rows, base[:part]).astype(BF16)
             if part < 16:
                 out_ref[dest, part:] = base[part:].astype(BF16)
@@ -416,7 +418,7 @@
     )(conv_t, head_weight.reshape(1, ch), tile_table.transpose(0, 3, 1, 2))
     keep, give = pl.pallas_call(
         functools.partial(tiles_kernel, rows_dev, slots),
-        out_shape=(jax.ShapeDtypeStruct((rows_dev // 2 + 1, ch, LANES), F32),) * 2,
+        out_shape=(jax.ShapeDtypeStruct((rows_dev + 2, ch, LANES), F32),) * 2,
         in_specs=[vmem] * 8,
         out_specs=(vmem, vmem),
         scratch_shapes=[

time: 41.6 us -> 41.2 us (level)
  Pallas kernels: 11.8 us -> 11.2 us
    pallas_call x1, Pallas kernels: 9.53 us -> 8.86 us  [body(): pl.pallas_call(functools.partial(tiles_kernel, rows_dev, slots), out_shap...]
where the time goes in v8:
time: 41.2 us; the launch traced here: 40.9 us
  blocking collectives  25.3 us (61%)
  Pallas kernels  11.2 us (27%)
  waiting for transfers between devices  2.19 us (5%)
  starting transfers between devices  0.78 us (2%)
  local copies, waits for them, and re-layouts  0.75 us (2%)
  between operations  0.7 us (2%)
    all_to_all x1, blocking collectives, body(): lax.all_to_all(jnp.broadcast_to(feats, (devices // halves,) + feats.shape...  15.3 us
    all_to_all x1, blocking collectives, body(): got = lax.all_to_all(partial, ('row', 'col'), 0, 0, tiled=True)  10 us
    pallas_call x1, Pallas kernels, body(): pl.pallas_call(functools.partial(tiles_kernel, rows_dev, slots), out_shap...  8.86 us
    ppermute x1, waiting for transfers between devices, body(): took = lax.ppermute(give, 'col', cores)  1.3 us
    pallas_call x1, Pallas kernels, body(): pl.pallas_call(functools.partial(weights_kernel, scale), out_shape=(jax.S...  0.9 us
  transfers between devices with their start and end apart: 3, of which 3 were waited for; matrix products, arithmetic and copies ran while one was open for 0% of the time, Pallas kernels for 3%

profile of v8, /device:TPU:0, one launch (start us, length us, event | category | flops | bytes accessed | tf_op | source)
XLA Modules:
  0.0 40.9 jit_solution(14460860510567404393)
XLA Ops:
  0.6 0.0 copy-start.3
  0.6 0.0 copy-start.4
  0.7 0.7 %broadcast_in_dim.8 = bf16[16,2,16,96]{3,2,1,0:T(8,128)(2,1)S(1)} broadcast(bf16[2,16,96]{2,1,0:T(8,128)(2,1)} %bitcast.16), dimensions={1,2,3} | broadcast | bytes 104448 | tf_op jit(solution)/shard_map/broadcast_in_dim | solution.py:393
  1.4 0.0 copy-start
  1.4 0.0 copy-start.1
  1.4 15.3 %all_to_all.10.mine_ref = bf16[32,16,96]{2,1,0:T(8,128)(2,1)S(1)} all-to-all(bf16[32,16,96]{2,1,0:T(8,128)(2,1)S(1)} %bitcast.15), channel_id=1, replica_groups=mesh['row'=8,'col'=4] {'row','col'}, dimensions={0} | all-to-all | bytes 196608 | tf_op jit(solution)/shard_map/all_to_all | solution.py:392
  16.7 0.2 collective-permute-start
  17.0 0.0 copy-done.3
  17.0 0.0 copy-done.4
  17.0 0.0 copy-done
  17.0 0.0 copy-start.2
  17.0 0.5 %taps.1 = (bf16[144,384]{1,0:T(8,128)(2,1)S(1)}, bf16[384,144]{1,0:T(8,128)(2,1)S(1)}, f32[48,128]{1,0:T(8,128)S(1)}, s32[8,128]{1,0:T(8,128)S(1)}) custom-call(bf16[9,48,48]{2,1,0:T(8,128)(2,1)S(1)} %bitcast.9, f32[1,48]{1,0:T(1,128)S(1)} %bitcast.14, s32[1,3,1,5]{3,2,1,0:T(1,128)S(1)} %bitcast.13), custom_call_target="tpu_custom_call" | custom-call | flops 10000000 | bytes 1000000 | tf_op jit(solution)/shard_map/taps/pallas_call | solution.py:405
  17.4 0.7 %collective-permute-done.other_ref = bf16[32,16,96]{2,1,0:T(8,128)(2,1)S(1)} collective-permute-done((bf16[32,16,96]{2,1,0:T(8,128)(2,1)S(1)}, bf16[32,16,96]{2,1,0:T(8,128)(2,1)S(1)}, u32[]{:S(2)}, u32[]{:S(2)}) %collective-permute-start) | collective-permute-done | bytes 98336 | tf_op jit(solution)/shard_map/ppermute | solution.py:400
  18.1 0.0 copy-done.1
  18.1 0.0 copy-done.2
  18.1 8.9 %tiles.1 = (f32[10,48,128]{2,1,0:T(8,128)S(1)}, f32[10,48,128]{2,1,0:T(8,128)S(1)}) custom-call(bf16[32,16,96]{2,1,0:T(8,128)(2,1)S(1)} %all_to_all.10.mine_ref, bf16[32,16,96]{2,1,0:T(8,128)(2,1)S(1)} %collective-permute-done.other_ref, bf16[48,96]{1,0:T(8,128)(2,1)S(1)} %bitcast.11, bf16[144,384]{1,0:T(8,128)(2,1)S(1)} %get-tuple-element.13.forward_ref, ...), custom_call_target="tpu_custom_call" | custom-call | tf_op jit(solution)/shard_map/tiles/pallas_call | solution.py:419
  27.0 0.3 collective-permute-start.1
  27.2 1.3 %collective-permute-done.1.took_ref = f32[10,48,128]{2,1,0:T(8,128)S(1)} collective-permute-done((f32[10,48,128]{2,1,0:T(8,128)S(1)}, f32[10,48,128]{2,1,0:T(8,128)S(1)}, u32[]{:S(2)}, u32[]{:S(2)}) %collective-permute-start.1) | collective-permute-done | bytes 245792 | tf_op jit(solution)/shard_map/ppermute | solution.py:437
  28.5 0.2 pair.1
  28.8 10.0 %all_to_all.11.got_ref = bf16[32,16,128]{2,1,0:T(8,128)(2,1)S(1)} all-to-all(bf16[32,16,128]{2,1,0:T(8,128)(2,1)S(1)} %pair.1), channel_id=1, replica_groups=mesh['row'=8,'col'=4] {'row','col'}, dimensions={0} | all-to-all | bytes 262144 | tf_op jit(solution)/shard_map/all_to_all | solution.py:446
  38.8 0.3 collective-permute-start.2
  39.1 0.7 %features.1 = f32[1,2,16,96]{3,2,1,0:T(8,128)} custom-call(f32[32,128]{1,0:T(8,128)S(1)} %total.1.total_ref.mine_ref, bf16[48,96]{1,0:T(8,128)(2,1)S(1)} %bitcast.12), custom_call_target="tpu_custom_call" | custom-call | flops 10000000 | bytes 1000000 | tf_op jit(solution)/shard_map/features/pallas_call | solution.py:456
  39.8 0.2 collective-permute-done.2.other_ref
  40.0 0.9 %weights.1 = (f32[48,96]{1,0:T(8,128)}, f32[9,48,48]{2,1,0:T(8,128)}, f32[1,48]{1,0:T(1,128)}) custom-call(f32[32,128]{1,0:T(8,128)S(1)} %total.1.total_ref.mine_ref, f32[32,128]{1,0:T(8,128)S(1)} %collective-permute-done.2.other_ref, bf16[9,48,48]{2,1,0:T(8,128)(2,1)S(1)} %bitcast.10, f32[48,128]{1,0:T(8,128)S(1)} %get-tuple-element.15.column_ref), custom_call_target="tpu_custom_call" | custom-call | tf_op jit(solution)/shard_map/weights/pallas_call | solution.py:465
  (1 shorter events, 0.0 us)
Async XLA Ops:
  0.6 16.3 %copy-start.3 = (s32[1,1,5,3]{2,1,3,0:T(1,128)S(1)}, s32[1,1,5,3]{2,1,3,0:T(1,128)}, u32[]{:S(2)}) copy-start(s32[1,1,5,3]{2,1,3,0:T(1,128)} %param.10) | copy-start | bytes 184
  0.6 16.3 %copy-start.4 = (f32[48]{0:T(128)S(1)}, f32[48]{0:T(128)}, u32[]{:S(2)}) copy-start(f32[48]{0:T(128)} %param.9) | copy-start | bytes 580
  1.4 15.6 %copy-start = (bf16[48,9,48]{2,0,1:T(8,128)(2,1)S(1)}, bf16[48,9,48]{2,0,1:T(8,128)(2,1)}, u32[]{:S(2)}) copy-start(bf16[48,9,48]{2,0,1:T(8,128)(2,1)} %param.8) | copy-start | bytes 124420
  1.4 16.7 %copy-start.1 = (f32[1,1,5,64,64]{4,3,2,1,0:T(8,128)S(1)}, f32[1,1,5,64,64]{4,3,2,1,0:T(8,128)}, u32[]{:S(2)}) copy-start(f32[1,1,5,64,64]{4,3,2,1,0:T(8,128)} %targets_ref.1) | copy-start | bytes 245764
  16.7 1.3 %collective-permute-start = (bf16[32,16,96]{2,1,0:T(8,128)(2,1)S(1)}, bf16[32,16,96]{2,1,0:T(8,128)(2,1)S(1)}, u32[]{:S(2)}, u32[]{:S(2)}) collective-permute-start(bf16[32,16,96]{2,1,0:T(8,128)(2,1)S(1)} %all_to_all.10.mine_ref), channel_id=1, source_target_pairs={{0,1},{1,0},{2,3},{3,2},{4,5},{5,4},{6,7},{7,6},{8,9},{9,8},{10,11... | collective-permute-start | bytes 294920 | tf_op jit(solution)/shard_map/ppermute | solution.py:400
  17.0 1.1 %copy-start.2 = (bf16[96,48]{0,1:T(8,128)(2,1)S(1)}, bf16[96,48]{0,1:T(8,128)(2,1)}, u32[]{:S(2)}) copy-start(bf16[96,48]{0,1:T(8,128)(2,1)} %param.7) | copy-start | bytes 27652
  27.0 1.6 %collective-permute-start.1 = (f32[10,48,128]{2,1,0:T(8,128)S(1)}, f32[10,48,128]{2,1,0:T(8,128)S(1)}, u32[]{:S(2)}, u32[]{:S(2)}) collective-permute-start(f32[10,48,128]{2,1,0:T(8,128)S(1)} %get-tuple-element.18), channel_id=1, source_target_pairs={{0,1},{1,0},{2,3},{3,2},{4,5},{5,4},{6,7},{7,6},{8,9},{9,8},{10,11... | collective-permute-start | bytes 737288 | tf_op jit(solution)/shard_map/ppermute | solution.py:437
  38.8 1.2 %collective-permute-start.2 = (f32[32,128]{1,0:T(8,128)S(1)}, f32[32,128]{1,0:T(8,128)S(1)}, u32[]{:S(2)}, u32[]{:S(2)}) collective-permute-start(f32[32,128]{1,0:T(8,128)S(1)} %total.1.total_ref.mine_ref), channel_id=1, source_target_pairs={{0,1},{1,0},{2,3},{3,2},{4,5},{5,4},{6,7},{7,6},{8,9},{9,8},{10,11... | collective-permute-start | bytes 49160 | tf_op jit(solution)/shard_map/ppermute | solution.py:455

commit v9 on v8

--- a/solution.py
+++ b/solution.py
@@ -13,6 +13,7 @@
 HALO = 16
 F32 = jnp.float32
 BF16 = jnp.bfloat16
+FIELD = 32
 OUTSIDE = -1e30
 
 
@@ -36,7 +37,11 @@
 
 def taps_kernel(conv_ref, head_ref, table_ref, forward_ref, backward_ref, column_ref, entries_ref):
     ch = conv_ref.shape[1]
-    entries_ref[...] = pad_to(table_ref[0, :, 0, :], 8, LANES)
+    table = pad_to(table_ref[0, :, 0, :], 8, LANES)
+    row = table[:1]
+    for k in (1, 2):
+        row = row + pltpu.roll(table[k : k + 1], FIELD * k, 1)
+    entries_ref[...] = row
     head_col = jnp.transpose(jnp.broadcast_to(pad_to(head_ref[...], 1, LANES), (LANES, LANES)))[:ch]
     taps = [
         jnp.sum(head_col[:, :ch] * conv_ref[t].astype(F32), axis=0, keepdims=True)
@@ -131,7 +136,7 @@
     inner = (lane1 >= HALO) & (lane1 < HALO + bins)
 
     def slot(s, x_acc):
-        a, b, live = table_ref[0, s], table_ref[1, s], table_ref[2, s]
+        a, b, live = table_ref[0, FIELD * 0 + s], table_ref[0, FIELD * 1 + s], table_ref[0, FIELD * 2 + s]
         weight = jnp.where(inner, live.astype(F32), 0.0)
         gr, gc = gwin_ref[a].astype(F32), gwin_ref[b].astype(F32)
         pred_r = jnp.sum(jnp.where(lane < HALO + bins, head_col * gr, 0.0), axis=0, keepdims=True)
@@ -204,9 +209,12 @@
                 preferred_element_type=F32,
             )
 
+        activations(0)
+        activations(1)
         for g in range(0, groups + 2, 2):
-            activations(g)
-            activations(g + 1)
+            if g + 2 < groups + 2:
+                activations(g + 2)
+                activations(g + 3)
             pair = jnp.dot(
                 forward_ref[...],
                 u_ref[:, g * LANES : (g + 2) * LANES],
@@ -217,10 +225,13 @@
             m_cols = next_misfit(c, m_cols)
         for g in range(0, groups + 2, 2):
             d_rows, d_cols = gradients(g, d_rows, d_cols)
-            tap_sums(g)
+            if g >= 4:
+                tap_sums(g - 4)
             for c in (groups // 2 + g, groups // 2 + g + 1):
                 if c < groups:
                     m_cols = next_misfit(c, m_cols)
+        for g in (groups - 2, groups):
+            tap_sums(g)
         row_sums.append(jnp.zeros((LANES - HALO - bins, LANES), F32))
         m_rows = jnp.transpose(jnp.concatenate(row_sums, axis=0))[:1]
         m_cols = jnp.sum(m_cols, axis=0, keepdims=True)
@@ -262,10 +273,10 @@
     for r in range(rows_dev + 1):
         lower, upper = r, blocks - 1 - r
         keep_ref[r] = dwin_ref[jnp.where(odd, upper, lower)]
-        give_ref[r] = dwin_ref[jnp.where(odd, lower, upper)]
+        give_ref[r] = dwin_ref[jnp.where(odd, lower, upper)].astype(BF16)
     weights = jnp.where(lane < 2 * ch, proj_acc, sums)
     keep_ref[rows_dev + 1] = weights
-    give_ref[rows_dev + 1] = weights
+    give_ref[rows_dev + 1] = weights.astype(BF16)
 
 
 def pair_kernel(keep_ref, took_ref, out_ref):
@@ -274,7 +285,7 @@
     bins = LANES // 2
     cols_dev = out_ref.shape[0] // bands
     part = bins // cols_dev
-    weights = keep_ref[bands + 1] + took_ref[bands + 1]
+    weights = keep_ref[bands + 1] + took_ref[bands + 1].astype(F32)
     chunks = [weights[16 * q : 16 * q + 16] for q in range(3)]
     lane16 = lane_iota(16)
 
@@ -291,7 +302,8 @@
     shares = [jnp.where(odd, share(dest, 1), share(dest, 0)) for dest in range(2)]
     lane_part = lane_iota(part)
     windows = [
-        jnp.transpose(pad_to(keep_ref[r] + took_ref[r], LANES, LANES)) for r in range(bands + 1)
+        jnp.transpose(pad_to(keep_ref[r] + took_ref[r].astype(F32), LANES, LANES))
+        for r in range(bands + 1)
     ]
     first, end = HALO, HALO + bins
     for r in range(bands):
@@ -408,7 +420,7 @@
             jax.ShapeDtypeStruct((144, 8 * ch), BF16),
             jax.ShapeDtypeStruct((8 * ch, 144), BF16),
             jax.ShapeDtypeStruct((ch, LANES), F32),
-            jax.ShapeDtypeStruct((8, LANES), jnp.int32),
+            jax.ShapeDtypeStruct((1, LANES), jnp.int32),
         ),
         in_specs=[vmem, vmem, vmem],
         out_specs=(vmem, vmem, vmem, vmem),
@@ -418,7 +430,9 @@
     )(conv_t, head_weight.reshape(1, ch), tile_table.transpose(0, 3, 1, 2))
     keep, give = pl.pallas_call(
         functools.partial(tiles_kernel, rows_dev, slots),
-        out_shape=(jax.ShapeDtypeStruct((rows_dev + 2, ch, LANES), F32),) * 2,
+        out_shape=tuple(
+            jax.ShapeDtypeStruct((rows_dev + 2, ch, LANES), dtype) for dtype in (F32, BF16)
+        ),
         in_specs=[vmem] * 8,
         out_specs=(vmem, vmem),
         scratch_shapes=[
@@ -428,7 +442,7 @@
             pltpu.VMEM((8 * ch, (bins // 8 + 2) * LANES), BF16),
             pltpu.VMEM((48, (bins // 8 + 4) * LANES), BF16),
             pltpu.VMEM((96, 8 * ch), F32),
-            pltpu.SMEM((8, LANES), jnp.int32),
+            pltpu.SMEM((1, LANES), jnp.int32),
             pltpu.SemaphoreType.DMA,
         ],
         compiler_params=params,

time: 41.2 us -> 41.1 us (level)
  no operation moved by 1% of the time
where the time goes in v9:
time: 41.1 us; the launch traced here: 40.9 us
  blocking collectives  25.3 us (62%)
  Pallas kernels  11.3 us (27%)
  waiting for transfers between devices  2.01 us (5%)
  starting transfers between devices  0.78 us (2%)
  local copies, waits for them, and re-layouts  0.75 us (2%)
  between operations  0.7 us (2%)
    all_to_all x1, blocking collectives, body(): lax.all_to_all(jnp.broadcast_to(feats, (devices // halves,) + feats.shape...  15.3 us
    all_to_all x1, blocking collectives, body(): got = lax.all_to_all(partial, ('row', 'col'), 0, 0, tiled=True)  10 us
    pallas_call x1, Pallas kernels, body(): pl.pallas_call(functools.partial(tiles_kernel, rows_dev, slots), out_shap...  8.99 us
    ppermute x1, waiting for transfers between devices, body(): took = lax.ppermute(give, 'col', cores)  1.12 us
    pallas_call x1, Pallas kernels, body(): pl.pallas_call(functools.partial(weights_kernel, scale), out_shape=(jax.S...  0.9 us
  transfers between devices with their start and end apart: 3, of which 3 were waited for; matrix products, arithmetic and copies ran while one was open for 0% of the time, Pallas kernels for 3%

profile of v9, /device:TPU:0, one launch (start us, length us, event | category | flops | bytes accessed | tf_op | source)
XLA Modules:
  0.0 40.9 jit_solution(1994525838286868005)
XLA Ops:
  0.6 0.0 copy-start.3
  0.6 0.0 copy-start.4
  0.7 0.7 %broadcast_in_dim.8 = bf16[16,2,16,96]{3,2,1,0:T(8,128)(2,1)S(1)} broadcast(bf16[2,16,96]{2,1,0:T(8,128)(2,1)} %bitcast.16), dimensions={1,2,3} | broadcast | bytes 104448 | tf_op jit(solution)/shard_map/broadcast_in_dim | solution.py:405
  1.4 0.0 copy-start
  1.4 0.0 copy-start.1
  1.4 15.3 %all_to_all.10.mine_ref = bf16[32,16,96]{2,1,0:T(8,128)(2,1)S(1)} all-to-all(bf16[32,16,96]{2,1,0:T(8,128)(2,1)S(1)} %bitcast.15), channel_id=1, replica_groups=mesh['row'=8,'col'=4] {'row','col'}, dimensions={0} | all-to-all | bytes 196608 | tf_op jit(solution)/shard_map/all_to_all | solution.py:404
  16.7 0.2 collective-permute-start
  17.0 0.0 copy-done.3
  17.0 0.0 copy-done.4
  17.0 0.0 copy-done
  17.0 0.0 copy-start.2
  17.0 0.5 %taps.1 = (bf16[144,384]{1,0:T(8,128)(2,1)S(1)}, bf16[384,144]{1,0:T(8,128)(2,1)S(1)}, f32[48,128]{1,0:T(8,128)S(1)}, s32[1,128]{1,0:T(1,128)S(1)}) custom-call(bf16[9,48,48]{2,1,0:T(8,128)(2,1)S(1)} %bitcast.9, f32[1,48]{1,0:T(1,128)S(1)} %bitcast.14, s32[1,3,1,5]{3,2,1,0:T(1,128)S(1)} %bitcast.13), custom_call_target="tpu_custom_call" | custom-call | flops 10000000 | bytes 1000000 | tf_op jit(solution)/shard_map/taps/pallas_call | solution.py:417
  17.4 0.7 %collective-permute-done.other_ref = bf16[32,16,96]{2,1,0:T(8,128)(2,1)S(1)} collective-permute-done((bf16[32,16,96]{2,1,0:T(8,128)(2,1)S(1)}, bf16[32,16,96]{2,1,0:T(8,128)(2,1)S(1)}, u32[]{:S(2)}, u32[]{:S(2)}) %collective-permute-start) | collective-permute-done | bytes 98336 | tf_op jit(solution)/shard_map/ppermute | solution.py:412
  18.1 0.0 copy-done.1
  18.1 0.0 copy-done.2
  18.1 9.0 %tiles.1 = (f32[10,48,128]{2,1,0:T(8,128)S(1)}, bf16[10,48,128]{2,1,0:T(8,128)(2,1)S(1)}) custom-call(bf16[32,16,96]{2,1,0:T(8,128)(2,1)S(1)} %all_to_all.10.mine_ref, bf16[32,16,96]{2,1,0:T(8,128)(2,1)S(1)} %collective-permute-done.other_ref, bf16[48,96]{1,0:T(8,128)(2,1)S(1)} %bitcast.11, bf16[144,384]{1,0:T(8,128)(2,1)S(1)} %get-tuple-element.13.forward_ref, ...), custom_call_target="tpu_custom_call" | custom-call | tf_op jit(solution)/shard_map/tiles/pallas_call | solution.py:431
  27.1 0.3 collective-permute-start.1
  27.4 1.1 %collective-permute-done.1.took_ref = bf16[10,48,128]{2,1,0:T(8,128)(2,1)S(1)} collective-permute-done((bf16[10,48,128]{2,1,0:T(8,128)(2,1)S(1)}, bf16[10,48,128]{2,1,0:T(8,128)(2,1)S(1)}, u32[]{:S(2)}, u32[]{:S(2)}) %collective-permute-start.1) | collective-permute-done | bytes 122912 | tf_op jit(solution)/shard_map/ppermute | solution.py:451
  28.5 0.2 pair.1
  28.7 10.0 %all_to_all.11.got_ref = bf16[32,16,128]{2,1,0:T(8,128)(2,1)S(1)} all-to-all(bf16[32,16,128]{2,1,0:T(8,128)(2,1)S(1)} %pair.1), channel_id=1, replica_groups=mesh['row'=8,'col'=4] {'row','col'}, dimensions={0} | all-to-all | bytes 262144 | tf_op jit(solution)/shard_map/all_to_all | solution.py:460
  38.7 0.3 collective-permute-start.2
  39.0 0.7 %features.1 = f32[1,2,16,96]{3,2,1,0:T(8,128)} custom-call(f32[32,128]{1,0:T(8,128)S(1)} %total.1.total_ref.mine_ref, bf16[48,96]{1,0:T(8,128)(2,1)S(1)} %bitcast.12), custom_call_target="tpu_custom_call" | custom-call | flops 10000000 | bytes 1000000 | tf_op jit(solution)/shard_map/features/pallas_call | solution.py:470
  39.8 0.2 collective-permute-done.2.other_ref
  40.0 0.9 %weights.1 = (f32[48,96]{1,0:T(8,128)}, f32[9,48,48]{2,1,0:T(8,128)}, f32[1,48]{1,0:T(1,128)}) custom-call(f32[32,128]{1,0:T(8,128)S(1)} %total.1.total_ref.mine_ref, f32[32,128]{1,0:T(8,128)S(1)} %collective-permute-done.2.other_ref, bf16[9,48,48]{2,1,0:T(8,128)(2,1)S(1)} %bitcast.10, f32[48,128]{1,0:T(8,128)S(1)} %get-tuple-element.15.column_ref), custom_call_target="tpu_custom_call" | custom-call | tf_op jit(solution)/shard_map/weights/pallas_call | solution.py:479
  (1 shorter events, 0.0 us)
Async XLA Ops:
  0.6 16.3 %copy-start.3 = (s32[1,1,5,3]{2,1,3,0:T(1,128)S(1)}, s32[1,1,5,3]{2,1,3,0:T(1,128)}, u32[]{:S(2)}) copy-start(s32[1,1,5,3]{2,1,3,0:T(1,128)} %param.10) | copy-start | bytes 184
  0.6 16.3 %copy-start.4 = (f32[48]{0:T(128)S(1)}, f32[48]{0:T(128)}, u32[]{:S(2)}) copy-start(f32[48]{0:T(128)} %param.9) | copy-start | bytes 580
  1.4 15.6 %copy-start = (bf16[48,9,48]{2,0,1:T(8,128)(2,1)S(1)}, bf16[48,9,48]{2,0,1:T(8,128)(2,1)}, u32[]{:S(2)}) copy-start(bf16[48,9,48]{2,0,1:T(8,128)(2,1)} %param.8) | copy-start | bytes 124420
  1.4 16.7 %copy-start.1 = (f32[1,1,5,64,64]{4,3,2,1,0:T(8,128)S(1)}, f32[1,1,5,64,64]{4,3,2,1,0:T(8,128)}, u32[]{:S(2)}) copy-start(f32[1,1,5,64,64]{4,3,2,1,0:T(8,128)} %targets_ref.1) | copy-start | bytes 245764
  16.7 1.3 %collective-permute-start = (bf16[32,16,96]{2,1,0:T(8,128)(2,1)S(1)}, bf16[32,16,96]{2,1,0:T(8,128)(2,1)S(1)}, u32[]{:S(2)}, u32[]{:S(2)}) collective-permute-start(bf16[32,16,96]{2,1,0:T(8,128)(2,1)S(1)} %all_to_all.10.mine_ref), channel_id=1, source_target_pairs={{0,1},{1,0},{2,3},{3,2},{4,5},{5,4},{6,7},{7,6},{8,9},{9,8},{10,11... | collective-permute-start | bytes 294920 | tf_op jit(solution)/shard_map/ppermute | solution.py:412
  17.0 1.1 %copy-start.2 = (bf16[96,48]{0,1:T(8,128)(2,1)S(1)}, bf16[96,48]{0,1:T(8,128)(2,1)}, u32[]{:S(2)}) copy-start(bf16[96,48]{0,1:T(8,128)(2,1)} %param.7) | copy-start | bytes 27652
  27.1 1.4 %collective-permute-start.1 = (bf16[10,48,128]{2,1,0:T(8,128)(2,1)S(1)}, bf16[10,48,128]{2,1,0:T(8,128)(2,1)S(1)}, u32[]{:S(2)}, u32[]{:S(2)}) collective-permute-start(bf16[10,48,128]{2,1,0:T(8,128)(2,1)S(1)} %get-tuple-element.18), channel_id=1, source_target_pairs={{0,1},{1,0},{2,3},{3,2},{4,5},{5,4},{6,7},{7,6},{8,9},{9,8},{10,11... | collective-permute-start | bytes 368648 | tf_op jit(solution)/shard_map/ppermute | solution.py:451
  38.7 1.2 %collective-permute-start.2 = (f32[32,128]{1,0:T(8,128)S(1)}, f32[32,128]{1,0:T(8,128)S(1)}, u32[]{:S(2)}, u32[]{:S(2)}) collective-permute-start(f32[32,128]{1,0:T(8,128)S(1)} %total.1.total_ref.mine_ref), channel_id=1, source_target_pairs={{0,1},{1,0},{2,3},{3,2},{4,5},{5,4},{6,7},{7,6},{8,9},{9,8},{10,11... | collective-permute-start | bytes 49160 | tf_op jit(solution)/shard_map/ppermute | solution.py:469
